TPU v7x, 32 devices: a whole 2x2x4 slice. The times are simulated.
32 devices in a mesh: seq: 16 (over z, y, x), tensor: 2 (over core).
Axes of the slice: x: 2, y: 2, z: 4, core: 2. Of those that a mesh axis runs over, the one named last changes fastest.
Arguments:
- tokens: bfloat16 [4096, 2048], P('seq'), may hold values from -6 to 6
- gain_attn: bfloat16 [2048], P('seq'), may hold values from 0.5 to 1.5
- w_query: bfloat16 [2048, 256], P('seq', 'tensor'), may hold values from -0.125 to 0.125
- w_key: bfloat16 [2048, 256], P('seq', 'tensor'), may hold values from -0.125 to 0.125
- w_value: bfloat16 [2048, 2048], P('seq', 'tensor'), may hold values from -0.125 to 0.125
- w_output: bfloat16 [2048, 2048], P('tensor', 'seq'), may hold values from -2 to 2
- gain_mlp: bfloat16 [2048], P('seq'), may hold values from 0.5 to 1.5
- w_gate: bfloat16 [2048, 5504], P('seq', 'tensor'), may hold values from -0.125 to 0.125
- w_up: bfloat16 [2048, 5504], P('seq', 'tensor'), may hold values from -0.125 to 0.125
- w_down: bfloat16 [5504, 2048], P('tensor', 'seq'), may hold values from -0.078125 to 0.078125
- seq_lengths: int32 [3], replicated, may hold values from 64 to 3968, as said below
- cotangent: bfloat16 [4096, 2048], P('seq'), may hold values from -6 to 6
Outputs:
- output: bfloat16 [4096, 2048], P('seq')
- grad_tokens: float32 [4096, 2048], P('seq')
- grad_gain_attn: float32 [2048], P('seq')
- grad_w_query: float32 [2048, 256], P('seq', 'tensor')
- grad_w_key: float32 [2048, 256], P('seq', 'tensor')
- grad_w_value: float32 [2048, 2048], P('seq', 'tensor')
- grad_w_output: float32 [2048, 2048], P('tensor', 'seq')
- grad_gain_mlp: float32 [2048], P('seq')
- grad_w_gate: float32 [2048, 5504], P('seq', 'tensor')
- grad_w_up: float32 [2048, 5504], P('seq', 'tensor')
- grad_w_down: float32 [5504, 2048], P('tensor', 'seq')
Inputs may be any that keep to these rules, and one draw needn't show every extreme that they name: `seq_lengths`: the lengths sum to 4096; the first and the last sequence each have fewer than 256 tokens, and the middle one holds the rest.
All inputs are finite; a program needn't handle non-finite values.
Results may differ from a plain program's by a relative error of at most 0.014.
Values may be sent and summed in bfloat16 or wider, within the bound.
A program may use at most 448 MiB of HBM per device.

v0:
```python
import math

import jax
import jax.numpy as jnp
from jax import lax
from jax.sharding import PartitionSpec as P

HEADS = 16
FEAT = 16


EPS = 1e-06
HIGH = lax.Precision.HIGHEST


def carried_in(part, axis, combine, identity):
    place = lax.axis_index(axis)
    gathered = jax.tree.map(lambda a: lax.all_gather(a, axis), part)
    state = jax.tree.map(lambda a, e: jnp.zeros_like(a) + jnp.asarray(e, a.dtype), part, identity)

    def one(hop, state):
        return combine(
            state, jax.tree.map(lambda a: lax.dynamic_index_in_dim(a, hop, 0, False), gathered)
        )

    return lax.fori_loop(0, place, one, state)


def prefix(x, axis, combine, identity):
    devices, place = (lax.axis_size(axis), lax.axis_index(axis))
    everything = jax.tree.map(
        lambda part, kind: lax.all_gather(part.astype(kind), axis),
        x,
        jax.tree.map(lambda a: jnp.bfloat16 if a.dtype == jnp.float32 else a.dtype, x),
    )
    start = jax.tree.map(
        lambda part, zero: jnp.broadcast_to(jnp.asarray(zero, part.dtype), part.shape), x, identity
    )

    def hop(k, before):
        at = devices - 1 - k
        reached = at > place
        new = combine(
            before, jax.tree.map(lambda part, own: part[at].astype(own.dtype), everything, x)
        )
        return jax.tree.map(lambda a, b: jnp.where(reached, a, b), new, before)

    return lax.fori_loop(0, devices, hop, start)


def split_up(x, dim, devices):
    before, after = (x.shape[:dim], x.shape[dim + 1 :])
    return jnp.moveaxis(x.reshape(*before, devices, -1, *after), dim, 0)


def summed_on_arrival(x, axis, dim):
    tiles = split_up(x, dim, lax.axis_size(axis))
    arrived = lax.all_to_all(tiles, axis, split_axis=0, concat_axis=0, tiled=True)
    return arrived.astype(jnp.float32).sum(axis=0)


def in_one_piece(arrays, axis, dim, along):
    widths = [math.prod(a.shape[along:]) for a in arrays]
    both = jnp.concatenate(
        [a.reshape(*a.shape[:along], w) for a, w in zip(arrays, widths)], axis=along
    )
    filled = summed_on_arrival(both, axis, dim)
    tiles = jnp.split(filled, [sum(widths[:k]) for k in range(1, len(widths))], axis=along)
    return tuple(
        (b.reshape(*filled.shape[:along], *a.shape[along:]) for a, b in zip(arrays, tiles))
    )


def features(scaled):
    feat_width = scaled.shape[-1]
    products = (scaled[..., :, None] * scaled[..., None, :]).reshape(
        scaled.shape[:-1] + (feat_width * feat_width,)
    )
    constant = jnp.ones(scaled.shape[:-1] + (1,), jnp.float32)
    return jnp.concatenate([constant, scaled, products * 0.5**0.5], axis=-1)


def attend(queries, keys_in, values_in, prefix_sum, prefix_norm, use_prefix, causal):
    scores = jnp.einsum("htf,hsf->hts", queries, keys_in, precision=HIGH)
    kernel = (1.0 + scores + 0.5 * scores * scores) * causal[None]
    numerator = jnp.einsum("hts,hse->hte", kernel, values_in, precision=HIGH)
    denominator = jnp.sum(kernel, axis=-1)
    lifted = features(queries) * use_prefix[None, :, None]
    numerator = numerator + jnp.einsum("htp,hpe->hte", lifted, prefix_sum, precision=HIGH)
    denominator = denominator + jnp.einsum("htp,hp->ht", lifted, prefix_norm, precision=HIGH)
    return numerator / denominator[..., None]


def group_state(keys_in, values_in, contrib):
    lifted = features(keys_in) * contrib[None, :, None]
    return (jnp.einsum("htp,hte->hpe", lifted, values_in, precision=HIGH), jnp.sum(lifted, axis=1))


def token_masks(starts, position):
    group_first = position[0]
    group_last = position[-1]
    start_cols = starts[None, :]
    token_rows = position[:, None]
    seen_starts = jnp.sum(
        ((start_cols >= group_first) & (start_cols <= token_rows)).astype(jnp.int32), axis=1
    )
    later_starts = jnp.sum(
        ((start_cols > token_rows) & (start_cols <= group_last)).astype(jnp.int32), axis=1
    )
    reset_flag = jnp.max(((starts >= group_first) & (starts <= group_last)).astype(jnp.float32))
    segment = jnp.sum((start_cols <= token_rows).astype(jnp.int32), axis=1)
    causal = (
        (position[None, :] <= position[:, None]) & (segment[None, :] == segment[:, None])
    ).astype(jnp.float32)
    return (
        (seen_starts == 0).astype(jnp.float32),
        (later_starts == 0).astype(jnp.float32),
        reset_flag,
        causal,
    )


def combine(earlier, later):
    keep = 1.0 - later[2]
    return (
        later[0] + keep * earlier[0],
        later[1] + keep * earlier[1],
        jnp.maximum(earlier[2], later[2]),
    )


def rms_norm(inputs, gain):
    inv_root = lax.rsqrt(jnp.mean(inputs * inputs, axis=-1, keepdims=True) + EPS)
    normed = inputs * inv_root
    return (normed, inv_root, normed * gain.astype(jnp.float32))


def norm_back(grad_out, normed, inv_root, gain):
    scaled_grad = grad_out * gain.astype(jnp.float32)
    grad_in = inv_root * (
        scaled_grad - normed * jnp.mean(scaled_grad * normed, axis=-1, keepdims=True)
    )
    return (grad_in, jnp.sum(grad_out * normed, axis=0))


def split_heads(matrix, head_count):
    return matrix.reshape(matrix.shape[0], head_count, -1).transpose(1, 0, 2)


def join_heads(per_head):
    return per_head.transpose(1, 0, 2).reshape(per_head.shape[1], -1)


def product_plain(left, right):
    return jnp.dot(left, right, preferred_element_type=jnp.float32)


def transposed_left(left, right):
    return lax.dot_general(
        left, right, (((0,), (0,)), ((), ())), preferred_element_type=jnp.float32
    )


def transposed_right(left, right):
    return lax.dot_general(
        left, right, (((1,), (1,)), ((), ())), preferred_element_type=jnp.float32
    )


def body(
    tokens,
    gain_attn,
    w_query,
    w_key,
    w_value,
    w_output,
    gain_mlp,
    w_gate,
    w_up,
    w_down,
    seq_lengths,
    cotangent,
):
    row_count = tokens.shape[0]
    head_count = HEADS // lax.axis_size("tensor")
    scale = FEAT ** (-0.25)
    position = lax.axis_index("seq") * row_count + jnp.arange(row_count, dtype=jnp.int32)
    starts = jnp.cumsum(seq_lengths) - seq_lengths
    use_prefix, contrib, reset_flag, causal = token_masks(starts, position)
    gain_one, query_w, key_w, value_w, output_w = (
        lax.all_gather(gain_attn, "seq", axis=0, tiled=True),
        lax.all_gather(w_query, "seq", axis=0, tiled=True),
        lax.all_gather(w_key, "seq", axis=0, tiled=True),
        lax.all_gather(w_value, "seq", axis=0, tiled=True),
        lax.all_gather(w_output, "seq", axis=1, tiled=True),
    )
    inputs = tokens.astype(jnp.float32)
    normed_one, root_one, pre_one = rms_norm(inputs, gain_one)
    low_one = pre_one.astype(jnp.bfloat16)
    query_low = product_plain(low_one, query_w).astype(jnp.bfloat16)
    key_low = product_plain(low_one, key_w).astype(jnp.bfloat16)
    value_low = product_plain(low_one, value_w).astype(jnp.bfloat16)
    queries = split_heads(query_low.astype(jnp.float32) * scale, head_count)
    keys_in = split_heads(key_low.astype(jnp.float32) * scale, head_count)
    values_in = split_heads(value_low.astype(jnp.float32), head_count)

    def state_of(keys_given, values_given):
        return group_state(keys_given, values_given, contrib)

    (local_sum, local_norm), state_back = jax.vjp(state_of, keys_in, values_in)
    identity = (jnp.zeros_like(local_sum), jnp.zeros_like(local_norm), jnp.zeros_like(reset_flag))
    prefix_sum, prefix_norm, prefix_reset = carried_in(
        (local_sum, local_norm, reset_flag), "seq", combine, identity
    )

    def local_attend(queries_given, keys_given, values_given, sum_given, norm_given):
        return attend(
            queries_given, keys_given, values_given, sum_given, norm_given, use_prefix, causal
        )

    heads_out, attend_back = jax.vjp(
        local_attend, queries, keys_in, values_in, prefix_sum, prefix_norm
    )
    attn_low = join_heads(heads_out).astype(jnp.bfloat16)
    attn_out = lax.psum(product_plain(attn_low, output_w), "tensor")
    residual = inputs + attn_out
    gain_two, gate_w, up_w, down_w = (
        lax.all_gather(gain_mlp, "seq", axis=0, tiled=True),
        lax.all_gather(w_gate, "seq", axis=0, tiled=True),
        lax.all_gather(w_up, "seq", axis=0, tiled=True),
        lax.all_gather(w_down, "seq", axis=1, tiled=True),
    )
    normed_two, root_two, pre_two = rms_norm(residual, gain_two)
    low_two = pre_two.astype(jnp.bfloat16)
    gate_pre = product_plain(low_two, gate_w)
    up_pre = product_plain(low_two, up_w)
    sigma = jax.nn.sigmoid(gate_pre)
    silu_gate = gate_pre * sigma
    hidden = (silu_gate * up_pre).astype(jnp.bfloat16)
    mlp_out = lax.psum(product_plain(hidden, down_w).astype(jnp.bfloat16), "tensor").astype(
        jnp.float32
    )
    output = (residual + mlp_out).astype(jnp.bfloat16)
    gain_two, gate_w, up_w, down_w = (
        lax.all_gather(gain_mlp, "seq", axis=0, tiled=True),
        lax.all_gather(w_gate, "seq", axis=0, tiled=True),
        lax.all_gather(w_up, "seq", axis=0, tiled=True),
        lax.all_gather(w_down, "seq", axis=1, tiled=True),
    )
    d_hidden = transposed_right(cotangent, down_w)
    d_gate = (d_hidden * up_pre * sigma * (1.0 + gate_pre * (1.0 - sigma))).astype(jnp.bfloat16)
    d_up = (d_hidden * silu_gate).astype(jnp.bfloat16)
    d_low_two = lax.psum(
        (transposed_right(d_gate, gate_w) + transposed_right(d_up, up_w)).astype(jnp.bfloat16),
        "tensor",
    ).astype(jnp.float32)
    d_from_two, grad_gain_two = norm_back(d_low_two, normed_two, root_two, gain_two)
    d_residual = cotangent.astype(jnp.float32) + d_from_two
    mlp_grads = (
        lax.psum_scatter(grad_gain_two, "seq", scatter_dimension=0, tiled=True),
        lax.psum_scatter(transposed_left(low_two, d_gate), "seq", scatter_dimension=0, tiled=True),
        lax.psum_scatter(transposed_left(low_two, d_up), "seq", scatter_dimension=0, tiled=True),
        lax.psum_scatter(
            transposed_left(hidden, cotangent), "seq", scatter_dimension=1, tiled=True
        ),
    )
    mlp_gain_share, grad_gate_share, grad_up_share, grad_down_share = mlp_grads
    gain_one, query_w, key_w, value_w, output_w = (
        lax.all_gather(gain_attn, "seq", axis=0, tiled=True),
        lax.all_gather(w_query, "seq", axis=0, tiled=True),
        lax.all_gather(w_key, "seq", axis=0, tiled=True),
        lax.all_gather(w_value, "seq", axis=0, tiled=True),
        lax.all_gather(w_output, "seq", axis=1, tiled=True),
    )
    d_attn = d_residual.astype(jnp.bfloat16)
    d_heads = split_heads(transposed_right(d_attn, output_w), head_count)
    d_queries, d_keys, d_values, d_prefix_sum, d_prefix_norm = attend_back(d_heads)
    suffix_sum, suffix_norm, suffix_reset = prefix(
        (d_prefix_sum, d_prefix_norm, reset_flag), "seq", combine, identity
    )
    d_keys_state, d_values_state = state_back((suffix_sum, suffix_norm))
    d_query = (join_heads(d_queries) * scale).astype(jnp.bfloat16)
    d_key = (join_heads(d_keys + d_keys_state) * scale).astype(jnp.bfloat16)
    d_value = join_heads(d_values + d_values_state).astype(jnp.bfloat16)
    d_low_one = lax.psum(
        (
            transposed_right(d_query, query_w)
            + transposed_right(d_key, key_w)
            + transposed_right(d_value, value_w)
        ).astype(jnp.bfloat16),
        "tensor",
    ).astype(jnp.float32)
    d_from_one, grad_gain_one = norm_back(d_low_one, normed_one, root_one, gain_one)
    grad_tokens = d_residual + d_from_one
    attn_grads = (
        *in_one_piece(
            (
                grad_gain_one.astype(jnp.bfloat16),
                transposed_left(low_one, d_query).astype(jnp.bfloat16),
                transposed_left(low_one, d_key).astype(jnp.bfloat16),
                transposed_left(low_one, d_value).astype(jnp.bfloat16),
            ),
            "seq",
            0,
            1,
        ),
        summed_on_arrival(transposed_left(attn_low, d_attn).astype(jnp.bfloat16), "seq", 1),
    )
    attn_gain_share, grad_query_share, grad_key_share, grad_value_share, grad_output_share = (
        attn_grads
    )
    return (
        output,
        grad_tokens,
        attn_gain_share,
        grad_query_share,
        grad_key_share,
        grad_value_share,
        grad_output_share,
        mlp_gain_share,
        grad_gate_share,
        grad_up_share,
        grad_down_share,
    )


def solution(mesh):
    return jax.shard_map(
        body,
        mesh=mesh,
        in_specs=(
            P("seq", None),
            P("seq"),
            P("seq", "tensor"),
            P("seq", "tensor"),
            P("seq", "tensor"),
            P("tensor", "seq"),
            P("seq"),
            P("seq", "tensor"),
            P("seq", "tensor"),
            P("tensor", "seq"),
            P(),
            P("seq", None),
        ),
        out_specs=(
            P("seq", None),
            P("seq", None),
            P("seq"),
            P("seq", "tensor"),
            P("seq", "tensor"),
            P("seq", "tensor"),
            P("tensor", "seq"),
            P("seq"),
            P("seq", "tensor"),
            P("seq", "tensor"),
            P("tensor", "seq"),
        ),
        check_vma=False,
    )
```

profile of v0, /device:TPU:9, one launch (start us, length us, event | category | flops | bytes accessed | tf_op | source)
XLA Modules:
  0.0 2964.5 jit_solution(9119100937119821800)
XLA Ops:
  8.0 28.0 all-gather.4
  37.4 2.6 fusion.57
  40.1 1.5 fusion.25
  41.7 37.4 %all_gather.74 = bf16[2048,128]{1,0:T(8,128)(2,1)S(1)} all-gather(bf16[128,128]{1,0:T(8,128)(2,1)} %param.19), channel_id=1, replica_groups=mesh['seq'=16,'tensor'=2] {'seq'}, dimensions={0}, use_global_device_ids=true | all-gather | bytes 557056 | tf_op jit(solution)/shard_map/all_gather | solution.py:193
  79.0 2.0 fusion.33
  81.4 12.9 all-gather.14.cloned.1.call-done
  94.3 3.5 convolution_convert_fusion.5
  104.2 42.8 %all-reduce = f32[16]{0:T(128)S(1)} all-reduce(f32[16]{0:T(128)S(1)} %dynamic-update-slice), channel_id=1, replica_groups=mesh['seq'=16,'tensor'=2] {'seq'}, use_global_device_ids=true, to_apply=%add | all-reduce | flops 16 | bytes 128
  147.7 42.2 %all-gather.1 = f32[128,273]{1,0:T(8,128)} all-gather(f32[8,273]{1,0:T(8,128)S(1)} %fusion.62), channel_id=3, replica_groups=mesh['seq'=16,'tensor'=2] {'seq'}, dimensions={0}, use_global_device_ids=true | all-gather | bytes 148512 | tf_op jit(solution)/shard_map/all_gather | solution.py:18
  190.1 56.8 %all_gather.73 = bf16[2048,128]{1,0:T(8,128)(2,1)S(1)} all-gather(bf16[128,128]{1,0:T(8,128)(2,1)S(1)} %copy-done.46), channel_id=1, replica_groups=mesh['seq'=16,'tensor'=2] {'seq'}, dimensions={0}, use_global_device_ids=true | all-gather | bytes 557056 | tf_op jit(solution)/shard_map/all_gather | solution.py:192
  248.0 2.8 fusion.39
  252.1 2.3 fusion.40
  254.3 235.0 %all-gather.24.cloned.1.call-done = f32[128,273,128]{2,0,1:T(8,128)} async-done(((f32[8,273,128]{2,0,1:T(8,128)}), f32[128,273,128]{2,0,1:T(8,128)}) %all-gather.24.cloned.1.call-update) | async-done | bytes 17891344 | tf_op jit(solution)/shard_map/all_gather | solution.py:18
  489.4 15.1 while.32
  504.6 1.9 fusion.52
  506.5 5.0 fusion.36
  511.5 69.6 %all-gather.16.cloned.1.call-done = bf16[1024,2048]{1,0:T(8,128)(2,1)} async-done(((bf16[1024,128]{1,0:T(8,128)(2,1)}), bf16[1024,2048]{1,0:T(8,128)(2,1)}) %all-gather.16.cloned.1.call-update) | async-done | bytes 4194320 | tf_op jit(solution)/shard_map/all_gather | solution.py:195
  581.1 4.9 fusion.73
  588.1 26.5 all-gather.5
  614.6 2.2 multiply_reduce_fusion.4
  618.3 170.8 %all-gather.18.cloned.1.call-done = bf16[2048,2752]{0,1:T(8,128)(2,1)} async-done(((bf16[128,2752]{0,1:T(8,128)(2,1)}), bf16[2048,2752]{0,1:T(8,128)(2,1)}) %all-gather.18.cloned.1.call-update) | async-done | bytes 11272208 | tf_op jit(solution)/shard_map/all_gather | solution.py:229
  789.1 9.2 fusion.74
  798.3 171.2 %all-gather.20.cloned.1.call-done = bf16[2048,2752]{0,1:T(8,128)(2,1)} async-done(((bf16[128,2752]{0,1:T(8,128)(2,1)}), bf16[2048,2752]{0,1:T(8,128)(2,1)}) %all-gather.20.cloned.1.call-update) | async-done | bytes 11272208 | tf_op jit(solution)/shard_map/all_gather | solution.py:230
  969.4 9.3 fusion.75
  978.7 171.2 %all-gather.22.cloned.1.call-done = bf16[2752,2048]{1,0:T(8,128)(2,1)} async-done(((bf16[2752,128]{1,0:T(8,128)(2,1)}), bf16[2752,2048]{1,0:T(8,128)(2,1)}) %all-gather.22.cloned.1.call-update) | async-done | bytes 11272208 | tf_op jit(solution)/shard_map/all_gather | solution.py:231
  1149.9 11.6 multiply_convert_fusion
  1161.6 7.3 fusion.76
  1168.9 4.1 fusion.9
  1173.1 20.9 all-reduce.10.cloned.1.call-done
  1194.0 2.2 fusion.19
  1200.4 2.5 convolution_convert_fusion.4
  1205.3 28.7 all-reduce.1
  1234.0 8.9 convolution_convert_fusion.1
  1243.0 2.2 fusion.54
  1245.2 32.1 %all-gather.3 = bf16[128,273]{1,0:T(8,128)(2,1)S(1)} all-gather(bf16[8,273]{1,0:T(8,128)(2,1)S(1)} %bitcast.232), channel_id=5, replica_groups=mesh['seq'=16,'tensor'=2] {'seq'}, dimensions={0}, use_global_device_ids=true | all-gather | bytes 74256 | tf_op jit(solution)/shard_map/all_gather | solution.py:32
  1277.3 2.2 add_multiply_fusion.1
  1281.6 1.6 fusion.26
  1284.6 1.8 fusion.77
  1286.4 3.7 fusion.37
  1290.1 62.8 %all-gather.26.cloned.1.call-done = bf16[128,273,128]{2,0,1:T(8,128)(2,1)} async-done(((bf16[8,273,128]{2,0,1:T(8,128)(2,1)}), bf16[128,273,128]{2,0,1:T(8,128)(2,1)}) %all-gather.26.cloned.1.call-update) | async-done | bytes 8945680 | tf_op jit(solution)/shard_map/all_gather | solution.py:32
  1352.9 45.2 %while.33 = (s32[]{:T(128)}, f32[8,273,128]{2,1,0:T(8,128)S(1)}, f32[8,273]{1,0:T(8,128)S(1)}, s32[]{:T(128)}, bf16[16,8,273,128]{3,1,0,2:T(8,128)(2,1)}, /*inde...) while((s32[]{:T(128)}, f32[8,273,128]{2,1,0:T(8,128)S(1)}, ...), condition=%wide.region_19.20_spmd.clone, body=%wide.region_18.19_spmd.clone.sunk | while | flops 1408689 | bytes 3935787 | solution.py:48
  1401.4 3.2 fusion.27
  1404.7 1.9 fusion.31
  1411.0 9.8 fusion.80
  1422.2 10.0 fusion.81
  1433.8 9.8 fusion.79
  1443.7 1.6 copy-done.5
  1446.6 3.1 copy.161
  1449.7 6.3 all-to-all-start.1
  1457.4 2.0 copy.105
  1460.8 2.0 copy.106
  1462.9 4.5 convolution_convert_fusion
  1467.3 6.4 copy.107
  1473.7 2.1 fusion.24
  1475.8 35.7 %concatenate.21 = bf16[16,128,1281]{1,2,0:T(8,128)(2,1)} concatenate(bf16[16,128,1]{1,2,0:T(2,128)(2,1)S(1)} %copy.104, bf16[16,128,128]{1,2,0:T(8,128)(2,1)} %copy.105, bf16[16,128,128]{1,2,0:T(8,128)(2,1)} %copy.106, bf16[16,128,1024]{1,2,0:T(8,128)(2,1)} %copy.107), dimensions={2} | concatenate | bytes 10493952 | tf_op jit(solution)/shard_map/concatenate | solution.py:64
  1511.4 97.9 %all-to-all-done.1 = bf16[16,1024,128]{2,1,0:T(8,128)(2,1)} async-done(((bf16[16,1024,128]{2,1,0:T(8,128)(2,1)}), bf16[16,1024,128]{2,1,0:T(8,128)(2,1)}, u32[]{:S(2)}, u32[]{:S(2)}) %all-to-all-start.1) | async-done | bytes 4194336 | tf_op jit(solution)/shard_map/all_to_all | solution.py:58
  1609.3 7.4 all-to-all-start
  1617.3 218.8 %all-reduce.2 = f32[2048]{0:T(1024)S(1)} all-reduce(f32[2048]{0:T(1024)S(1)} %get-tuple-element.339), channel_id=6, replica_groups=mesh['seq'=16,'tensor'=2] {'seq'}, use_global_device_ids=true, to_apply=%region_28.29.clone | all-reduce | flops 2048 | bytes 16384
  1836.7 3.9 convert_reduce_fusion.1
  1840.6 2.8 fusion.15
  1843.4 3.3 convert_reduce_fusion
  1849.7 165.7 %reduce-scatter.4.cloned.1.call-done = f32[128,2752]{0,1:T(8,128)} async-done(((f32[2048,2752]{0,1:T(8,128)}), f32[128,2752]{0,1:T(8,128)}) %reduce-scatter.4.cloned.1.call-update) | async-done | bytes 1409040 | tf_op jit(solution)/shard_map/reduce_scatter | solution.py:261
  2015.5 469.9 %reduce-scatter.6.cloned.1.call-done = f32[128,2752]{0,1:T(8,128)} async-done(((f32[2048,2752]{0,1:T(8,128)}), f32[128,2752]{0,1:T(8,128)}) %reduce-scatter.6.cloned.1.call-update) | async-done | bytes 1409040 | tf_op jit(solution)/shard_map/reduce_scatter | solution.py:262
  2485.4 472.4 %reduce-scatter.8.cloned.1.call-done = f32[2752,128]{1,0:T(8,128)} async-done(((f32[2752,2048]{1,0:T(8,128)}), f32[2752,128]{1,0:T(8,128)}) %reduce-scatter.8.cloned.1.call-update) | async-done | bytes 1409040 | tf_op jit(solution)/shard_map/reduce_scatter | solution.py:263
  (297 shorter events, 89.3 us)
Async XLA Ops:
  7.2 87.1 %all-gather.14.cloned.1.call-start = ((), (), s32[]{:S(2)}) async-start(), calls=%async_computation.5 | async-start | bytes 4456448 | tf_op jit(solution)/shard_map/all_gather | solution.py:194
  7.9 481.4 %all-gather.24.cloned.1.call-start = ((), (), s32[]{:S(2)}) async-start(), calls=%async_computation.15 | async-start | bytes 19009536 | tf_op jit(solution)/shard_map/all_gather | solution.py:18
  36.8 469.7 %copy-start.47 = (f32[273]{0:T(512)}, f32[273]{0:T(512)S(1)}, u32[]{:S(2)}) copy-start(f32[273]{0:T(512)S(1)} %pad.3.clone) | copy-start | bytes 3280
  41.6 105.4 %copy-start.51 = (f32[256]{0:T(256)}, f32[256]{0:T(256)S(1)}, u32[]{:S(2)}) copy-start(f32[256]{0:T(256)S(1)} %compare_convert_fusion.1) | copy-start | bytes 3076
  79.0 2.0 copy-start.23
  79.0 15.2 copy-start.2
  81.4 65.6 %copy-start.6 = (f32[8,256,16,16]{1,3,2,0:T(8,128)}, f32[8,256,16,16]{1,3,2,0:T(8,128)S(1)}, u32[]{:S(2)}) copy-start(f32[8,256,16,16]{1,3,2,0:T(8,128)S(1)} %multiply_multiply_fusion.1) | copy-start | bytes 6291460
  100.1 2.0 copy-start.57
  101.3 88.8 %copy-start.46 = (bf16[128,128]{1,0:T(8,128)(2,1)S(1)}, bf16[128,128]{1,0:T(8,128)(2,1)}, u32[]{:S(2)}) copy-start(bf16[128,128]{1,0:T(8,128)(2,1)} %param.18) | copy-start | bytes 98308
  101.3 479.9 %all-gather.16.cloned.1.call-start = ((), (), s32[]{:S(2)}) async-start(), calls=%async_computation.6 | async-start | bytes 4456448 | tf_op jit(solution)/shard_map/all_gather | solution.py:195
  102.0 512.6 %all-reduce.8.cloned.1.call-start = ((), (), s32[]{:S(2)}) async-start(), calls=%async_computation.7 | async-start | bytes 4194304 | tf_op jit(solution)/shard_map/psum | solution.py:225
  189.9 314.7 %copy-start.58 = (f32[256]{0:T(256)}, f32[256]{0:T(256)S(1)}, u32[]{:S(2)}) copy-start(f32[256]{0:T(256)S(1)} %compare_convert_fusion.2) | copy-start | bytes 3076
  190.0 60.8 %copy-start.42 = (f32[256,256]{0,1:T(8,128)}, f32[256,256]{0,1:T(8,128)S(1)}, u32[]{:S(2)}) copy-start(f32[256,256]{0,1:T(8,128)S(1)} %and_convert_fusion) | copy-start | bytes 786436
  247.7 3.1 copy-start.33
  248.0 258.5 %copy-start.25 = (f32[8,256,16,16]{1,3,2,0:T(8,128)}, f32[8,256,16,16]{1,3,2,0:T(8,128)S(1)}, u32[]{:S(2)}) copy-start(f32[8,256,16,16]{1,3,2,0:T(8,128)S(1)} %multiply_multiply_fusion.2) | copy-start | bytes 6291460
  504.6 1.9 copy-start.56
  504.6 2.0 copy-start.38
  506.5 5.0 copy-start.53
  586.1 2.0 copy-start.61
  586.1 203.0 %all-gather.18.cloned.1.call-start = ((), (), s32[]{:S(2)}) async-start(), calls=%async_computation.8 | async-start | bytes 11976704 | tf_op jit(solution)/shard_map/all_gather | solution.py:229
  586.7 382.7 %all-gather.20.cloned.1.call-start = ((), (), s32[]{:S(2)}) async-start(), calls=%async_computation.9 | async-start | bytes 11976704 | tf_op jit(solution)/shard_map/all_gather | solution.py:230
  587.3 562.6 %all-gather.22.cloned.1.call-start = ((), (), s32[]{:S(2)}) async-start(), calls=%async_computation.10 | async-start | bytes 11976704 | tf_op jit(solution)/shard_map/all_gather | solution.py:231
  588.0 606.0 %all-reduce.10.cloned.1.call-start = ((), (), s32[]{:S(2)}) async-start(), calls=%async_computation.11 | async-start | bytes 2097152 | tf_op jit(solution)/shard_map/psum | solution.py:253
  616.8 579.4 %copy-start = (f32[256,2048]{1,0:T(8,128)}, f32[256,2048]{1,0:T(8,128)S(1)}, u32[]{:S(2)}) copy-start(f32[256,2048]{1,0:T(8,128)S(1)} %get-tuple-element.383) | copy-start | bytes 6291460
  616.8 181.4 %copy-start.50 = (f32[256]{0:T(256)}, f32[256]{0:T(256)S(1)}, u32[]{:S(2)}) copy-start(f32[256]{0:T(256)S(1)} %add_rsqrt_fusion) | copy-start | bytes 3076
  1149.9 19.0 slice-start
  1149.9 19.0 slice-start.1
  1161.6 7.3 copy-start.11
  1161.6 7.3 copy-start.8
  1161.6 7.3 slice-start.2
  1173.1 179.8 %all-gather.26.cloned.1.call-start = ((), (), s32[]{:S(2)}) async-start(), calls=%async_computation.16 | async-start | bytes 9504768 | tf_op jit(solution)/shard_map/all_gather | solution.py:32
  1194.0 2.2 copy-start.19
  1194.0 2.2 copy-start.21
  1196.2 2.2 copy-start.18
  1196.2 2.6 copy-start.39
  1197.7 2.5 copy-start.4
  1200.2 2.7 copy-start.40
  1203.8 269.9 %all-reduce.12.cloned.1.call-start = ((), (), s32[]{:S(2)}) async-start(), calls=%async_computation.17 | async-start | bytes 4194304 | tf_op jit(solution)/shard_map/psum | solution.py:240
  1234.0 8.9 copy-start.27
  1234.0 8.9 copy-start.49
  1234.0 8.9 copy-start.60
  1242.9 34.3 %copy-start.41 = (f32[256,1024]{0,1:T(8,128)S(1)}, f32[256,1024]{0,1:T(8,128)}, u32[]{:S(2)}) copy-start(f32[256,1024]{0,1:T(8,128)} %copy-done.40) | copy-start | bytes 3145732
  1243.0 34.3 %copy-start.55 = (f32[8,256]{1,0:T(8,128)S(1)}, f32[8,256]{1,0:T(8,128)}, u32[]{:S(2)}) copy-start(f32[8,256]{1,0:T(8,128)} %copy-done.53) | copy-start | bytes 24580
  1279.7 1.7 copy-start.29
  1279.8 1.8 copy-start.34
  1279.8 1.8 copy-start.43
  1283.2 3.2 copy-start.14
  1284.4 2.0 copy-start.44
  1352.9 45.2 %copy-start.52 = (f32[256]{0:T(256)S(1)}, f32[256]{0:T(256)}, u32[]{:S(2)}) copy-start(f32[256]{0:T(256)} %copy-done.51) | copy-start | bytes 3076
  1399.6 1.8 copy-start.37
  1401.4 3.2 copy-start.15
  1401.4 5.1 copy-start.62
  1404.6 3.3 copy-start.22
  1409.7 605.8 %reduce-scatter.4.cloned.1.call-start = ((), (), s32[]{:S(2)}) async-start(), calls=%async_computation.12 | async-start | bytes 23953408 | tf_op jit(solution)/shard_map/reduce_scatter | solution.py:261
  1420.9 1064.5 %reduce-scatter.6.cloned.1.call-start = ((), (), s32[]{:S(2)}) async-start(), calls=%async_computation.13 | async-start | bytes 23953408 | tf_op jit(solution)/shard_map/reduce_scatter | solution.py:262
  1432.2 1525.5 %reduce-scatter.8.cloned.1.call-start = ((), (), s32[]{:S(2)}) async-start(), calls=%async_computation.14 | async-start | bytes 23953408 | tf_op jit(solution)/shard_map/reduce_scatter | solution.py:263
  1443.6 1.7 copy-start.35
  1449.7 6.3 copy-start.3
  1449.7 6.3 copy-start.45
  1449.7 159.6 %all-to-all-start.1 = ((bf16[16,1024,128]{2,1,0:T(8,128)(2,1)}), bf16[16,1024,128]{2,1,0:T(8,128)(2,1)}, u32[]{:S(2)}, u32[]{:S(2)}) async-start(bf16[16,1024,128]{2,1,0:T(8,128)(2,1)} %bitcast.182), calls=%async_computation.1 | async-start | bytes 8388608 | tf_op jit(solution)/shard_map/all_to_all | solution.py:58
  1609.3 234.1 %all-to-all-start = ((bf16[16,128,1281]{1,2,0:T(8,128)(2,1)}), bf16[16,128,1281]{1,2,0:T(8,128)(2,1)}, u32[]{:S(2)}, u32[]{:S(2)}) async-start(bf16[16,128,1281]{1,2,0:T(8,128)(2,1)} %concatenate.21), calls=%async_computation | async-start | bytes 10551296 | tf_op jit(solution)/shard_map/all_to_all | solution.py:58
  1836.7 3.9 copy-start.1
  1836.7 3.9 copy-start.17
  1836.7 3.9 copy-start.36
  (17 other events, 24.4 us)
Sparse Core Ops, SparseCore 0:
  10.8 83.4 all-gather.13
  101.4 387.8 all-gather.23
  492.0 89.0 all-gather.15
  586.2 22.4 all-reduce.7
  611.6 177.3 all-gather.17
  792.0 177.3 all-gather.19
  972.5 177.3 all-gather.21
  1173.2 20.7 all-reduce.9
  1204.0 148.8 all-gather.25
  1409.8 22.3 all-reduce.11
  1435.3 580.1 reduce-scatter.3
  2018.3 467.0 reduce-scatter.5
  2488.4 469.3 reduce-scatter.7
where the time goes:
time: 2990 us; the launch traced here: 2960 us
  waiting for transfers between devices  2120 us (71%)
  blocking collectives  513 us (17%)
  matrix products  138 us (5%)
  local copies, waits for them, and re-layouts  105 us (4%)
  other arithmetic  39.3 us (1%)
    reduce_scatter x1, waiting for transfers between devices, body(): lax.psum_scatter(transposed_left(hidden, cotangent), 'seq', scatter_dimen...  472 us
    reduce_scatter x1, waiting for transfers between devices, body(): lax.psum_scatter(transposed_left(low_two, d_up), 'seq', scatter_dimension...  470 us
    unnamed x3, blocking collectives  290 us
    all_gather x1, waiting for transfers between devices, carried_in(): gathered = jax.tree.map(lambda a: lax.all_gather(a, axis), part)  235 us
    all_gather x1, waiting for transfers between devices, body(): lax.all_gather(w_down, 'seq', axis=1, tiled=True)  171 us
    all_gather x1, waiting for transfers between devices, body(): lax.all_gather(w_up, 'seq', axis=0, tiled=True)  171 us
    all_gather x1, waiting for transfers between devices, body(): lax.all_gather(w_gate, 'seq', axis=0, tiled=True)  171 us
    reduce_scatter x1, waiting for transfers between devices, body(): lax.psum_scatter(transposed_left(low_two, d_gate), 'seq', scatter_dimensi...  166 us
  transfers between devices with their start and end apart: 15, of which 12 were waited for; matrix products, arithmetic and copies ran while one was open for 6% of the time, Pallas kernels for 0%

commit v1 on v0

v1 whole, which is shorter than its diff:
```python
import functools

import jax
import jax.numpy as jnp
import numpy as np
from jax import lax
from jax.experimental import pallas as pl
from jax.experimental.pallas import tpu as pltpu
from jax.sharding import PartitionSpec as P

MESH = pl.DeviceIdType.MESH
HEADS = 16
FEAT = 16
CUBE = 8
UNITS = 352
EPS = 1e-06
F32 = jnp.float32
BF16 = jnp.bfloat16
ORDERS = ((0, 1, 2), (1, 2, 0), (2, 0, 1))
PIECES = ((0, 48), (48, 48), (96, 32))
MIB = 1 << 20


def flip(place, mask):
    total = 0
    for b in range(3):
        bit = (place // (1 << b)) % 2
        total = total + ((1 - bit) if (mask >> b) & 1 else bit) * (1 << b)
    return total


def subsets(dims):
    out = [0]
    for d in dims:
        out = out + [r | (1 << d) for r in out]
    return out


def whereabouts():
    s = lax.axis_index("seq")
    t = lax.axis_index("tensor")
    j = s % CUBE
    return s, t, j, s - j


def remote(src, dst, send, recv, device):
    return pltpu.make_async_remote_copy(
        src_ref=src, dst_ref=dst, send_sem=send, recv_sem=recv, device_id=device, device_id_type=MESH
    )


def greet(devices):
    barrier = pltpu.get_barrier_semaphore()
    for device in devices:
        pl.semaphore_signal(barrier, inc=1, device_id=device, device_id_type=MESH)
    pl.semaphore_wait(barrier, len(devices))


def near():
    s, t, j, base = whereabouts()
    return [(base + flip(j, 1 << d), t) for d in range(3)] + [(s, 1 - t)]


def greet_all(n):
    s, t, _, _ = whereabouts()
    barrier = pltpu.get_barrier_semaphore()

    def one(k, carry):
        pl.semaphore_signal(barrier, inc=1, device_id=((s + k) % n, t), device_id_type=MESH)
        return carry

    lax.fori_loop(1, n, one, 0)
    pl.semaphore_signal(barrier, inc=1, device_id=(s, 1 - t), device_id_type=MESH)
    pl.semaphore_wait(barrier, n)


class Gather:
    def __init__(self, own, full, sems):
        self.own, self.full = own, full
        self.ssem, self.rsem, self.csend, self.crecv, self.lsem = sems
        self.s, self.t, self.j, self.base = whereabouts()

    def view(self, r, i):
        off, rows = PIECES[i]
        return self.full.at[flip(self.j, r), self.t, pl.ds(off, rows)]

    def other(self, r, i):
        off, rows = PIECES[i]
        return self.full.at[flip(self.j, r), 1 - self.t, pl.ds(off, rows)]

    def hop(self, p, i, r):
        d = ORDERS[i][p]
        off, rows = PIECES[i]
        src = self.own.at[self.t, pl.ds(off, rows)] if r == 0 else self.view(r, i)
        k = r | (1 << d)
        return remote(src, self.view(r, i), self.ssem.at[i, k], self.rsem.at[i, k], (self.base + flip(self.j, 1 << d), self.t))

    def arrival(self, p, i, r):
        d = ORDERS[i][p]
        k = r | (1 << d)
        return remote(self.view(k, i), self.view(k, i), self.ssem.at[i, k], self.rsem.at[i, k], (self.base + flip(self.j, 1 << d), self.t))

    def across(self, r, i, mine):
        ref = self.view(r, i) if mine else self.other(r, i)
        return remote(ref, ref, self.csend.at[i, r], self.crecv.at[i, r], (self.s, 1 - self.t))

    def local(self):
        return pltpu.make_async_copy(self.own, self.full.at[self.j], self.lsem)

    def start(self, p):
        if p == 0:
            self.local().start()
        for i in range(3):
            for r in subsets(ORDERS[i][:p]):
                self.hop(p, i, r).start()

    def arrive(self, p):
        for i in range(3):
            for r in subsets(ORDERS[i][:p]):
                self.arrival(p, i, r).wait_recv()

    def share(self, p):
        for i in range(3):
            for r in subsets(ORDERS[i][:p]):
                self.across(r | (1 << ORDERS[i][p]), i, True).start()

    def finish(self):
        for i in range(3):
            for r in range(1, CUBE):
                self.across(r, i, False).wait_recv()
        for i in range(3):
            for r in range(1, CUBE):
                self.across(r, i, True).wait_send()
        for p in range(3):
            for i in range(3):
                for r in subsets(ORDERS[i][:p]):
                    self.hop(p, i, r).wait_send()
        self.local().wait()

    def run(self):
        for p in range(3):
            self.start(p)
            self.arrive(p)
            self.share(p)
        self.finish()


def gather_sems():
    return [pltpu.SemaphoreType.DMA((3, CUBE))] * 4 + [pltpu.SemaphoreType.DMA]


def gather_kernel(own, full, *sems):
    greet(near())
    Gather(own, full, sems).run()


def gather(x, number):
    rows, width = x.shape
    out = pl.pallas_call(
        gather_kernel,
        out_shape=jax.ShapeDtypeStruct((CUBE, 2, rows // 2, width), x.dtype),
        in_specs=[pl.BlockSpec(memory_space=pl.ANY)],
        out_specs=pl.BlockSpec(memory_space=pl.ANY),
        scratch_shapes=gather_sems(),
        compiler_params=pltpu.CompilerParams(collective_id=number, has_side_effects=True),
    )(x.reshape(2, rows // 2, width))
    return out.reshape(CUBE * rows, width)


SLOT = {0: 0, 1: 4, 2: 6}


def slot_of(p, i, r):
    kept = subsets(ORDERS[i][p + 1 :])
    return SLOT[p] + kept.index(r)


class Sum:
    def __init__(self, part, heap, total, sems):
        self.part, self.heap, self.total = part, heap, total
        self.csend, self.crecv, self.ssem, self.rsem, self.fsend, self.frecv = sems
        self.s, self.t, self.j, self.base = whereabouts()

    def across(self, r, mine):
        jj = flip(self.j, r)
        src = self.part.at[jj, 1 - self.t]
        return remote(src, self.heap.at[r], self.csend.at[r], self.crecv.at[r], (self.s, 1 - self.t))

    def hop(self, p, i, r):
        d = ORDERS[i][p]
        off, rows = PIECES[i]
        k = slot_of(p, i, r ^ (1 << d))
        return remote(
            self.part.at[flip(self.j, r), self.t, pl.ds(off, rows)],
            self.heap.at[CUBE + k, pl.ds(off, rows)],
            self.ssem.at[i, k],
            self.rsem.at[i, k],
            (self.base + flip(self.j, 1 << d), self.t),
        )

    def start(self):
        order = [7, 6, 5, 3, 4, 2, 1, 0]
        for r in order:
            self.across(r, True).start()
        for r in order:
            self.across(r, False).wait_recv()
            jj = flip(self.j, r)
            self.part[jj, self.t] = (self.part[jj, self.t].astype(F32) + self.heap[r].astype(F32)).astype(BF16)

    def phase(self, p):
        for i in range(3):
            d = ORDERS[i][p]
            for r in subsets(ORDERS[i][p + 1 :]):
                self.hop(p, i, r | (1 << d)).start()
        for i in range(3):
            d = ORDERS[i][p]
            off, rows = PIECES[i]
            for r in subsets(ORDERS[i][p + 1 :]):
                self.hop(p, i, r | (1 << d)).wait_recv()
                jj = flip(self.j, r)
                k = slot_of(p, i, r)
                mine = self.part[jj, self.t, pl.ds(off, rows)].astype(F32)
                new = mine + self.heap[CUBE + k, pl.ds(off, rows)].astype(F32)
                if p == 2:
                    self.total[self.t, pl.ds(off, rows)] = new
                else:
                    self.part[jj, self.t, pl.ds(off, rows)] = new.astype(BF16)

    def last(self):
        mine = self.total.at[self.t]
        cp = remote(mine, mine, self.fsend, self.frecv, (self.s, 1 - self.t))
        cp.start()
        theirs = self.total.at[1 - self.t]
        remote(theirs, theirs, self.fsend, self.frecv, (self.s, 1 - self.t)).wait_recv()
        cp.wait_send()

    def finish(self):
        for r in range(CUBE):
            self.across(r, True).wait_send()
        for p in range(3):
            for i in range(3):
                d = ORDERS[i][p]
                for r in subsets(ORDERS[i][p + 1 :]):
                    self.hop(p, i, r | (1 << d)).wait_send()

    def run(self):
        self.start()
        for p in range(3):
            self.phase(p)
        self.last()
        self.finish()


def sum_sems():
    return [
        pltpu.SemaphoreType.DMA((CUBE,)),
        pltpu.SemaphoreType.DMA((CUBE,)),
        pltpu.SemaphoreType.DMA((3, CUBE)),
        pltpu.SemaphoreType.DMA((3, CUBE)),
        pltpu.SemaphoreType.DMA,
        pltpu.SemaphoreType.DMA,
    ]


def sum_kernel(given, total, part, heap, lsem, *sems):
    greet(near())
    load = pltpu.make_async_copy(given, part, lsem)
    load.start()
    load.wait()
    Sum(part, heap, total, sems).run()


def cube_sum(x, number):
    rows, width = x.shape[0] // CUBE, x.shape[1]
    half = rows // 2
    out = pl.pallas_call(
        sum_kernel,
        out_shape=jax.ShapeDtypeStruct((2, half, width), F32),
        in_specs=[pl.BlockSpec(memory_space=pl.ANY)],
        out_specs=pl.BlockSpec(memory_space=pltpu.VMEM),
        scratch_shapes=[
            pltpu.VMEM((CUBE, 2, half, width), BF16),
            pltpu.VMEM((15, half, width), BF16),
            pltpu.SemaphoreType.DMA,
            *sum_sems(),
        ],
        compiler_params=pltpu.CompilerParams(collective_id=number, has_side_effects=True, vmem_limit_bytes=50 * MIB),
    )(x.reshape(CUBE, 2, half, width))
    return out.reshape(rows, width)


def columns_of(ref, s):
    if len(ref.shape) == 3:
        return ref.at[s]
    return ref.at[:, pl.ds(pl.multiple_of(s * 128, 128), 128)]


def columns_apart(n, rows, width):
    return (rows, width) if width // n % 128 == 0 else (n, rows, width // n)


def together(x):
    return x if x.ndim == 2 else x.transpose(1, 0, 2).reshape(x.shape[1], -1)


def apart(n, x):
    return x if x.shape[1] // n % 128 == 0 else x.reshape(x.shape[0], n, -1).transpose(1, 0, 2)


class Spread:
    def __init__(self, n, pack, full, sems):
        self.n, self.pack, self.full = n, pack, full
        self.ssem, self.rsem, self.lsem = sems
        self.s, self.t, self.j, self.base = whereabouts()

    def columns(self, s):
        return columns_of(self.full, s)

    def copy(self, k):
        to = (self.s + k) % self.n
        return remote(self.pack.at[to % CUBE], self.columns(self.s), self.ssem.at[k], self.rsem.at[k], (to, self.t))

    def arrival(self, k):
        at = (self.s + self.n - k) % self.n
        return remote(self.pack.at[0], self.columns(at), self.ssem.at[k], self.rsem.at[k], (at, self.t))

    def local(self):
        return pltpu.make_async_copy(self.pack.at[self.j], self.columns(self.s), self.lsem)

    def start(self):
        lax.fori_loop(1, self.n, lambda k, c: (self.copy(k).start(), c)[1], 0)
        self.local().start()

    def finish(self):
        self.local().wait()
        lax.fori_loop(1, self.n, lambda k, c: (self.arrival(k).wait_recv(), c)[1], 0)
        lax.fori_loop(1, self.n, lambda k, c: (self.copy(k).wait_send(), c)[1], 0)


class Back:
    def __init__(self, n, grads, tiles, sems):
        self.n, self.grads, self.tiles = n, grads, tiles
        self.ssem, self.rsem, self.lsem = sems
        self.s, self.t, self.j, self.base = whereabouts()

    def columns(self, s):
        return columns_of(self.grads, s)

    def copy(self, k):
        to = (self.s + k) % self.n
        return remote(self.columns(to), self.tiles.at[self.s], self.ssem.at[k], self.rsem.at[k], (to, self.t))

    def arrival(self, k):
        at = (self.s + self.n - k) % self.n
        return remote(self.tiles.at[at], self.tiles.at[at], self.ssem.at[k], self.rsem.at[k], (at, self.t))

    def local(self):
        return pltpu.make_async_copy(self.columns(self.s), self.tiles.at[self.s], self.lsem)

    start = Spread.start
    finish = Spread.finish


def spread_sems(n):
    return [pltpu.SemaphoreType.DMA((n,)), pltpu.SemaphoreType.DMA((n,)), pltpu.SemaphoreType.DMA]


def head_kernel(n, pack_a, pack_b, tokens, cot, w_a, w_b, tokens_all, cot_all, *sems):
    greet_all(n)
    first = Spread(n, pack_a, w_a, sems[0:3])
    second = Spread(n, pack_b, w_b, sems[3:6])
    g_tok = Gather(tokens, tokens_all, sems[6:11])
    g_cot = Gather(cot, cot_all, sems[11:16])
    first.start()
    g_tok.start(0)
    second.start()
    for p in range(3):
        g_tok.arrive(p)
        if p < 2:
            g_tok.start(p + 1)
        else:
            g_cot.start(0)
        g_tok.share(p)
    for p in range(3):
        g_cot.arrive(p)
        if p < 2:
            g_cot.start(p + 1)
        g_cot.share(p)
    g_tok.finish()
    g_cot.finish()
    first.finish()
    second.finish()


def head_call(n, pack_a, pack_b, tokens, cot):
    rows, width = tokens.shape
    shape = (CUBE, 2, rows // 2, width)
    any_space = pl.BlockSpec(memory_space=pl.ANY)
    w_a, w_b, tok, ct = pl.pallas_call(
        functools.partial(head_kernel, n),
        out_shape=[
            jax.ShapeDtypeStruct(columns_apart(n, pack_a.shape[1], width), BF16),
            jax.ShapeDtypeStruct(columns_apart(n, pack_b.shape[1], width), BF16),
            jax.ShapeDtypeStruct(shape, BF16),
            jax.ShapeDtypeStruct(shape, BF16),
        ],
        in_specs=[any_space] * 4,
        out_specs=[any_space] * 4,
        scratch_shapes=[*spread_sems(n), *spread_sems(n), *gather_sems(), *gather_sems()],
        compiler_params=pltpu.CompilerParams(collective_id=0, has_side_effects=True),
    )(pack_a, pack_b, tokens.reshape(2, rows // 2, width), cot.reshape(2, rows // 2, width))
    return together(w_a), together(w_b), tok.reshape(-1, width), ct.reshape(-1, width)


def back_kernel(n, grads, tiles, *sems):
    greet_all(n)
    back = Back(n, grads, tiles, sems)
    back.start()
    back.finish()


def back_call(n, grads, number):
    rows, width = grads.shape
    any_space = pl.BlockSpec(memory_space=pl.ANY)
    return pl.pallas_call(
        functools.partial(back_kernel, n),
        out_shape=jax.ShapeDtypeStruct((n, rows, width // n), BF16),
        in_specs=[any_space],
        out_specs=any_space,
        scratch_shapes=spread_sems(n),
        compiler_params=pltpu.CompilerParams(collective_id=number, has_side_effects=True),
    )(apart(n, grads))


def dot(a, b):
    return jnp.dot(a, b, preferred_element_type=F32)


def dot_nt(a, b):
    return lax.dot_general(a, b, (((1,), (1,)), ((), ())), preferred_element_type=F32)


def dot_tn(a, b):
    return lax.dot_general(a, b, (((0,), (0,)), ((), ())), preferred_element_type=F32)


def spreaders():
    first = np.repeat(np.eye(FEAT), FEAT, axis=1)
    second = np.tile(np.eye(FEAT), (1, FEAT))
    third = np.eye(FEAT, 128)
    return [jnp.asarray(m, BF16) for m in (first, second, third)]


ROOT_HALF = 0.5**0.5


def lift(u, keep, first, second, third):
    quad = dot(u, first) * dot(u, second) * (0.25 * ROOT_HALF) * keep
    lane = lax.broadcasted_iota(jnp.int32, (u.shape[0], 128), 1)
    line = (dot(u, third) * 0.5 + jnp.where(lane == FEAT, 1.0, 0.0)) * keep
    return quad.astype(BF16), line.astype(BF16)


def lift_back(u, d_quad, d_line, first, second):
    one, two = dot(u, first) * 0.5, dot(u, second) * 0.5
    back = dot_nt((d_quad * two).astype(BF16), first) + dot_nt((d_quad * one).astype(BF16), second)
    return back * ROOT_HALF + d_line[:, :FEAT]


def two_terms(x):
    high = x.astype(BF16)
    return high, (x - high.astype(F32)).astype(BF16)


def segments(start_two, start_three, first_position, count, axis):
    shape = (count, 1) if axis == 0 else (1, count)
    position = first_position + lax.broadcasted_iota(jnp.int32, shape, axis)
    return position, (position >= start_two).astype(jnp.int32) + (position >= start_three).astype(jnp.int32)


def pair_mask(two, three, at_t, at_s, block):
    pos_t, seg_t = segments(two, three, at_t, block, 0)
    pos_s, seg_s = segments(two, three, at_s, block, 1)
    return (pos_s <= pos_t) & (seg_s == seg_t)


def other_groups(groups):
    s, t, j, base = whereabouts()
    return [((s + CUBE * k) % (CUBE * groups), t) for k in range(1, groups)]


def exchange(groups, mine, theirs, ssem, rsem, before):
    s, t, j, base = whereabouts()
    c = s // CUBE
    for k, device in enumerate(other_groups(groups)):
        remote(mine, theirs.at[k], ssem.at[k], rsem.at[k], device).start()

    def finish():
        total = jnp.zeros(mine.shape, F32)
        for k, device in enumerate(other_groups(groups)):
            remote(mine, theirs.at[k], ssem.at[k], rsem.at[k], device).wait_recv()
            source = (c + groups - (k + 1)) % groups
            counts = (source < c) if before else (source > c)
            total = total + jnp.where(counts, theirs[k], 0.0)
        for k, device in enumerate(other_groups(groups)):
            remote(mine, theirs.at[k], ssem.at[k], rsem.at[k], device).wait_send()
        return total

    return finish


BLOCK = 256


def attend_kernel(
    groups, lengths, x_ref, w_ref, first, second, third,
    low_ref, q_ref, k_ref, v_ref, y_ref, den_ref, state_ref,
    state_mine, state_theirs, ssem, rsem,
):
    step = pl.program_id(0)
    steps = pl.num_programs(0)
    s, t, j, base = whereabouts()
    rows = x_ref.shape[0]
    two, three = lengths[0], lengths[0] + lengths[1]
    start = base * rows
    here = pl.ds(pl.multiple_of(step * rows, rows), rows)

    @pl.when(step == 0)
    def _():
        greet(other_groups(groups))
        state_mine[...] = jnp.zeros_like(state_mine)

    x = x_ref[...].astype(F32)
    root = lax.rsqrt(jnp.mean(x * x, axis=-1, keepdims=True) + EPS)
    low = (x * root * w_ref[160:161, :].astype(F32)).astype(BF16)
    low_ref[...] = low
    q = dot_nt(low, w_ref[128:144, :]).astype(BF16)
    k = dot_nt(low, w_ref[144:160, :]).astype(BF16)
    v = dot_nt(low, w_ref[0:128, :]).astype(BF16)
    lane = lax.broadcasted_iota(jnp.int32, (rows, 128), 1)
    v_ext = jnp.concatenate([v, jnp.where(lane < 2, 1.0, 0.0).astype(BF16)], axis=1)
    q_ref[here, :] = q
    k_ref[here, :] = k
    v_ref[here, :] = v_ext
    _, seg = segments(two, three, start + step * rows, rows, 0)
    quad, line = lift(k, (seg == 1).astype(F32), first[...], second[...], third[...])
    state_mine[0:256, :] += dot_tn(quad, v_ext)
    state_mine[256:384, :] += dot_tn(line, v_ext)

    @pl.when(step == steps - 1)
    def _():
        done = exchange(groups, state_mine, state_theirs, ssem, rsem, True)
        total = q_ref.shape[0]

        def outer(tb, carry):
            tq = pl.ds(pl.multiple_of(tb * BLOCK, BLOCK), BLOCK)
            qt = q_ref[tq, :]

            def inner(sb, acc):
                sq = pl.ds(pl.multiple_of(sb * BLOCK, BLOCK), BLOCK)
                score = dot_nt(qt, k_ref[sq, :]) * 0.25
                mask = pair_mask(two, three, start + tb * BLOCK, start + sb * BLOCK, BLOCK)
                weight = jnp.where(mask, 1.0 + score + 0.5 * score * score, 0.0).astype(BF16)
                return acc + dot(weight, v_ref[sq, :])

            acc = lax.fori_loop(0, tb + 1, inner, jnp.zeros((BLOCK, 256), F32))
            y_ref[tq, :] = acc[:, :128]
            den_ref[tq, :] = acc[:, 128:]
            return carry

        lax.fori_loop(0, total // BLOCK, outer, 0)
        state = done()
        state_ref[...] = state
        high, lowp = two_terms(state)

        def late(tb, carry):
            tq = pl.ds(pl.multiple_of(tb * BLOCK, BLOCK), BLOCK)
            _, seg = segments(two, three, start + tb * BLOCK, BLOCK, 0)
            quad, line = lift(q_ref[tq, :], (seg == 1).astype(F32), first[...], second[...], third[...])
            more = dot(quad, high[0:256]) + dot(quad, lowp[0:256]) + dot(line, high[256:384]) + dot(line, lowp[256:384])
            num = y_ref[tq, :] + more[:, :128]
            den = den_ref[tq, :] + more[:, 128:]
            den_ref[tq, :] = den
            y_ref[tq, :] = num / den[:, 0:1]
            return carry

        lax.fori_loop(0, total // BLOCK, late, 0)


def attend_call(n, lengths, x_all, w_a):
    groups = n // CUBE
    count, width = x_all.shape
    rows = count // CUBE
    vm = pl.BlockSpec(memory_space=pltpu.VMEM)
    whole = lambda *shape: pl.BlockSpec(shape, lambda i: (0,) * len(shape))
    peers = max(groups - 1, 1)
    return pl.pallas_call(
        functools.partial(attend_kernel, groups),
        grid=(CUBE,),
        out_shape=[
            jax.ShapeDtypeStruct((count, width), BF16),
            jax.ShapeDtypeStruct((count, FEAT), BF16),
            jax.ShapeDtypeStruct((count, FEAT), BF16),
            jax.ShapeDtypeStruct((count, 256), BF16),
            jax.ShapeDtypeStruct((count, 128), F32),
            jax.ShapeDtypeStruct((count, 128), F32),
            jax.ShapeDtypeStruct((384, 256), F32),
        ],
        in_specs=[
            pl.BlockSpec(memory_space=pltpu.SMEM),
            pl.BlockSpec((rows, width), lambda i: (i, 0)),
            whole(*w_a.shape),
            whole(FEAT, 256),
            whole(FEAT, 256),
            whole(FEAT, 128),
        ],
        out_specs=[
            pl.BlockSpec((rows, width), lambda i: (i, 0)),
            whole(count, FEAT),
            whole(count, FEAT),
            whole(count, 256),
            whole(count, 128),
            whole(count, 128),
            whole(384, 256),
        ],
        scratch_shapes=[
            pltpu.VMEM((384, 256), F32),
            pltpu.VMEM((peers, 384, 256), F32),
            pltpu.SemaphoreType.DMA((peers,)),
            pltpu.SemaphoreType.DMA((peers,)),
        ],
        compiler_params=pltpu.CompilerParams(collective_id=1, has_side_effects=True, vmem_limit_bytes=50 * MIB),
    )(lengths, x_all, w_a, *spreaders())


def attend_back_kernel(
    groups, lengths, q_ref, k_ref, v_ref, y_ref, den_ref, state_ref, dy_ref, first, second, third,
    dq_ref, dk_ref, dv_ref,
    c_ref, da, db, dv, state_mine, state_theirs, ssem, rsem,
):
    s, t, j, base = whereabouts()
    total = q_ref.shape[0]
    blocks = total // BLOCK
    two, three = lengths[0], lengths[0] + lengths[1]
    start = base * (total // CUBE)
    greet(other_groups(groups))
    state_mine[...] = jnp.zeros_like(state_mine)
    db[...] = jnp.zeros_like(db)
    dv[...] = jnp.zeros_like(dv)
    state = state_ref[...].astype(BF16)

    def early(tb, carry):
        tq = pl.ds(pl.multiple_of(tb * BLOCK, BLOCK), BLOCK)
        _, seg = segments(two, three, start + tb * BLOCK, BLOCK, 0)
        keep = (seg == 1).astype(F32)
        c = (dy_ref[tq, :].astype(F32) / den_ref[tq, 0:1]).astype(BF16)
        m = -jnp.sum(c.astype(F32) * y_ref[tq, :], axis=-1, keepdims=True)
        m_high = m.astype(BF16).astype(F32)
        lane = lax.broadcasted_iota(jnp.int32, (BLOCK, 128), 1)
        extra = jnp.where(lane == 0, m_high, jnp.where(lane == 1, m - m_high, 0.0)).astype(BF16)
        c_ext = jnp.concatenate([c, extra], axis=1)
        c_ref[tq, :] = c_ext
        u = q_ref[tq, :]
        quad, line = lift(u, keep, first[...], second[...], third[...])
        state_mine[0:256, :] += dot_tn(quad, c_ext)
        state_mine[256:384, :] += dot_tn(line, c_ext)
        d_quad = dot_nt(c_ext, state[0:256]) * keep
        d_line = dot_nt(c_ext, state[256:384]) * keep
        da[tq, :] = lift_back(u, d_quad, d_line, first[...], second[...])
        return carry

    lax.fori_loop(0, blocks, early, 0)
    done = exchange(groups, state_mine, state_theirs, ssem, rsem, False)

    def outer(tb, carry):
        tq = pl.ds(pl.multiple_of(tb * BLOCK, BLOCK), BLOCK)
        qt = q_ref[tq, :]
        ct = c_ref[tq, :]

        def inner(sb, acc):
            sq = pl.ds(pl.multiple_of(sb * BLOCK, BLOCK), BLOCK)
            ks = k_ref[sq, :]
            score = dot_nt(qt, ks) * 0.25
            d_w = dot_nt(ct, v_ref[sq, :])
            mask = pair_mask(two, three, start + tb * BLOCK, start + sb * BLOCK, BLOCK)
            weight = jnp.where(mask, 1.0 + score + 0.5 * score * score, 0.0).astype(BF16)
            inner_grad = jnp.where(mask, d_w * (1.0 + score), 0.0).astype(BF16)
            db[sq, :] += dot_tn(inner_grad, qt) * 0.5
            dv[sq, :] += dot_tn(weight, ct)[:, :128]
            return acc + dot(inner_grad, ks)

        acc = lax.fori_loop(0, tb + 1, inner, jnp.zeros((BLOCK, FEAT), F32))
        dq_ref[tq, :] = ((da[tq, :] + acc * 0.5) * 0.5).astype(BF16)
        return carry

    lax.fori_loop(0, blocks, outer, 0)
    state_back = done().astype(BF16)

    def late(sb, carry):
        sq = pl.ds(pl.multiple_of(sb * BLOCK, BLOCK), BLOCK)
        _, seg = segments(two, three, start + sb * BLOCK, BLOCK, 0)
        keep = (seg == 1).astype(F32)
        u = k_ref[sq, :]
        v = v_ref[sq, :]
        quad, line = lift(u, keep, first[...], second[...], third[...])
        d_quad = dot_nt(v, state_back[0:256]) * keep
        d_line = dot_nt(v, state_back[256:384]) * keep
        more = dot(quad, state_back[0:256]) + dot(line, state_back[256:384])
        dk_ref[sq, :] = ((db[sq, :] + lift_back(u, d_quad, d_line, first[...], second[...])) * 0.5).astype(BF16)
        dv_ref[sq, :] = (dv[sq, :] + more[:, :128]).astype(BF16)
        return carry

    lax.fori_loop(0, blocks, late, 0)


def attend_back_call(n, lengths, q, k, v, y, den, state, dy):
    groups = n // CUBE
    count = q.shape[0]
    vm = pl.BlockSpec(memory_space=pltpu.VMEM)
    peers = max(groups - 1, 1)
    return pl.pallas_call(
        functools.partial(attend_back_kernel, groups),
        out_shape=[
            jax.ShapeDtypeStruct((count, FEAT), BF16),
            jax.ShapeDtypeStruct((count, FEAT), BF16),
            jax.ShapeDtypeStruct((count, 128), BF16),
        ],
        in_specs=[pl.BlockSpec(memory_space=pltpu.SMEM)] + [vm] * 10,
        out_specs=[vm] * 3,
        scratch_shapes=[
            pltpu.VMEM((count, 256), BF16),
            pltpu.VMEM((count, FEAT), F32),
            pltpu.VMEM((count, FEAT), F32),
            pltpu.VMEM((count, 128), F32),
            pltpu.VMEM((384, 256), F32),
            pltpu.VMEM((peers, 384, 256), F32),
            pltpu.SemaphoreType.DMA((peers,)),
            pltpu.SemaphoreType.DMA((peers,)),
        ],
        compiler_params=pltpu.CompilerParams(collective_id=2, has_side_effects=True, vmem_limit_bytes=50 * MIB),
    )(lengths, q, k, v, y, den, state, dy, *spreaders())


def units_first(w):
    return jnp.pad(w, ((0, CUBE * UNITS - w.shape[0]), (0, 0))).reshape(CUBE, UNITS, w.shape[1])


def body(
    n, tokens, gain_attn, w_query, w_key, w_value, w_output, gain_mlp, w_gate, w_up, w_down, seq_lengths, cotangent
):
    per = HEADS // lax.axis_size("tensor")
    gains = jnp.concatenate([gain_attn[None], gain_mlp[None], jnp.zeros((14, gain_attn.shape[0]), BF16)], axis=0)
    pack_a = jnp.concatenate(
        [
            w_value.T.reshape(per, 128, -1),
            w_query.T.reshape(per, FEAT, -1),
            w_key.T.reshape(per, FEAT, -1),
            jnp.broadcast_to(gains[None], (per, *gains.shape)),
            w_output.reshape(per, 128, -1),
        ],
        axis=1,
    )
    pack_b = jnp.concatenate([units_first(w_gate.T), units_first(w_up.T), units_first(w_down)], axis=1)
    w_a, w_b, tokens_all, cot_all = head_call(n, pack_a, pack_b, tokens, cotangent)
    gate_w, up_w, down_w = w_b[:UNITS], w_b[UNITS : 2 * UNITS], w_b[2 * UNITS :]
    out_w = w_a[176:304]

    low_one, q, k, v, y, den, state = attend_call(n, seq_lengths, tokens_all, w_a)
    attn_low = y.astype(BF16)
    attn_out = cube_sum(dot(attn_low, out_w).astype(BF16), 3)

    inputs = tokens.astype(F32)
    mid = inputs + attn_out
    gain_two = w_a[161:162].astype(F32)
    root_two = lax.rsqrt(jnp.mean(mid * mid, axis=-1, keepdims=True) + EPS)
    normed_two = mid * root_two
    low_two = gather((normed_two * gain_two).astype(BF16), 4)

    gate = dot_nt(low_two, gate_w)
    up = dot_nt(low_two, up_w)
    sigma = jax.nn.sigmoid(gate)
    silu = gate * sigma
    hidden = (silu * up).astype(BF16)
    out_part = dot(hidden, down_w).astype(BF16)
    d_hidden = dot_nt(cot_all, down_w)
    d_gate = (d_hidden * up * sigma * (1.0 + gate * (1.0 - sigma))).astype(BF16)
    d_up = (d_hidden * silu).astype(BF16)
    d_low_part = (dot(d_gate, gate_w) + dot(d_up, up_w)).astype(BF16)
    d_low_two = cube_sum(d_low_part, 5)
    output = (mid + cube_sum(out_part, 6)).astype(BF16)
    grads_b = jnp.concatenate(
        [dot_tn(d_gate, low_two), dot_tn(d_up, low_two), dot_tn(hidden, cot_all)], axis=0
    ).astype(BF16)

    scaled = d_low_two * gain_two
    d_mid = cotangent.astype(F32) + root_two * (
        scaled - normed_two * jnp.mean(scaled * normed_two, axis=-1, keepdims=True)
    )
    d_attn = gather(d_mid.astype(BF16), 7)
    dy = dot_nt(d_attn, out_w).astype(BF16)
    dq, dk, dv = attend_back_call(n, seq_lengths, q, k, v, y, den, state, dy)
    d_low_one = cube_sum(
        (dot(dv, w_a[0:128]) + dot(dq, w_a[128:144]) + dot(dk, w_a[144:160])).astype(BF16), 8
    )
    grads_a = jnp.concatenate(
        [dot_tn(dv, low_one), dot_tn(dq, low_one), dot_tn(dk, low_one), dot_tn(attn_low, d_attn)], axis=0
    ).astype(BF16)
    root_one = lax.rsqrt(jnp.mean(inputs * inputs, axis=-1, keepdims=True) + EPS)
    normed_one = inputs * root_one
    scaled = d_low_one * w_a[160:161].astype(F32)
    grad_tokens = d_mid + root_one * (
        scaled - normed_one * jnp.mean(scaled * normed_one, axis=-1, keepdims=True)
    )

    def arrived(grads, number):
        tiles = back_call(n, grads, number)
        return tiles.reshape(-1, CUBE, *tiles.shape[1:]).astype(F32).sum(axis=0)

    back_b = arrived(grads_b, 9)
    back_a = arrived(grads_a, 10)

    def units(part):
        return part.reshape(CUBE * UNITS, -1)[: w_gate.shape[1]]

    grad_gate = units(back_b[:, :UNITS]).T
    grad_up = units(back_b[:, UNITS : 2 * UNITS]).T
    grad_down = units(back_b[:, 2 * UNITS :])
    grad_value = back_a[:, 0:128].reshape(per * 128, -1).T
    grad_query = back_a[:, 128:144].reshape(per * FEAT, -1).T
    grad_key = back_a[:, 144:160].reshape(per * FEAT, -1).T
    grad_output = back_a[:, 160:288].reshape(per * 128, -1)

    def weighed(*pairs):
        return sum(jnp.sum(w.astype(F32) * g, axis=1) for w, g in pairs)

    gain_one_part = weighed((w_value, grad_value), (w_query, grad_query), (w_key, grad_key))
    gain_two_part = weighed((w_gate, grad_gate), (w_up, grad_up))
    both = lax.psum(jnp.stack([gain_one_part, gain_two_part]), "tensor")
    grad_gain_one = both[0] / gain_attn.astype(F32)
    grad_gain_two = both[1] / gain_mlp.astype(F32)
    return (
        output,
        grad_tokens,
        grad_gain_one,
        grad_query,
        grad_key,
        grad_value,
        grad_output,
        grad_gain_two,
        grad_gate,
        grad_up,
        grad_down,
    )


def solution(mesh):
    return jax.shard_map(
        functools.partial(body, mesh.shape["seq"]),
        mesh=mesh,
        in_specs=(
            P("seq", None),
            P("seq"),
            P("seq", "tensor"),
            P("seq", "tensor"),
            P("seq", "tensor"),
            P("tensor", "seq"),
            P("seq"),
            P("seq", "tensor"),
            P("seq", "tensor"),
            P("tensor", "seq"),
            P(),
            P("seq", None),
        ),
        out_specs=(
            P("seq", None),
            P("seq", None),
            P("seq"),
            P("seq", "tensor"),
            P("seq", "tensor"),
            P("seq", "tensor"),
            P("tensor", "seq"),
            P("seq"),
            P("seq", "tensor"),
            P("seq", "tensor"),
            P("tensor", "seq"),
        ),
        check_vma=False,
    )
```

time: 2990 us -> 864 us (0.29)
  waiting for transfers between devices: 2120 us -> 0 us
  Pallas kernels: 0 us -> 695 us
  blocking collectives: 513 us -> 3.29 us
  local copies, waits for them, and re-layouts: 105 us -> 19.1 us
    reduce_scatter x3 -> x0, waiting for transfers between devices: 1110 us -> none  [the longest x1 472 us: body(): lax.psum_scatter(transposed_left(hidden, cotangent), 'seq', scatter_dimen...]
    all_gather x7 -> x0, waiting for transfers between devices: 894 us -> none  [the longest x1 235 us: carried_in(): gathered = jax.tree.map(lambda a: lax.all_gather(a, axis), part)]
    pallas_call x0 -> x11, Pallas kernels: none -> 695 us  [the longest x4 210 us: cube_sum(): pl.pallas_call(sum_kernel, out_shape=jax.ShapeDtypeStruct((2, half, width...]
    unnamed x3 -> x0, blocking collectives: 290 us -> none
    all_gather x6 -> x0, blocking collectives: 223 us -> none  [the longest x1 56.8 us: body(): lax.all_gather(w_query, 'seq', axis=0, tiled=True)]
    all_to_all x2 -> x0, waiting for transfers between devices: 97.9 us -> none  [summed_on_arrival(): lax.all_to_all(tiles, axis, split_axis=0, concat_axis=0, tiled=True)]
    concatenate x5 -> x2, local copies, waits for them, and re-layouts: 46.1 us -> 1.12 us  [the longest x1 1.04 us: body(): jnp.concatenate([w_value.T.reshape(per, 128, -1), w_query.T.reshape(per,...]
    dynamic_slice x40 -> x0, local copies, waits for them, and re-layouts: 34.7 us -> none  [the longest x32 27 us: hop(): part[at].astype(own.dtype)]
  transfers between devices with their start and end apart: 15 -> 0, of which waited for: 12 -> 0; matrix products, arithmetic and copies ran while one was open for 6% -> 0% of each run, Pallas kernels for 0% -> 0%
where the time goes in v1:
time: 864 us; the launch traced here: 855 us
  Pallas kernels  695 us (80%)
  matrix products  110 us (13%)
  other arithmetic  25.7 us (3%)
  local copies, waits for them, and re-layouts  19.1 us (2%)
    pallas_call x4, Pallas kernels, cube_sum(): pl.pallas_call(sum_kernel, out_shape=jax.ShapeDtypeStruct((2, half, width...  210 us
    pallas_call x1, Pallas kernels, head_call(): pl.pallas_call(functools.partial(head_kernel, n), out_shape=[jax.ShapeDty...  184 us
    pallas_call x2, Pallas kernels, back_call(): pl.pallas_call(functools.partial(back_kernel, n), out_shape=jax.ShapeDtyp...  143 us
    pallas_call x2, Pallas kernels, gather(): pl.pallas_call(gather_kernel, out_shape=jax.ShapeDtypeStruct((CUBE, 2, ro...  81.6 us
    dot_general x7, matrix products, dot(): return jnp.dot(a, b, preferred_element_type=F32)  66.1 us
    pallas_call x1, Pallas kernels, attend_call(): pl.pallas_call(functools.partial(attend_kernel, groups), grid=(CUBE,), ou...  42.9 us
    pallas_call x1, Pallas kernels, attend_back_call(): pl.pallas_call(functools.partial(attend_back_kernel, groups), out_shape=[...  33.6 us
    dot_general x4, matrix products, dot_nt(): lax.dot_general(a, b, (((1,), (1,)), ((), ())), preferred_element_type=F32)  25.7 us

profile of v1, /device:TPU:9, one launch (start us, length us, event | category | flops | bytes accessed | tf_op | source)
XLA Modules:
  0.0 854.9 jit_solution(13986726470953752830)
XLA Ops:
  0.8 0.9 maximum_maximum_fusion
  1.6 0.9 copy.37
  2.5 0.9 copy.36
  3.4 1.5 copy.39
  4.8 1.5 copy.40
  6.3 1.1 copy.35
  7.5 1.0 constant_dynamic-update-slice_fusion.pack_a
  8.8 0.6 copy-done.33
  9.4 1.5 pad_maximum_fusion.1.pack_b
  10.9 184.1 %shard_map.257 = (bf16[304,2048]{1,0:T(8,128)(2,1)}, bf16[1056,2048]{1,0:T(8,128)(2,1)}, bf16[8,2,128,2048]{3,2,1,0:T(8,128)(2,1)}, bf16[8,2,128,2048]{3,2,1,0:T(8,128)(2,1)}) custom-call(bf16[8,304,128]{2,1,0:T(8,128)(2,1)} %copy-done.33, bf16[8,1056,128]{2,1,0:T(8,128)(2,1)} %pad_maximum_fusion.1.pack_b, bf16[2,128,2048]{2,1,0:T(8,128)(2,1)} %bitcast.126, ...), custom_call_target="tpu_custom_call" | custom-call | tf_op jit(solution)/shard_map/pallas_call | solution.py:399
  195.0 1.4 slice_convert_fusion
  196.5 42.9 %shard_map.258 = (bf16[2048,2048]{1,0:T(8,128)(2,1)}, bf16[2048,16]{1,0:T(8,128)(2,1)S(1)}, bf16[2048,16]{1,0:T(8,128)(2,1)S(1)}, bf16[2048,256]{1,0:T(8,128)(2,...) custom-call(s32[3]{0:T(128)S(1)} %copy-done.16, bf16[2048,2048]{1,0:T(8,128)(2,1)} %bitcast.135, ...), custom_call_target="tpu_custom_call" | custom-call | tf_op jit(solution)/shard_map/pallas_call | solution.py:597
  239.4 7.0 convolution_convert_fusion.1
  246.5 52.5 %shard_map.259 = f32[2,128,2048]{2,1,0:T(8,128)S(1)} custom-call(bf16[8,2,128,2048]{3,2,1,0:T(8,128)(2,1)} %bitcast.125), custom_call_target="tpu_custom_call" | custom-call | tf_op jit(solution)/shard_map/pallas_call | solution.py:276
  299.4 1.3 multiply_convert_fusion.3
  300.7 40.8 %shard_map.260 = bf16[8,2,128,2048]{3,2,1,0:T(8,128)(2,1)} custom-call(bf16[2,128,2048]{2,1,0:T(8,128)(2,1)} %bitcast.140), custom_call_target="tpu_custom_call" | custom-call | tf_op jit(solution)/shard_map/pallas_call | solution.py:159
  341.5 6.7 fusion.13
  348.2 6.3 fusion.17
  354.4 9.0 %multiply_convert_fusion = (bf16[2048,352]{0,1:T(8,128)(2,1)S(1)}, bf16[2048,352]{0,1:T(8,128)(2,1)S(1)}, bf16[2048,352]{0,1:T(8,128)(2,1)S(1)}) fusion(f32[2048,352]{0,1:T(8,128)} %fusion.17, f32[2048,352]{0,1:T(8,128)S(1)} %fusion.13, bf16[2048,2048]{1,0:T(8,128)(2,1)} %bitcast.169, bf16[1056,2048]{1,0:T(8,128)(2,1)} %get-tuple-element.28), kind=kOutput, calls=%fused_computation.9 | convolution fusion | flops 2963603456 | bytes 19922944 | tf_op jit(solution)/shard_map/dot_general | solution.py:440
  363.5 3.2 convolution_convert_fusion.2
  366.8 3.2 convolution_convert_fusion.3
  370.0 3.6 convolution_convert_fusion.4
  373.6 2.4 pad_maximum_fusion.grads
  376.0 113.7 %shard_map.267 = bf16[16,1056,128]{2,1,0:T(8,128)(2,1)} custom-call(bf16[1056,2048]{1,0:T(8,128)(2,1)} %pad_maximum_fusion.grads), custom_call_target="tpu_custom_call" | custom-call | tf_op jit(solution)/shard_map/pallas_call | solution.py:425
  489.7 3.6 convert_reduce_fusion
  493.6 1.2 slice.93
  494.8 0.6 copy-done.28
  495.6 1.9 multiply_reduce_fusion.2
  497.5 0.5 add_bitcast_fusion
  498.1 7.0 convolution_convert_fusion
  505.0 54.9 %shard_map.261 = f32[2,128,2048]{2,1,0:T(8,128)S(1)} custom-call(bf16[8,2,128,2048]{3,2,1,0:T(8,128)(2,1)} %bitcast.130), custom_call_target="tpu_custom_call" | custom-call | tf_op jit(solution)/shard_map/pallas_call | solution.py:276
  560.0 1.4 copy-done.3
  561.3 8.1 fusion.15
  569.5 10.4 %add_convert_fusion.1 = bf16[2048,2048]{1,0:T(8,128)(2,1)} fusion(f32[2048,2048]{1,0:T(8,128)} %fusion.15, bf16[2048,352]{0,1:T(8,128)(2,1)S(1)} %copy-done.26, bf16[1056,2048]{1,0:T(8,128)(2,1)S(1)} %bitcast.150), kind=kOutput, calls=%fused_computation.1 | convolution fusion | flops 2961178624 | bytes 28049408 | tf_op jit(solution)/shard_map/dot_general | solution.py:436
  579.8 49.5 %shard_map.262 = f32[2,128,2048]{2,1,0:T(8,128)S(1)} custom-call(bf16[8,2,128,2048]{3,2,1,0:T(8,128)(2,1)} %bitcast.122), custom_call_target="tpu_custom_call" | custom-call | tf_op jit(solution)/shard_map/pallas_call | solution.py:276
  629.5 0.6 fusion.7
  630.1 0.6 add_rsqrt_fusion
  630.8 0.7 copy-done.22
  631.4 1.7 fusion.28
  633.1 40.8 %shard_map.263 = bf16[8,2,128,2048]{3,2,1,0:T(8,128)(2,1)} custom-call(bf16[2,128,2048]{2,1,0:T(8,128)(2,1)} %bitcast.141), custom_call_target="tpu_custom_call" | custom-call | tf_op jit(solution)/shard_map/pallas_call | solution.py:159
  674.0 4.8 convolution_convert_fusion.5
  678.8 0.9 copy-done.18
  679.7 3.7 convolution_convert_fusion.7.dy_ref
  683.5 33.6 %shard_map.264 = (bf16[2048,16]{1,0:T(8,128)(2,1)S(1)}, bf16[2048,16]{1,0:T(8,128)(2,1)S(1)}, bf16[2048,128]{1,0:T(8,128)(2,1)S(1)}) custom-call(s32[3]{0:T(128)S(1)} %copy-done.17, bf16[2048,16]{1,0:T(8,128)(2,1)S(1)} %copy-done.9, bf16[2048,16]{1,0:T(8,128)(2,1)S(1)} %copy-done.11, bf16[2048,256]{1,0:T(8,128)(2,1)} %copy-done.7, f32[2048,128]{1,0:T(8,128)} %copy-done.2, ...), custom_call_target="tpu_custom_call" | custom-call | tf_op jit(solution)/shard_map/pallas_call | solution.py:721
  717.2 1.2 convolution_convert_fusion.9
  718.4 1.2 convolution_convert_fusion.8
  719.6 1.3 convolution_convert_fusion.6
  720.9 1.1 pad_maximum_fusion.2.grads
  722.0 28.9 %shard_map.266 = bf16[16,288,128]{2,1,0:T(8,128)(2,1)} custom-call(bf16[288,2048]{1,0:T(8,128)(2,1)} %pad_maximum_fusion.2.grads), custom_call_target="tpu_custom_call" | custom-call | tf_op jit(solution)/shard_map/pallas_call | solution.py:425
  751.0 1.6 convert_reduce_fusion.1
  752.6 1.0 fusion.30
  753.7 0.7 copy.41
  754.5 0.7 copy.42
  755.2 2.0 copy.38
  757.2 1.2 multiply_reduce_fusion.4
  758.4 0.7 pad_maximum_fusion.3
  759.1 3.3 psum.7
  762.4 0.5 bitcast_divide_fusion
  762.9 9.1 %fusion.19 = f32[2048,2048]{1,0:T(8,128)} fusion(bf16[2048,128]{1,0:T(8,128)(2,1)S(1)} %get-tuple-element.35, bf16[304,2048]{1,0:T(8,128)(2,1)} %get-tuple-element.26.w_ref), kind=kOutput, calls=%fused_computation.55 | convolution fusion | flops 1073741824 | bytes 17825792 | tf_op jit(solution)/shard_map/dot_general | solution.py:436
  772.0 9.0 %fusion.26 = f32[2048,2048]{1,0:T(8,128)} fusion(bf16[2048,16]{1,0:T(8,128)(2,1)S(1)} %get-tuple-element.36, bf16[304,2048]{1,0:T(8,128)(2,1)} %get-tuple-element.26.w_ref), kind=kOutput, calls=%fused_computation.64 | convolution fusion | flops 134217728 | bytes 16908288 | tf_op jit(solution)/shard_map/dot_general | solution.py:436
  781.0 15.6 %add_convert_fusion = bf16[2048,2048]{1,0:T(8,128)(2,1)} fusion(f32[2048,2048]{1,0:T(8,128)} %fusion.19, f32[2048,2048]{1,0:T(8,128)} %fusion.26, bf16[2048,16]{1,0:T(8,128)(2,1)S(1)} %copy-done.6, bf16[304,2048]{1,0:T(8,128)(2,1)} %get-tuple-element.26.w_ref), kind=kOutput, calls=%fused_computation | convolution fusion | flops 146800640 | bytes 42074112 | tf_op jit(solution)/shard_map/dot_general | solution.py:436
  796.6 52.9 %shard_map.265 = f32[2,128,2048]{2,1,0:T(8,128)S(1)} custom-call(bf16[8,2,128,2048]{3,2,1,0:T(8,128)(2,1)} %bitcast.127), custom_call_target="tpu_custom_call" | custom-call | tf_op jit(solution)/shard_map/pallas_call | solution.py:276
  850.0 1.0 copy-done.1
  851.3 3.2 fusion.6
  (131 shorter events, 2.3 us)
Async XLA Ops:
  0.6 8.0 copy-start.27
  0.7 7.9 copy-start.35
  7.4 1.3 copy-start.29
  8.6 0.8 copy-start.33
  10.9 185.5 %copy-start.12 = (bf16[16,256]{1,0:T(8,128)(2,1)S(1)}, bf16[16,256]{1,0:T(8,128)(2,1)}, u32[]{:S(2)}) copy-start(bf16[16,256]{1,0:T(8,128)(2,1)} %constant.23.clone.second) | copy-start | bytes 24580
  10.9 185.5 %copy-start.13 = (bf16[16,256]{1,0:T(8,128)(2,1)S(1)}, bf16[16,256]{1,0:T(8,128)(2,1)}, u32[]{:S(2)}) copy-start(bf16[16,256]{1,0:T(8,128)(2,1)} %constant.22.clone.first) | copy-start | bytes 24580
  10.9 185.5 %copy-start.14 = (bf16[16,128]{1,0:T(8,128)(2,1)S(1)}, bf16[16,128]{1,0:T(8,128)(2,1)}, u32[]{:S(2)}) copy-start(bf16[16,128]{1,0:T(8,128)(2,1)} %constant.24.clone.third) | copy-start | bytes 12292
  10.9 185.5 %copy-start.16 = (s32[3]{0:T(128)S(1)}, s32[3]{0:T(128)}, u32[]{:S(2)}) copy-start(s32[3]{0:T(128)} %lengths.3) | copy-start | bytes 40
  196.4 102.9 %copy-start.36 = (f32[1,2048]{1,0:T(1,128)}, f32[1,2048]{1,0:T(1,128)S(1)}, u32[]{:S(2)}) copy-start(f32[1,2048]{1,0:T(1,128)S(1)} %get-tuple-element.65) | copy-start | bytes 24580
  239.4 7.1 copy-start.7
  239.4 7.1 copy-start.8
  239.4 7.1 copy-start.10
  239.4 434.5 %copy-start.2 = (f32[2048,128]{1,0:T(8,128)}, f32[2048,128]{1,0:T(8,128)S(1)}, u32[]{:S(2)}) copy-start(f32[2048,128]{1,0:T(8,128)S(1)} %get-tuple-element.27.y_ref) | copy-start | bytes 3145732
  246.5 52.5 %copy-start.19 = (bf16[256,2048]{1,0:T(8,128)(2,1)S(1)}, bf16[256,2048]{1,0:T(8,128)(2,1)}, u32[]{:S(2)}) copy-start(bf16[256,2048]{1,0:T(8,128)(2,1)} %param.18) | copy-start | bytes 3145732
  299.4 1.3 copy-start.42
  341.5 6.7 copy-start.24
  348.2 15.4 %slice-start.4 = ((s8[8388608]{0:T(1024)(128)(4,1)}), s8[4194304]{0:T(1024)(128)(4,1)S(1)}, s32[]{:S(2)}) async-start(s8[8388608]{0:T(1024)(128)(4,1)} %bitcast.170), calls=%async_computation.4 | async-start | bytes 8388608
  354.4 9.1 %slice-start.5 = ((s8[8388608]{0:T(1024)(128)(4,1)}), s8[4194304]{0:T(1024)(128)(4,1)S(1)}, s32[]{:S(2)}) async-start(s8[8388608]{0:T(1024)(128)(4,1)} %bitcast.170), calls=%async_computation.5 | async-start | bytes 8388608
  363.5 3.3 copy-start.50
  363.5 3.3 copy-start.25
  363.5 6.5 copy-start.31
  493.3 4.8 slice-start.2
  493.6 1.8 copy-start.28
  493.6 2.0 copy-start.30
  493.6 4.4 slice-start.3
  495.6 2.5 copy-start.51
  505.0 56.3 %copy-start.32 = (bf16[2048,352]{0,1:T(8,128)(2,1)S(1)}, bf16[2048,352]{0,1:T(8,128)(2,1)}, u32[]{:S(2)}) copy-start(bf16[2048,352]{0,1:T(8,128)(2,1)} %copy-done.31) | copy-start | bytes 4325380
  560.0 1.4 copy-start.3
  561.3 8.1 copy-start.26
  579.8 49.6 %copy-start.20 = (bf16[256,2048]{1,0:T(8,128)(2,1)S(1)}, bf16[256,2048]{1,0:T(8,128)(2,1)}, u32[]{:S(2)}) copy-start(bf16[256,2048]{1,0:T(8,128)(2,1)} %param.18) | copy-start | bytes 3145732
  579.8 49.6 %copy-start.37 = (f32[1,2048]{1,0:T(1,128)S(1)}, f32[1,2048]{1,0:T(1,128)}, u32[]{:S(2)}) copy-start(f32[1,2048]{1,0:T(1,128)} %copy-done.36) | copy-start | bytes 24580
  579.8 49.6 %copy-start.43 = (f32[256]{0:T(256)S(1)}, f32[256]{0:T(256)}, u32[]{:S(2)}) copy-start(f32[256]{0:T(256)} %copy-done.42) | copy-start | bytes 3076
  629.4 1.3 copy-start
  629.4 2.0 copy-start.22
  630.7 2.5 copy-start.46
  673.9 5.8 copy-start.18
  674.0 43.2 %slice-start = ((s8[8388608]{0:T(1024)(128)(4,1)}), s8[4194304]{0:T(1024)(128)(4,1)S(1)}, s32[]{:S(2)}) async-start(s8[8388608]{0:T(1024)(128)(4,1)} %bitcast.120), calls=%async_computation | async-start | bytes 8388608
  679.7 3.7 copy-start.9
  679.7 3.8 copy-start.11
  679.7 3.8 copy-start.15
  679.7 3.8 copy-start.17
  679.7 37.4 %slice-start.1 = ((s8[8388608]{0:T(1024)(128)(4,1)}), s8[4194304]{0:T(1024)(128)(4,1)S(1)}, s32[]{:S(2)}) async-start(s8[8388608]{0:T(1024)(128)(4,1)} %bitcast.120), calls=%async_computation.1 | async-start | bytes 8388608
  717.1 1.3 copy-start.5
  750.9 2.7 copy-start.40
  751.0 2.7 copy-start.39
  752.6 4.7 copy-start.34
  752.6 9.8 %copy-start.48 = (bf16[128]{0:T(256)(128)(2,1)S(1)}, bf16[128]{0:T(256)(128)(2,1)}, u32[]{:S(2)}) copy-start(bf16[128]{0:T(256)(128)(2,1)} %param.24) | copy-start | bytes 772
  752.6 9.8 %copy-start.49 = (bf16[128]{0:T(256)(128)(2,1)S(1)}, bf16[128]{0:T(256)(128)(2,1)}, u32[]{:S(2)}) copy-start(bf16[128]{0:T(256)(128)(2,1)} %param.19) | copy-start | bytes 772
  772.0 9.0 %copy-start.6 = (bf16[2048,16]{1,0:T(8,128)(2,1)S(1)}, bf16[2048,16]{1,0:T(8,128)(2,1)}, u32[]{:S(2)}) copy-start(bf16[2048,16]{1,0:T(8,128)(2,1)} %copy-done.5) | copy-start | bytes 196612
  796.5 52.9 %copy-start.21 = (bf16[256,2048]{1,0:T(8,128)(2,1)S(1)}, bf16[256,2048]{1,0:T(8,128)(2,1)}, u32[]{:S(2)}) copy-start(bf16[256,2048]{1,0:T(8,128)(2,1)} %param.18) | copy-start | bytes 3145732
  796.5 52.9 %copy-start.41 = (f32[1,2048]{1,0:T(1,128)S(1)}, f32[1,2048]{1,0:T(1,128)}, u32[]{:S(2)}) copy-start(f32[1,2048]{1,0:T(1,128)} %get-tuple-element.64) | copy-start | bytes 24580
  796.5 52.9 %copy-start.45 = (f32[256]{0:T(256)S(1)}, f32[256]{0:T(256)}, u32[]{:S(2)}) copy-start(f32[256]{0:T(256)} %get-tuple-element.72) | copy-start | bytes 3076
  796.6 53.5 %copy-start.4 = (f32[2,128,2048]{2,1,0:T(8,128)S(1)}, f32[2,128,2048]{2,1,0:T(8,128)}, u32[]{:S(2)}) copy-start(f32[2,128,2048]{2,1,0:T(8,128)} %copy-done.3) | copy-start | bytes 6291460
  849.5 1.6 copy-start.1
  849.5 1.8 copy-start.23
  849.5 1.8 copy-start.38
  849.5 1.8 copy-start.44
  849.5 1.8 copy-start.47

commit v2 on v1

--- a/solution.py
+++ b/solution.py
@@ -176,14 +176,15 @@
 
 
 class Sum:
+    ORDER = (7, 6, 5, 3, 4, 2, 1, 0)
+
     def __init__(self, part, heap, total, sems):
         self.part, self.heap, self.total = part, heap, total
         self.csend, self.crecv, self.ssem, self.rsem, self.fsend, self.frecv = sems
         self.s, self.t, self.j, self.base = whereabouts()
 
-    def across(self, r, mine):
-        jj = flip(self.j, r)
-        src = self.part.at[jj, 1 - self.t]
+    def across(self, r):
+        src = self.part.at[flip(self.j, r), 1 - self.t]
         return remote(src, self.heap.at[r], self.csend.at[r], self.crecv.at[r], (self.s, 1 - self.t))
 
     def hop(self, p, i, r):
@@ -198,45 +199,56 @@
             (self.base + flip(self.j, 1 << d), self.t),
         )
 
-    def start(self):
-        order = [7, 6, 5, 3, 4, 2, 1, 0]
-        for r in order:
-            self.across(r, True).start()
-        for r in order:
-            self.across(r, False).wait_recv()
-            jj = flip(self.j, r)
-            self.part[jj, self.t] = (self.part[jj, self.t].astype(F32) + self.heap[r].astype(F32)).astype(BF16)
+    def send(self, r):
+        self.across(r).start()
+
+    def take(self, r):
+        self.across(r).wait_recv()
+        jj = flip(self.j, r)
+        step = 32
+
+        def one(m, c):
+            at = pl.ds(pl.multiple_of(m * step, step), step)
+            self.part[jj, self.t, at] = (
+                self.part[jj, self.t, at].astype(F32) + self.heap[r, at].astype(F32)
+            ).astype(BF16)
+            return c
+
+        lax.fori_loop(0, self.part.shape[2] // step, one, 0)
+        for i in range(3):
+            if r >> ORDERS[i][0] & 1:
+                self.hop(0, i, r).start()
 
     def phase(self, p):
         for i in range(3):
             d = ORDERS[i][p]
-            for r in subsets(ORDERS[i][p + 1 :]):
-                self.hop(p, i, r | (1 << d)).start()
-        for i in range(3):
-            d = ORDERS[i][p]
             off, rows = PIECES[i]
-            for r in subsets(ORDERS[i][p + 1 :]):
+            for r in reversed(subsets(ORDERS[i][p + 1 :])):
                 self.hop(p, i, r | (1 << d)).wait_recv()
                 jj = flip(self.j, r)
                 k = slot_of(p, i, r)
-                mine = self.part[jj, self.t, pl.ds(off, rows)].astype(F32)
-                new = mine + self.heap[CUBE + k, pl.ds(off, rows)].astype(F32)
-                if p == 2:
-                    self.total[self.t, pl.ds(off, rows)] = new
-                else:
-                    self.part[jj, self.t, pl.ds(off, rows)] = new.astype(BF16)
-
-    def last(self):
-        mine = self.total.at[self.t]
-        cp = remote(mine, mine, self.fsend, self.frecv, (self.s, 1 - self.t))
-        cp.start()
-        theirs = self.total.at[1 - self.t]
-        remote(theirs, theirs, self.fsend, self.frecv, (self.s, 1 - self.t)).wait_recv()
-        cp.wait_send()
+                for q in range(0, rows, 16):
+                    at = pl.ds(off + q, 16)
+                    new = self.part[jj, self.t, at].astype(F32) + self.heap[CUBE + k, at].astype(F32)
+                    if p == 2:
+                        self.total[self.t, at] = new
+                    else:
+                        self.part[jj, self.t, at] = new.astype(BF16)
+                if p < 2 and r >> ORDERS[i][p + 1] & 1:
+                    self.hop(p + 1, i, r).start()
+
+    def both(self, half):
+        ref = self.total.at[half]
+        return remote(ref, ref, self.fsend, self.frecv, (self.s, 1 - self.t))
+
+    def trade(self):
+        self.both(self.t).start()
 
     def finish(self):
+        self.both(1 - self.t).wait_recv()
+        self.both(self.t).wait_send()
         for r in range(CUBE):
-            self.across(r, True).wait_send()
+            self.across(r).wait_send()
         for p in range(3):
             for i in range(3):
                 d = ORDERS[i][p]
@@ -244,10 +256,13 @@
                     self.hop(p, i, r | (1 << d)).wait_send()
 
     def run(self):
-        self.start()
+        for r in self.ORDER:
+            self.send(r)
+        for r in self.ORDER:
+            self.take(r)
         for p in range(3):
             self.phase(p)
-        self.last()
+        self.trade()
         self.finish()
 
 
@@ -633,21 +648,80 @@
     )(lengths, x_all, w_a, *spreaders())
 
 
-def attend_back_kernel(
-    groups, lengths, q_ref, k_ref, v_ref, y_ref, den_ref, state_ref, dy_ref, first, second, third,
-    dq_ref, dk_ref, dv_ref,
-    c_ref, da, db, dv, state_mine, state_theirs, ssem, rsem,
+def row_loop(count, step, work):
+    def one(m, c):
+        work(pl.ds(pl.multiple_of(m * step, step), step))
+        return c
+
+    lax.fori_loop(0, count // step, one, 0)
+
+
+def tail_kernel(
+    n, lengths, q_ref, k_ref, v_ref, y_ref, den_ref, state_ref, w_ref, mid_ref, cot_ref, tok_ref,
+    dlow_hbm, out_hbm, low_hbm, grads_b, first, second, third,
+    output_ref, grad_ref, tiles_b, tiles_a,
+    part, heap_a, heap_b, wide, own, total, d_mid, c_ref, dy_ref, da, db, dv, dqkv, grads_a,
+    state_mine, state_theirs, xsend, xrecv, lsem, *sems,
 ):
+    groups = n // CUBE
     s, t, j, base = whereabouts()
-    total = q_ref.shape[0]
-    blocks = total // BLOCK
+    tokens = q_ref.shape[0]
+    rows = tokens // CUBE
+    half = rows // 2
+    width = w_ref.shape[1]
     two, three = lengths[0], lengths[0] + lengths[1]
-    start = base * (total // CUBE)
-    greet(other_groups(groups))
+    start = base * rows
+    in_kernel = len(tiles_a.shape) == 3
+    sum_low, sum_out, sum_one = sems[0:6], sems[6:12], sems[12:18]
+    gsems, bsems, asems = sems[18:23], sems[23:26], sems[26:29]
+
+    load = pltpu.make_async_copy(dlow_hbm, part, lsem.at[0])
+    load.start()
+    greet_all(n)
+    load.wait()
+    low_sum = Sum(part, heap_a, total, sum_low)
+    low_sum.run()
+    back_b = Back(n, grads_b, tiles_b, bsems) if in_kernel else None
+    if in_kernel:
+        back_b.start()
+    load_out = pltpu.make_async_copy(out_hbm, part, lsem.at[1])
+    load_out.start()
+
+    gain_two = w_ref[161:162, :].astype(F32)
+    for h in range(2):
+
+        def norm_back_two(at):
+            mid = mid_ref[h, at]
+            root = lax.rsqrt(jnp.mean(mid * mid, axis=-1, keepdims=True) + EPS)
+            normed = mid * root
+            scaled = total[h, at] * gain_two
+            grad = cot_ref[h, at].astype(F32) + root * (
+                scaled - normed * jnp.mean(scaled * normed, axis=-1, keepdims=True)
+            )
+            d_mid[h, at] = grad
+            own[h, at] = grad.astype(BF16)
+
+        row_loop(half, 16, norm_back_two)
+
+    Gather(own, wide, gsems).run()
+
+    def project(jj, c):
+        for h in range(2):
+            at = pl.ds(pl.multiple_of(jj * rows + h * half, half), half)
+            dy_ref[at, :] = dot_nt(wide[jj, h], w_ref[176:304, :]).astype(BF16)
+        return c
+
+    lax.fori_loop(0, CUBE, project, 0)
+    load_out.wait()
+    out_sum = Sum(part, heap_b, total, sum_out)
+    for r in Sum.ORDER:
+        out_sum.send(r)
+
     state_mine[...] = jnp.zeros_like(state_mine)
     db[...] = jnp.zeros_like(db)
     dv[...] = jnp.zeros_like(dv)
     state = state_ref[...].astype(BF16)
+    blocks = tokens // BLOCK
 
     def early(tb, carry):
         tq = pl.ds(pl.multiple_of(tb * BLOCK, BLOCK), BLOCK)
@@ -670,7 +744,19 @@
         return carry
 
     lax.fori_loop(0, blocks, early, 0)
-    done = exchange(groups, state_mine, state_theirs, ssem, rsem, False)
+    done = exchange(groups, state_mine, state_theirs, xsend, xrecv, False)
+    for r in Sum.ORDER:
+        out_sum.take(r)
+
+    for col in range(0, width, 512):
+        acc = jnp.zeros((128, 512), F32)
+        for jj in range(CUBE):
+            for h in range(2):
+                at = pl.ds(jj * rows + h * half, half)
+                acc = acc + dot_tn(y_ref[at, :].astype(BF16), wide[jj, h, :, pl.ds(col, 512)])
+        grads_a[160:288, col : col + 512] = acc.astype(BF16)
+    load_low = pltpu.make_async_copy(low_hbm, wide, lsem.at[2])
+    load_low.start()
 
     def outer(tb, carry):
         tq = pl.ds(pl.multiple_of(tb * BLOCK, BLOCK), BLOCK)
@@ -690,10 +776,14 @@
             return acc + dot(inner_grad, ks)
 
         acc = lax.fori_loop(0, tb + 1, inner, jnp.zeros((BLOCK, FEAT), F32))
-        dq_ref[tq, :] = ((da[tq, :] + acc * 0.5) * 0.5).astype(BF16)
+        da[tq, :] = (da[tq, :] + acc * 0.5) * 0.5
         return carry
 
-    lax.fori_loop(0, blocks, outer, 0)
+    cuts = [0, blocks // 2, 3 * blocks // 4, blocks]
+    for p in range(3):
+        lax.fori_loop(cuts[p], cuts[p + 1], outer, 0)
+        out_sum.phase(p)
+    out_sum.trade()
     state_back = done().astype(BF16)
 
     def late(sb, carry):
@@ -706,39 +796,133 @@
         d_quad = dot_nt(v, state_back[0:256]) * keep
         d_line = dot_nt(v, state_back[256:384]) * keep
         more = dot(quad, state_back[0:256]) + dot(line, state_back[256:384])
-        dk_ref[sq, :] = ((db[sq, :] + lift_back(u, d_quad, d_line, first[...], second[...])) * 0.5).astype(BF16)
-        dv_ref[sq, :] = (dv[sq, :] + more[:, :128]).astype(BF16)
+        dk = (db[sq, :] + lift_back(u, d_quad, d_line, first[...], second[...])) * 0.5
+        dqkv[sq, 0:128] = (dv[sq, :] + more[:, :128]).astype(BF16)
+        side = dot(da[sq, :].astype(BF16), third[...]) + dot(dk.astype(BF16), third_shifted(third[...]))
+        dqkv[sq, 128:256] = side.astype(BF16)
         return carry
 
     lax.fori_loop(0, blocks, late, 0)
-
-
-def attend_back_call(n, lengths, q, k, v, y, den, state, dy):
+    out_sum.finish()
+    for h in range(2):
+
+        def finish_output(at):
+            output_ref[h, at] = (mid_ref[h, at] + total[h, at]).astype(BF16)
+
+        row_loop(half, 16, finish_output)
+
+    load_low.wait()
+    one_sum = Sum(part, heap_a, total, sum_one)
+    w_one = w_ref[0:160, :]
+    for idx, r in enumerate(Sum.ORDER):
+        jj = flip(j, r)
+        for h in range(2):
+            at = pl.ds(pl.multiple_of(jj * rows + h * half, half), half)
+            part[jj, h] = dot(dqkv[at, 0:160], w_one).astype(BF16)
+        one_sum.send(r)
+        if idx:
+            one_sum.take(Sum.ORDER[idx - 1])
+    one_sum.take(Sum.ORDER[-1])
+    for col in range(0, width, 512):
+        acc = jnp.zeros((256, 512), F32)
+        for jj in range(CUBE):
+            for h in range(2):
+                at = pl.ds(jj * rows + h * half, half)
+                acc = acc + dot_tn(dqkv[at, :], wide[jj, h, :, pl.ds(col, 512)])
+        grads_a[0:160, col : col + 512] = acc[0:160].astype(BF16)
+    if in_kernel:
+        back_a = Back(n, grads_a, tiles_a, asems)
+        back_a.start()
+    else:
+        copy = pltpu.make_async_copy(grads_a, tiles_a, lsem.at[3])
+        copy.start()
+    for p in range(3):
+        one_sum.phase(p)
+    one_sum.trade()
+    one_sum.finish()
+
+    gain_one = w_ref[160:161, :].astype(F32)
+    for h in range(2):
+
+        def norm_back_one(at):
+            x = tok_ref[h, at].astype(F32)
+            root = lax.rsqrt(jnp.mean(x * x, axis=-1, keepdims=True) + EPS)
+            normed = x * root
+            scaled = total[h, at] * gain_one
+            grad_ref[h, at] = d_mid[h, at] + root * (
+                scaled - normed * jnp.mean(scaled * normed, axis=-1, keepdims=True)
+            )
+
+        row_loop(half, 16, norm_back_one)
+
+    if in_kernel:
+        back_b.finish()
+        back_a.finish()
+    else:
+        copy.wait()
+
+
+def third_shifted(third):
+    return jnp.concatenate([jnp.zeros_like(third[:, :FEAT]), third[:, : 128 - FEAT]], axis=1)
+
+
+def tail_call(n, lengths, q, k, v, y, den, state, w_a, mid, cot, tokens, d_low, out_part, low_one, grads_b):
     groups = n // CUBE
-    count = q.shape[0]
+    count, width = low_one.shape
+    rows = count // CUBE
+    half = rows // 2
+    wide_columns = width // n % 128 == 0
     vm = pl.BlockSpec(memory_space=pltpu.VMEM)
+    any_space = pl.BlockSpec(memory_space=pl.ANY)
     peers = max(groups - 1, 1)
-    return pl.pallas_call(
-        functools.partial(attend_back_kernel, groups),
-        out_shape=[
-            jax.ShapeDtypeStruct((count, FEAT), BF16),
-            jax.ShapeDtypeStruct((count, FEAT), BF16),
-            jax.ShapeDtypeStruct((count, 128), BF16),
-        ],
-        in_specs=[pl.BlockSpec(memory_space=pltpu.SMEM)] + [vm] * 10,
-        out_specs=[vm] * 3,
+    cut = lambda x: x.reshape(-1, 2, half, width) if x.shape[0] > rows else x.reshape(2, half, width)
+    out_shape = [
+        jax.ShapeDtypeStruct((2, half, width), BF16),
+        jax.ShapeDtypeStruct((2, half, width), F32),
+        jax.ShapeDtypeStruct((n, grads_b.shape[0], width // n) if wide_columns else (8, 128), BF16),
+        jax.ShapeDtypeStruct((n, 288, width // n) if wide_columns else (288, width), BF16),
+    ]
+    output, grad, tiles_b, tiles_a = pl.pallas_call(
+        functools.partial(tail_kernel, n),
+        out_shape=out_shape,
+        in_specs=[pl.BlockSpec(memory_space=pltpu.SMEM)] + [vm] * 10 + [any_space] * 4 + [vm] * 3,
+        out_specs=[vm, vm, any_space, any_space],
         scratch_shapes=[
+            pltpu.VMEM((CUBE, 2, half, width), BF16),
+            pltpu.VMEM((15, half, width), BF16),
+            pltpu.VMEM((15, half, width), BF16),
+            pltpu.VMEM((CUBE, 2, half, width), BF16),
+            pltpu.VMEM((2, half, width), BF16),
+            pltpu.VMEM((2, half, width), F32),
+            pltpu.VMEM((2, half, width), F32),
             pltpu.VMEM((count, 256), BF16),
+            pltpu.VMEM((count, 128), BF16),
             pltpu.VMEM((count, FEAT), F32),
             pltpu.VMEM((count, FEAT), F32),
             pltpu.VMEM((count, 128), F32),
+            pltpu.VMEM((count, 256), BF16),
+            pltpu.VMEM((288, width), BF16),
             pltpu.VMEM((384, 256), F32),
             pltpu.VMEM((peers, 384, 256), F32),
             pltpu.SemaphoreType.DMA((peers,)),
             pltpu.SemaphoreType.DMA((peers,)),
+            pltpu.SemaphoreType.DMA((4,)),
+            *sum_sems(),
+            *sum_sems(),
+            *sum_sems(),
+            *gather_sems(),
+            *spread_sems(n),
+            *spread_sems(n),
         ],
-        compiler_params=pltpu.CompilerParams(collective_id=2, has_side_effects=True, vmem_limit_bytes=50 * MIB),
-    )(lengths, q, k, v, y, den, state, dy, *spreaders())
+        compiler_params=pltpu.CompilerParams(collective_id=2, has_side_effects=True, vmem_limit_bytes=62 * MIB),
+    )(
+        lengths, q, k, v, y, den, state, w_a, cut(mid), cut(cot), cut(tokens), cut(d_low), cut(out_part),
+        cut(low_one), grads_b, *spreaders(),
+    )
+    if not wide_columns:
+        tiles_b = back_call(n, grads_b, 9)
+        tiles_a = back_call(n, tiles_a, 10)
+    return output.reshape(rows, width), grad.reshape(rows, width), tiles_b, tiles_a
 
 
 def units_first(w):
@@ -786,38 +970,17 @@
     d_gate = (d_hidden * up * sigma * (1.0 + gate * (1.0 - sigma))).astype(BF16)
     d_up = (d_hidden * silu).astype(BF16)
     d_low_part = (dot(d_gate, gate_w) + dot(d_up, up_w)).astype(BF16)
-    d_low_two = cube_sum(d_low_part, 5)
-    output = (mid + cube_sum(out_part, 6)).astype(BF16)
     grads_b = jnp.concatenate(
         [dot_tn(d_gate, low_two), dot_tn(d_up, low_two), dot_tn(hidden, cot_all)], axis=0
     ).astype(BF16)
-
-    scaled = d_low_two * gain_two
-    d_mid = cotangent.astype(F32) + root_two * (
-        scaled - normed_two * jnp.mean(scaled * normed_two, axis=-1, keepdims=True)
+    output, grad_tokens, tiles_b, tiles_a = tail_call(
+        n, seq_lengths, q, k, v, y, den, state, w_a, mid, cotangent, tokens, d_low_part, out_part, low_one, grads_b
     )
-    d_attn = gather(d_mid.astype(BF16), 7)
-    dy = dot_nt(d_attn, out_w).astype(BF16)
-    dq, dk, dv = attend_back_call(n, seq_lengths, q, k, v, y, den, state, dy)
-    d_low_one = cube_sum(
-        (dot(dv, w_a[0:128]) + dot(dq, w_a[128:144]) + dot(dk, w_a[144:160])).astype(BF16), 8
-    )
-    grads_a = jnp.concatenate(
-        [dot_tn(dv, low_one), dot_tn(dq, low_one), dot_tn(dk, low_one), dot_tn(attn_low, d_attn)], axis=0
-    ).astype(BF16)
-    root_one = lax.rsqrt(jnp.mean(inputs * inputs, axis=-1, keepdims=True) + EPS)
-    normed_one = inputs * root_one
-    scaled = d_low_one * w_a[160:161].astype(F32)
-    grad_tokens = d_mid + root_one * (
-        scaled - normed_one * jnp.mean(scaled * normed_one, axis=-1, keepdims=True)
-    )
-
-    def arrived(grads, number):
-        tiles = back_call(n, grads, number)
+
+    def arrived(tiles):
         return tiles.reshape(-1, CUBE, *tiles.shape[1:]).astype(F32).sum(axis=0)
 
-    back_b = arrived(grads_b, 9)
-    back_a = arrived(grads_a, 10)
+    back_b, back_a = arrived(tiles_b), arrived(tiles_a)
 
     def units(part):
         return part.reshape(CUBE * UNITS, -1)[: w_gate.shape[1]]

time: 864 us -> 714 us (0.83)
  Pallas kernels: 695 us -> 609 us
  matrix products: 110 us -> 58.2 us
  other arithmetic: 25.7 us -> 14.1 us
    pallas_call x4 -> x1, Pallas kernels: 210 us -> 45.8 us  [cube_sum(): pl.pallas_call(sum_kernel, out_shape=jax.ShapeDtypeStruct((2, half, width...]
    pallas_call x3 -> x1, Pallas kernels: 176 us -> 296 us  [tail_call(): pl.pallas_call(functools.partial(tail_kernel, n), out_shape=out_shape, in...]
    pallas_call x2 -> x1, Pallas kernels: 81.6 us -> 40.7 us  [gather(): pl.pallas_call(gather_kernel, out_shape=jax.ShapeDtypeStruct((CUBE, 2, ro...]
    dot_general x7 -> x4, matrix products: 66.1 us -> 32.2 us  [dot(): return jnp.dot(a, b, preferred_element_type=F32)]
    dot_general x7 -> x3, matrix products: 18.6 us -> 9.44 us  [dot_tn(): lax.dot_general(a, b, (((0,), (0,)), ((), ())), preferred_element_type=F32)]
    dot_general x4 -> x3, matrix products: 25.7 us -> 16.5 us  [dot_nt(): lax.dot_general(a, b, (((1,), (1,)), ((), ())), preferred_element_type=F32)]
where the time goes in v2:
time: 714 us; the launch traced here: 701 us
  Pallas kernels  609 us (85%)
  matrix products  58.2 us (8%)
  local copies, waits for them, and re-layouts  15.5 us (2%)
  other arithmetic  14.1 us (2%)
    pallas_call x1, Pallas kernels, tail_call(): pl.pallas_call(functools.partial(tail_kernel, n), out_shape=out_shape, in...  296 us
    pallas_call x1, Pallas kernels, head_call(): pl.pallas_call(functools.partial(head_kernel, n), out_shape=[jax.ShapeDty...  183 us
    pallas_call x1, Pallas kernels, cube_sum(): pl.pallas_call(sum_kernel, out_shape=jax.ShapeDtypeStruct((2, half, width...  45.8 us
    pallas_call x1, Pallas kernels, attend_call(): pl.pallas_call(functools.partial(attend_kernel, groups), grid=(CUBE,), ou...  43.5 us
    pallas_call x1, Pallas kernels, gather(): pl.pallas_call(gather_kernel, out_shape=jax.ShapeDtypeStruct((CUBE, 2, ro...  40.7 us
    dot_general x4, matrix products, dot(): return jnp.dot(a, b, preferred_element_type=F32)  32.2 us
    dot_general x3, matrix products, dot_nt(): lax.dot_general(a, b, (((1,), (1,)), ((), ())), preferred_element_type=F32)  16.5 us

profile of v2, /device:TPU:9, one launch (start us, length us, event | category | flops | bytes accessed | tf_op | source)
XLA Modules:
  0.0 701.4 jit_solution(15890095509847251048)
XLA Ops:
  0.7 1.2 pad.10
  1.9 1.2 pad.11
  3.0 0.0 copy-start.16
  3.1 0.1 pad.12
  3.1 0.0 copy-start.21
  3.1 0.0 copy-start.22
  3.2 0.0 copy-start.20
  3.2 1.5 pad_maximum_fusion.1.pack_b
  4.7 0.2 copy.35
  4.9 0.0 copy-start.5
  4.9 0.0 copy-start.6
  4.9 0.0 copy-start.7
  4.9 0.0 copy-start.8
  4.9 0.1 copy.36
  5.1 0.1 copy.37
  5.2 0.1 pad.23.clone
  5.3 0.1 maximum_maximum_fusion
  5.4 0.0 copy-start.15
  5.5 0.8 copy-done.15
  6.3 182.9 %shard_map.257 = (bf16[304,2048]{1,0:T(8,128)(2,1)}, bf16[1056,2048]{1,0:T(8,128)(2,1)}, bf16[8,2,128,2048]{3,2,1,0:T(8,128)(2,1)}, bf16[8,2,128,2048]{3,2,1,0:T(8,128)(2,1)}) custom-call(bf16[8,304,128]{2,1,0:T(8,128)(2,1)} %copy-done.15, bf16[8,1056,128]{2,1,0:T(8,128)(2,1)} %pad_maximum_fusion.1.pack_b, bf16[2,128,2048]{2,1,0:T(8,128)(2,1)} %bitcast.79, ...), custom_call_target="tpu_custom_call" | custom-call | tf_op jit(solution)/shard_map/pallas_call | solution.py:414
  189.3 43.5 %shard_map.258 = (bf16[2048,2048]{1,0:T(8,128)(2,1)}, bf16[2048,16]{1,0:T(8,128)(2,1)S(1)}, bf16[2048,16]{1,0:T(8,128)(2,1)S(1)}, bf16[2048,256]{1,0:T(8,128)(2,...) custom-call(s32[3]{0:T(128)S(1)} %copy-done.8, bf16[2048,2048]{1,0:T(8,128)(2,1)} %bitcast.89, ...), custom_call_target="tpu_custom_call" | custom-call | tf_op jit(solution)/shard_map/pallas_call | solution.py:612
  232.8 0.0 copy-start
  232.8 0.0 copy-start.3
  232.8 0.0 copy-start.4
  232.8 7.0 convolution_convert_fusion.1
  239.8 0.0 copy-start.10
  239.9 45.8 %shard_map.259 = f32[2,128,2048]{2,1,0:T(8,128)S(1)} custom-call(bf16[8,2,128,2048]{3,2,1,0:T(8,128)(2,1)} %bitcast.77), custom_call_target="tpu_custom_call" | custom-call | tf_op jit(solution)/shard_map/pallas_call | solution.py:291
  285.7 0.4 multiply_reduce_fusion
  286.1 0.8 slice_convert_fusion
  286.9 1.2 multiply_convert_fusion.3
  288.1 40.7 %shard_map.260 = bf16[8,2,128,2048]{3,2,1,0:T(8,128)(2,1)} custom-call(bf16[2,128,2048]{2,1,0:T(8,128)(2,1)} %bitcast.96), custom_call_target="tpu_custom_call" | custom-call | tf_op jit(solution)/shard_map/pallas_call | solution.py:159
  328.9 6.2 fusion.3
  335.1 6.2 fusion.9
  341.4 4.2 multiply_convert_fusion
  345.5 3.1 convolution_convert_fusion.4
  348.7 3.2 convolution_convert_fusion.3
  351.9 3.1 convolution_convert_fusion.2
  355.0 2.4 pad_maximum_fusion.grads_b
  357.4 6.9 convolution_convert_fusion
  364.4 8.1 %fusion.1 = f32[2048,2048]{1,0:T(8,128)} fusion(bf16[2048,352]{0,1:T(8,128)(2,1)S(1)} %get-tuple-element.59, bf16[1056,2048]{1,0:T(8,128)(2,1)S(1)} %bitcast.106), kind=kOutput, calls=%fused_computation.22 | convolution fusion | flops 2952790016 | bytes 19660800 | tf_op jit(solution)/shard_map/dot_general | solution.py:451
  372.5 10.2 %add_convert_fusion = bf16[2048,2048]{1,0:T(8,128)(2,1)} fusion(f32[2048,2048]{1,0:T(8,128)} %fusion.1, bf16[2048,352]{0,1:T(8,128)(2,1)S(1)} %get-tuple-element.60, bf16[1056,2048]{1,0:T(8,128)(2,1)S(1)} %bitcast.106), kind=kOutput, calls=%fused_computation | convolution fusion | flops 2961178624 | bytes 28049408 | tf_op jit(solution)/shard_map/dot_general | solution.py:451
  382.7 296.3 %shard_map.261 = (bf16[2,128,2048]{2,1,0:T(8,128)(2,1)}, f32[2,128,2048]{2,1,0:T(8,128)}, bf16[16,1056,128]{2,1,0:T(8,128)(2,1)}, bf16[16,288,128]{2,1,0:T(8,128)(2,1)}) custom-call(s32[3]{0:T(128)} %lengths.3, bf16[2048,16]{1,0:T(8,128)(2,1)} %copy-done.2, bf16[2048,16]{1,0:T(8,128)(2,1)} %copy-done.3, bf16[2048,256]{1,0:T(8,128)(2,1)} %copy-done.1, ...), custom_call_target="tpu_custom_call" | custom-call | tf_op jit(solution)/shard_map/pallas_call | solution.py:885
  679.0 1.6 convert_reduce_fusion.1
  680.6 0.1 copy.39
  680.7 0.1 copy.40
  680.9 0.3 copy-done.18
  681.2 0.0 copy-done.19
  681.2 0.9 fusion.14
  682.1 0.2 copy.38
  682.3 0.0 copy-start.14
  682.3 0.1 multiply_reduce_fusion.3
  682.4 0.6 copy-done.14
  683.1 3.6 convert_reduce_fusion
  686.7 0.3 fusion.13
  687.0 0.8 copy-done.11
  687.8 0.2 copy-done.12
  688.0 1.9 multiply_reduce_fusion.1
  689.9 2.6 psum.7
  692.5 0.5 bitcast_divide_fusion
  693.0 1.2 slice.77
  694.2 1.6 copy.41
  695.8 1.6 copy.42
  697.4 2.3 copy.49
  699.7 1.3 copy.50
  (57 shorter events, 0.3 us)
Async XLA Ops:
  0.6 2.4 copy-start.17
  3.0 1.6 copy-start.16
  3.1 1.8 copy-start.21
  3.1 1.9 copy-start.22
  3.1 2.2 copy-start.23
  3.2 2.1 copy-start.24
  3.2 2.2 copy-start.20
  4.9 184.4 %copy-start.5 = (bf16[16,256]{1,0:T(8,128)(2,1)S(1)}, bf16[16,256]{1,0:T(8,128)(2,1)}, u32[]{:S(2)}) copy-start(bf16[16,256]{1,0:T(8,128)(2,1)} %constant.19.clone.first) | copy-start | bytes 24580
  4.9 184.4 %copy-start.6 = (bf16[16,256]{1,0:T(8,128)(2,1)S(1)}, bf16[16,256]{1,0:T(8,128)(2,1)}, u32[]{:S(2)}) copy-start(bf16[16,256]{1,0:T(8,128)(2,1)} %constant.20.clone.second) | copy-start | bytes 24580
  4.9 184.3 %copy-start.7 = (bf16[16,128]{1,0:T(8,128)(2,1)S(1)}, bf16[16,128]{1,0:T(8,128)(2,1)}, u32[]{:S(2)}) copy-start(bf16[16,128]{1,0:T(8,128)(2,1)} %constant.21.clone.third) | copy-start | bytes 12292
  4.9 184.3 %copy-start.8 = (s32[3]{0:T(128)S(1)}, s32[3]{0:T(128)}, u32[]{:S(2)}) copy-start(s32[3]{0:T(128)} %lengths.3) | copy-start | bytes 40
  5.4 0.8 copy-start.15
  232.8 7.0 %copy-start = (f32[2048,128]{1,0:T(8,128)}, f32[2048,128]{1,0:T(8,128)S(1)}, u32[]{:S(2)}) copy-start(f32[2048,128]{1,0:T(8,128)S(1)} %get-tuple-element.31.y_ref) | copy-start | bytes 3145732
  232.8 7.0 %copy-start.1 = (bf16[2048,256]{1,0:T(8,128)(2,1)}, bf16[2048,256]{1,0:T(8,128)(2,1)S(1)}, u32[]{:S(2)}) copy-start(bf16[2048,256]{1,0:T(8,128)(2,1)S(1)} %get-tuple-element.30.v_ref) | copy-start | bytes 3145732
  232.8 7.0 %copy-start.2 = (bf16[2048,16]{1,0:T(8,128)(2,1)}, bf16[2048,16]{1,0:T(8,128)(2,1)S(1)}, u32[]{:S(2)}) copy-start(bf16[2048,16]{1,0:T(8,128)(2,1)S(1)} %get-tuple-element.28.q_ref) | copy-start | bytes 196612
  232.8 7.0 %copy-start.3 = (bf16[2048,16]{1,0:T(8,128)(2,1)}, bf16[2048,16]{1,0:T(8,128)(2,1)S(1)}, u32[]{:S(2)}) copy-start(bf16[2048,16]{1,0:T(8,128)(2,1)S(1)} %get-tuple-element.29.k_ref) | copy-start | bytes 196612
  232.8 7.0 %copy-start.4 = (f32[384,256]{1,0:T(8,128)}, f32[384,256]{1,0:T(8,128)S(1)}, u32[]{:S(2)}) copy-start(f32[384,256]{1,0:T(8,128)S(1)} %get-tuple-element.33.state_ref) | copy-start | bytes 1179652
  239.8 45.9 %copy-start.10 = (bf16[256,2048]{1,0:T(8,128)(2,1)S(1)}, bf16[256,2048]{1,0:T(8,128)(2,1)}, u32[]{:S(2)}) copy-start(bf16[256,2048]{1,0:T(8,128)(2,1)} %param.18) | copy-start | bytes 3145732
  286.1 42.8 %copy-start.9 = (f32[256,2048]{1,0:T(8,128)}, f32[256,2048]{1,0:T(8,128)S(1)}, u32[]{:S(2)}) copy-start(f32[256,2048]{1,0:T(8,128)S(1)} %get-tuple-element.57) | copy-start | bytes 6291460
  288.1 47.0 %slice-start.2 = ((s8[4325376]{0:T(1024)(128)(4,1)}), s8[131072]{0:T(1024)(128)(4,1)S(1)}, s32[]{:S(2)}) async-start(s8[4325376]{0:T(1024)(128)(4,1)} %bitcast.105), calls=%async_computation.2 | async-start | bytes 262144
  328.9 6.2 slice-start.3
  328.9 12.5 %slice-start = ((s8[8388608]{0:T(1024)(128)(4,1)}), s8[4194304]{0:T(1024)(128)(4,1)S(1)}, s32[]{:S(2)}) async-start(s8[8388608]{0:T(1024)(128)(4,1)} %bitcast.84), calls=%async_computation | async-start | bytes 8388608
  335.1 6.3 slice-start.1
  345.5 6.3 slice-start.4
  348.7 3.2 slice-start.5
  680.6 0.6 copy-start.18
  680.6 0.6 copy-start.19
  682.3 0.8 copy-start.14
  686.7 1.1 copy-start.11
  686.7 1.3 copy-start.12
  689.9 9.8 %copy-start.13 = (f32[2,128,2048]{2,1,0:T(8,128)S(1)}, f32[2,128,2048]{2,1,0:T(8,128)}, u32[]{:S(2)}) copy-start(f32[2,128,2048]{2,1,0:T(8,128)} %get-tuple-element.38) | copy-start | bytes 6291460

commit v3 on v2

v3 whole, which is shorter than its diff:
```python
import functools

import jax
import jax.numpy as jnp
import numpy as np
from jax import lax
from jax.experimental import pallas as pl
from jax.experimental.pallas import tpu as pltpu
from jax.sharding import PartitionSpec as P

MESH = pl.DeviceIdType.MESH
HEADS = 16
FEAT = 16
CUBE = 8
UNITS = 352
EPS = 1e-06
F32 = jnp.float32
BF16 = jnp.bfloat16
ORDERS = ((0, 1, 2), (1, 2, 0), (2, 0, 1))
PIECES = ((0, 48), (48, 48), (96, 32))
UP_FIRST = ((2, 0, 1), (2, 1, 0))
UP_LAST = ((0, 1, 2), (1, 0, 2))
HALVES = ((0, 64), (64, 64))
MIB = 1 << 20


def flip(place, mask):
    total = 0
    for b in range(3):
        bit = (place // (1 << b)) % 2
        total = total + ((1 - bit) if (mask >> b) & 1 else bit) * (1 << b)
    return total


def subsets(dims):
    out = [0]
    for d in dims:
        out = out + [r | (1 << d) for r in out]
    return out


def whereabouts():
    s = lax.axis_index("seq")
    t = lax.axis_index("tensor")
    j = s % CUBE
    return s, t, j, s - j


def remote(src, dst, send, recv, device):
    return pltpu.make_async_remote_copy(
        src_ref=src, dst_ref=dst, send_sem=send, recv_sem=recv, device_id=device, device_id_type=MESH
    )


def greet(devices):
    barrier = pltpu.get_barrier_semaphore()
    for device in devices:
        pl.semaphore_signal(barrier, inc=1, device_id=device, device_id_type=MESH)
    pl.semaphore_wait(barrier, len(devices))


def near():
    s, t, j, base = whereabouts()
    return [(base + flip(j, 1 << d), t) for d in range(3)] + [(s, 1 - t)]


def greet_all(n):
    s, t, _, _ = whereabouts()
    barrier = pltpu.get_barrier_semaphore()

    def one(k, carry):
        pl.semaphore_signal(barrier, inc=1, device_id=((s + k) % n, t), device_id_type=MESH)
        return carry

    lax.fori_loop(1, n, one, 0)
    pl.semaphore_signal(barrier, inc=1, device_id=(s, 1 - t), device_id_type=MESH)
    pl.semaphore_wait(barrier, n)


class Gather:
    def __init__(self, own, full, sems, orders=ORDERS, pieces=PIECES):
        self.own, self.full, self.orders, self.pieces = own, full, orders, pieces
        self.ssem, self.rsem, self.csend, self.crecv, self.lsem = sems
        self.s, self.t, self.j, self.base = whereabouts()

    def view(self, r, i):
        off, rows = self.pieces[i]
        return self.full.at[flip(self.j, r), self.t, pl.ds(off, rows)]

    def other(self, r, i):
        off, rows = self.pieces[i]
        return self.full.at[flip(self.j, r), 1 - self.t, pl.ds(off, rows)]

    def hop(self, p, i, r):
        d = self.orders[i][p]
        off, rows = self.pieces[i]
        src = self.own.at[self.t, pl.ds(off, rows)] if r == 0 else self.view(r, i)
        k = r | (1 << d)
        return remote(src, self.view(r, i), self.ssem.at[i, k], self.rsem.at[i, k], (self.base + flip(self.j, 1 << d), self.t))

    def arrival(self, p, i, r):
        d = self.orders[i][p]
        k = r | (1 << d)
        return remote(self.view(k, i), self.view(k, i), self.ssem.at[i, k], self.rsem.at[i, k], (self.base + flip(self.j, 1 << d), self.t))

    def across(self, r, i, mine):
        ref = self.view(r, i) if mine else self.other(r, i)
        return remote(ref, ref, self.csend.at[i, r], self.crecv.at[i, r], (self.s, 1 - self.t))

    def local(self):
        return pltpu.make_async_copy(self.own, self.full.at[self.j], self.lsem)

    def start(self, p):
        if p == 0:
            self.local().start()
        for i in range(len(self.pieces)):
            for r in subsets(self.orders[i][:p]):
                self.hop(p, i, r).start()

    def arrive(self, p):
        for i in range(len(self.pieces)):
            for r in subsets(self.orders[i][:p]):
                self.arrival(p, i, r).wait_recv()

    def share(self, p):
        for i in range(len(self.pieces)):
            for r in subsets(self.orders[i][:p]):
                self.across(r | (1 << self.orders[i][p]), i, True).start()

    def finish(self):
        for i in range(len(self.pieces)):
            for r in range(1, CUBE):
                self.across(r, i, False).wait_recv()
        for i in range(len(self.pieces)):
            for r in range(1, CUBE):
                self.across(r, i, True).wait_send()
        for p in range(3):
            for i in range(len(self.pieces)):
                for r in subsets(self.orders[i][:p]):
                    self.hop(p, i, r).wait_send()
        self.local().wait()

    def advance(self, p, tick=lambda: None):
        for i in range(len(self.pieces)):
            for r in subsets(self.orders[i][:p]):
                k = r | (1 << self.orders[i][p])
                self.arrival(p, i, r).wait_recv()
                if p < 2:
                    self.hop(p + 1, i, r).start()
                    self.hop(p + 1, i, k).start()
                self.across(k, i, True).start()
                tick()

    def run(self, tick=lambda: None):
        self.start(0)
        for p in range(3):
            self.advance(p, tick)
        self.finish()


def gather_sems():
    return [pltpu.SemaphoreType.DMA((3, CUBE))] * 4 + [pltpu.SemaphoreType.DMA]


SLOT = {0: 0, 1: 4, 2: 6}


def slot_of(order, p, r):
    return SLOT[p] + subsets(order[p + 1 :]).index(r)


class Sum:
    ORDER = (7, 6, 5, 3, 4, 2, 1, 0)

    def __init__(self, part, heap, total, sems, orders=ORDERS, pieces=PIECES):
        self.part, self.heap, self.total = part, heap, total
        self.orders, self.pieces = orders, pieces
        self.csend, self.crecv, self.ssem, self.rsem, self.fsend, self.frecv = sems
        self.s, self.t, self.j, self.base = whereabouts()

    def across(self, r):
        src = self.part.at[flip(self.j, r), 1 - self.t]
        return remote(src, self.heap.at[r], self.csend.at[r], self.crecv.at[r], (self.s, 1 - self.t))

    def hop(self, p, i, r):
        d = self.orders[i][p]
        off, rows = self.pieces[i]
        k = slot_of(self.orders[i], p, r ^ (1 << d))
        return remote(
            self.part.at[flip(self.j, r), self.t, pl.ds(off, rows)],
            self.heap.at[CUBE + k, pl.ds(off, rows)],
            self.ssem.at[i, k],
            self.rsem.at[i, k],
            (self.base + flip(self.j, 1 << d), self.t),
        )

    def send(self, r):
        self.across(r).start()

    def take(self, r):
        self.across(r).wait_recv()
        jj = flip(self.j, r)
        step = 32

        def one(m, c):
            at = pl.ds(pl.multiple_of(m * step, step), step)
            self.part[jj, self.t, at] = (
                self.part[jj, self.t, at].astype(F32) + self.heap[r, at].astype(F32)
            ).astype(BF16)
            return c

        lax.fori_loop(0, self.part.shape[2] // step, one, 0)
        for i in range(len(self.pieces)):
            if r >> self.orders[i][0] & 1:
                self.hop(0, i, r).start()

    def phase(self, p, tick=lambda: None):
        for i in range(len(self.pieces)):
            d = self.orders[i][p]
            off, rows = self.pieces[i]
            for r in reversed(subsets(self.orders[i][p + 1 :])):
                self.hop(p, i, r | (1 << d)).wait_recv()
                jj = flip(self.j, r)
                k = slot_of(self.orders[i], p, r)
                for q in range(0, rows, 16):
                    at = pl.ds(off + q, 16)
                    new = self.part[jj, self.t, at].astype(F32) + self.heap[CUBE + k, at].astype(F32)
                    if p == 2:
                        self.total[self.t, at] = new
                    else:
                        self.part[jj, self.t, at] = new.astype(BF16)
                if p < 2 and r >> self.orders[i][p + 1] & 1:
                    self.hop(p + 1, i, r).start()
                tick()

    def both(self, half):
        ref = self.total.at[half]
        return remote(ref, ref, self.fsend, self.frecv, (self.s, 1 - self.t))

    def trade(self):
        self.both(self.t).start()

    def finish(self):
        self.both(1 - self.t).wait_recv()
        self.both(self.t).wait_send()
        for r in range(CUBE):
            self.across(r).wait_send()
        for p in range(3):
            for i in range(len(self.pieces)):
                d = self.orders[i][p]
                for r in subsets(self.orders[i][p + 1 :]):
                    self.hop(p, i, r | (1 << d)).wait_send()

    def run(self):
        for r in self.ORDER:
            self.send(r)
        for r in self.ORDER:
            self.take(r)
        for p in range(3):
            self.phase(p)
        self.trade()
        self.finish()


def sum_sems():
    return [
        pltpu.SemaphoreType.DMA((CUBE,)),
        pltpu.SemaphoreType.DMA((CUBE,)),
        pltpu.SemaphoreType.DMA((3, CUBE)),
        pltpu.SemaphoreType.DMA((3, CUBE)),
        pltpu.SemaphoreType.DMA,
        pltpu.SemaphoreType.DMA,
    ]


def columns_of(ref, s):
    if len(ref.shape) == 3:
        return ref.at[s]
    return ref.at[:, pl.ds(pl.multiple_of(s * 128, 128), 128)]


def columns_apart(n, rows, width):
    return (rows, width) if width // n % 128 == 0 else (n, rows, width // n)


def together(x):
    return x if x.ndim == 2 else x.transpose(1, 0, 2).reshape(x.shape[1], -1)


def apart(n, x):
    return x if x.shape[1] // n % 128 == 0 else x.reshape(x.shape[0], n, -1).transpose(1, 0, 2)


class Trickle:
    def __init__(self, copies):
        self.copies = list(copies)

    def __call__(self, count=1):
        for _ in range(min(count, len(self.copies))):
            self.copies.pop(0).start()

    def flush(self):
        self(len(self.copies))


def far_and_near(n):
    near, far = list(range(1, n // 2)), list(range(n // 2, n))
    return [k for pair in zip(far, near + [None]) for k in pair if k is not None]


class Spread:
    def __init__(self, n, pack, full, sems):
        self.n, self.pack, self.full = n, pack, full
        self.ssem, self.rsem, self.lsem = sems
        self.s, self.t, self.j, self.base = whereabouts()

    def columns(self, s):
        return columns_of(self.full, s)

    def copy(self, k):
        to = (self.s + k) % self.n
        return remote(self.pack.at[to % CUBE], self.columns(self.s), self.ssem.at[k], self.rsem.at[k], (to, self.t))

    def arrival(self, k):
        at = (self.s + self.n - k) % self.n
        return remote(self.pack.at[0], self.columns(at), self.ssem.at[k], self.rsem.at[k], (at, self.t))

    def local(self):
        return pltpu.make_async_copy(self.pack.at[self.j], self.columns(self.s), self.lsem)

    def start(self):
        lax.fori_loop(1, self.n, lambda k, c: (self.copy(k).start(), c)[1], 0)
        self.local().start()

    def trickle(self):
        return [self.local()] + [self.copy(k) for k in far_and_near(self.n)]

    def finish(self):
        self.local().wait()
        lax.fori_loop(1, self.n, lambda k, c: (self.arrival(k).wait_recv(), c)[1], 0)
        lax.fori_loop(1, self.n, lambda k, c: (self.copy(k).wait_send(), c)[1], 0)


class Back:
    def __init__(self, n, grads, tiles, sems):
        self.n, self.grads, self.tiles = n, grads, tiles
        self.ssem, self.rsem, self.lsem = sems
        self.s, self.t, self.j, self.base = whereabouts()

    def columns(self, s):
        return columns_of(self.grads, s)

    def copy(self, k):
        to = (self.s + k) % self.n
        return remote(self.columns(to), self.tiles.at[self.s], self.ssem.at[k], self.rsem.at[k], (to, self.t))

    def arrival(self, k):
        at = (self.s + self.n - k) % self.n
        return remote(self.tiles.at[at], self.tiles.at[at], self.ssem.at[k], self.rsem.at[k], (at, self.t))

    def local(self):
        return pltpu.make_async_copy(self.columns(self.s), self.tiles.at[self.s], self.lsem)

    start = Spread.start
    trickle = Spread.trickle
    finish = Spread.finish


def spread_sems(n):
    return [pltpu.SemaphoreType.DMA((n,)), pltpu.SemaphoreType.DMA((n,)), pltpu.SemaphoreType.DMA]


def spread_kernel(n, pack, full, *sems):
    greet_all(n)
    spread = Spread(n, pack, full, sems)
    spread.start()
    spread.finish()


def spread_call(n, pack, width, number):
    any_space = pl.BlockSpec(memory_space=pl.ANY)
    full = pl.pallas_call(
        functools.partial(spread_kernel, n),
        out_shape=jax.ShapeDtypeStruct(columns_apart(n, pack.shape[1], width), BF16),
        in_specs=[any_space],
        out_specs=any_space,
        scratch_shapes=spread_sems(n),
        compiler_params=pltpu.CompilerParams(collective_id=number, has_side_effects=True),
    )(pack)
    return together(full)


def back_kernel(n, grads, tiles, *sems):
    greet_all(n)
    back = Back(n, grads, tiles, sems)
    back.start()
    back.finish()


def back_call(n, grads, number):
    rows, width = grads.shape
    any_space = pl.BlockSpec(memory_space=pl.ANY)
    return pl.pallas_call(
        functools.partial(back_kernel, n),
        out_shape=jax.ShapeDtypeStruct((n, rows, width // n), BF16),
        in_specs=[any_space],
        out_specs=any_space,
        scratch_shapes=spread_sems(n),
        compiler_params=pltpu.CompilerParams(collective_id=number, has_side_effects=True),
    )(apart(n, grads))


def dot(a, b):
    return jnp.dot(a, b, preferred_element_type=F32)


def dot_nt(a, b):
    return lax.dot_general(a, b, (((1,), (1,)), ((), ())), preferred_element_type=F32)


def dot_tn(a, b):
    return lax.dot_general(a, b, (((0,), (0,)), ((), ())), preferred_element_type=F32)


def spreaders():
    first = np.repeat(np.eye(FEAT), FEAT, axis=1)
    second = np.tile(np.eye(FEAT), (1, FEAT))
    third = np.eye(FEAT, 128)
    return [jnp.asarray(m, BF16) for m in (first, second, third)]


ROOT_HALF = 0.5**0.5


def lift(u, keep, first, second, third):
    quad = dot(u, first) * dot(u, second) * (0.25 * ROOT_HALF) * keep
    lane = lax.broadcasted_iota(jnp.int32, (u.shape[0], 128), 1)
    line = (dot(u, third) * 0.5 + jnp.where(lane == FEAT, 1.0, 0.0)) * keep
    return quad.astype(BF16), line.astype(BF16)


def lift_back(u, d_quad, d_line, first, second):
    one, two = dot(u, first) * 0.5, dot(u, second) * 0.5
    back = dot_nt((d_quad * two).astype(BF16), first) + dot_nt((d_quad * one).astype(BF16), second)
    return back * ROOT_HALF + d_line[:, :FEAT]


def two_terms(x):
    high = x.astype(BF16)
    return high, (x - high.astype(F32)).astype(BF16)


def segments(start_two, start_three, first_position, count, axis):
    shape = (count, 1) if axis == 0 else (1, count)
    position = first_position + lax.broadcasted_iota(jnp.int32, shape, axis)
    return position, (position >= start_two).astype(jnp.int32) + (position >= start_three).astype(jnp.int32)


def pair_mask(two, three, at_t, at_s, block):
    pos_t, seg_t = segments(two, three, at_t, block, 0)
    pos_s, seg_s = segments(two, three, at_s, block, 1)
    return (pos_s <= pos_t) & (seg_s == seg_t)


def pair_mask_turned(two, three, at_s, at_t, block):
    pos_s, seg_s = segments(two, three, at_s, block, 0)
    pos_t, seg_t = segments(two, three, at_t, block, 1)
    return (pos_s <= pos_t) & (seg_s == seg_t)


def other_groups(groups):
    s, t, j, base = whereabouts()
    return [((s + CUBE * k) % (CUBE * groups), t) for k in range(1, groups)]


def exchange(groups, mine, theirs, ssem, rsem, before):
    s, t, j, base = whereabouts()
    c = s // CUBE
    for k, device in enumerate(other_groups(groups)):
        remote(mine, theirs.at[k], ssem.at[k], rsem.at[k], device).start()

    def finish():
        total = jnp.zeros(mine.shape, F32)
        for k, device in enumerate(other_groups(groups)):
            remote(mine, theirs.at[k], ssem.at[k], rsem.at[k], device).wait_recv()
            source = (c + groups - (k + 1)) % groups
            counts = (source < c) if before else (source > c)
            total = total + jnp.where(counts, theirs[k], 0.0)
        for k, device in enumerate(other_groups(groups)):
            remote(mine, theirs.at[k], ssem.at[k], rsem.at[k], device).wait_send()
        return total

    return finish


BLOCK = 256


def row_loop(count, step, work):
    def one(m, c):
        work(pl.ds(pl.multiple_of(m * step, step), step))
        return c

    lax.fori_loop(0, count // step, one, 0)


def pair_weight(score):
    return (score * 0.5 + 1.0) * score + 1.0


def head_kernel(
    n, lengths, tok_ref, pack_a, pack_b, cot_hbm, first, second, third,
    w_ref, w_b, cot_all, low_hbm, own, mid_ref, q_ref, k_ref, v_ref, y_ref, y_turned, den_ref, state_ref,
    wide, part, heap, total, kept, state_mine, state_theirs, xsend, xrecv, lsem, *sems,
):
    groups = n // CUBE
    s, t, j, base = whereabouts()
    half, width = tok_ref.shape[1:]
    rows = 2 * half
    tokens = CUBE * rows
    two, three = lengths[0], lengths[0] + lengths[1]
    start = base * rows
    in_kernel = len(pack_a.shape) == 3
    sum_sem, tok_sem, cot_sem, a_sem, b_sem = sems[0:6], sems[6:11], sems[11:16], sems[16:19], sems[19:22]

    greet_all(n)
    g_tok = Gather(tok_ref, wide, tok_sem)
    g_cot = Gather(cot_hbm, cot_all, cot_sem, UP_FIRST, HALVES)
    if in_kernel:
        spread_a = Spread(n, pack_a, w_ref, a_sem)
        spread_b = Spread(n, pack_b, w_b, b_sem)
        spread_a.start()
        tick = Trickle(spread_b.trickle())
    else:
        copy_a = pltpu.make_async_copy(pack_a, w_ref, lsem.at[CUBE])
        copy_b = pltpu.make_async_copy(pack_b, w_b, lsem.at[CUBE + 1])
        copy_a.start()
        tick = Trickle([copy_b])
    g_tok.start(0)
    for p in range(3):
        g_tok.advance(p)
    tick.flush()
    g_cot.start(0)
    g_tok.finish()
    if in_kernel:
        spread_a.finish()
    else:
        copy_a.wait()

    state_mine[...] = jnp.zeros_like(state_mine)
    gain_one = w_ref[160:161, :].astype(F32)

    def project(jj, c):
        for h in range(2):

            def norm(at):
                x = wide[jj, h, at].astype(F32)
                root = lax.rsqrt(jnp.mean(x * x, axis=-1, keepdims=True) + EPS)
                wide[jj, h, at] = (x * root * gain_one).astype(BF16)

            row_loop(half, 16, norm)
            low = wide[jj, h]
            at = pl.ds(pl.multiple_of(jj * rows + h * half, half), half)
            k = dot_nt(low, w_ref[144:160, :]).astype(BF16)
            v = dot_nt(low, w_ref[0:128, :]).astype(BF16)
            lane = lax.broadcasted_iota(jnp.int32, (half, 128), 1)
            v_ext = jnp.concatenate([v, jnp.where(lane < 2, 1.0, 0.0).astype(BF16)], axis=1)
            q_ref[at, :] = dot_nt(low, w_ref[128:144, :]).astype(BF16)
            k_ref[at, :] = k
            v_ref[at, :] = v_ext
            _, seg = segments(two, three, start + jj * rows + h * half, half, 0)
            keep = (seg == 1).astype(F32)
            kept[at, :] = v_ext * keep.astype(BF16)
            quad, line = lift(k, keep, first[...], second[...], third[...])
            state_mine[0:256, :] += dot_tn(quad, v_ext)
            state_mine[256:384, :] += dot_tn(line, v_ext)
        return c

    lax.fori_loop(0, CUBE, project, 0)
    save = pltpu.make_async_copy(wide, low_hbm, lsem.at[0])
    save.start()
    done = exchange(groups, state_mine, state_theirs, xsend, xrecv, True)
    g_cot.advance(0)

    blocks = tokens // BLOCK
    for tb in range(blocks):
        tq = pl.ds(tb * BLOCK, BLOCK)
        qt = q_ref[tq, :] * BF16(0.25)
        score = dot_nt(qt, k_ref[tq, :])
        mask = pair_mask(two, three, start + tb * BLOCK, start + tb * BLOCK, BLOCK)
        acc = dot(jnp.where(mask, pair_weight(score), 0.0).astype(BF16), v_ref[tq, :])
        if tb:
            _, seg = segments(two, three, start + tb * BLOCK, BLOCK, 0)
            far = jnp.zeros((BLOCK, 256), F32)
            for lo in range(0, tb * BLOCK, 512):
                sq = pl.ds(lo, min(512, tb * BLOCK - lo))
                far = far + dot(pair_weight(dot_nt(qt, k_ref[sq, :])).astype(BF16), kept[sq, :])
            acc = acc + far * (seg == 1).astype(F32)
        y_ref[tq, :] = acc[:, :128]
        den_ref[tq, :] = acc[:, 128:]

    g_cot.advance(1)
    state = done()
    state_ref[...] = state
    high, lowp = two_terms(state)
    out_sum = Sum(part, heap, total, sum_sem)
    out_w = w_ref[176:304, :]

    for idx, r in enumerate(Sum.ORDER):
        jj = flip(j, r)
        tq = pl.ds(pl.multiple_of(jj * rows, rows), rows)
        _, seg = segments(two, three, start + jj * rows, rows, 0)
        quad, line = lift(q_ref[tq, :], (seg == 1).astype(F32), first[...], second[...], third[...])
        more = dot(quad, high[0:256]) + dot(quad, lowp[0:256]) + dot(line, high[256:384]) + dot(line, lowp[256:384])
        den = den_ref[tq, :] + more[:, 128:]
        den_ref[tq, :] = den
        y = (y_ref[tq, :] + more[:, :128]) / den[:, 0:1]
        y_ref[tq, :] = y
        y_low = y.astype(BF16)
        y_turned[:, tq] = y_low.T
        for h in range(2):
            part[jj, h] = dot(y_low[h * half : (h + 1) * half], out_w).astype(BF16)
        out_sum.send(r)
        if idx:
            out_sum.take(Sum.ORDER[idx - 1])
    out_sum.take(Sum.ORDER[-1])
    for p in range(3):
        out_sum.phase(p)
    out_sum.trade()
    out_sum.finish()

    gain_two = w_ref[161:162, :].astype(F32)
    for h in range(2):

        def second_norm(at):
            mid = tok_ref[h, at].astype(F32) + total[h, at]
            mid_ref[h, at] = mid
            root = lax.rsqrt(jnp.mean(mid * mid, axis=-1, keepdims=True) + EPS)
            own[h, at] = (mid * root * gain_two).astype(BF16)

        row_loop(half, 16, second_norm)

    g_cot.advance(2)
    g_cot.finish()
    save.wait()
    if in_kernel:
        spread_b.finish()
    else:
        copy_b.wait()


def head_call(n, lengths, pack_a, pack_b, tokens, cot):
    groups = n // CUBE
    rows, width = tokens.shape
    half = rows // 2
    count = CUBE * rows
    vm = pl.BlockSpec(memory_space=pltpu.VMEM)
    any_space = pl.BlockSpec(memory_space=pl.ANY)
    peers = max(groups - 1, 1)
    w_rows = (pack_a.shape[1], pack_b.shape[1])
    if width // n % 128:
        pack_a, pack_b = spread_call(n, pack_a, width, 4), spread_call(n, pack_b, width, 5)
    shape = (CUBE, 2, half, width)
    return pl.pallas_call(
        functools.partial(head_kernel, n),
        out_shape=[
            jax.ShapeDtypeStruct((w_rows[0], width), BF16),
            jax.ShapeDtypeStruct((w_rows[1], width), BF16),
            jax.ShapeDtypeStruct(shape, BF16),
            jax.ShapeDtypeStruct(shape, BF16),
            jax.ShapeDtypeStruct((2, half, width), BF16),
            jax.ShapeDtypeStruct((2, half, width), F32),
            jax.ShapeDtypeStruct((count, FEAT), BF16),
            jax.ShapeDtypeStruct((count, FEAT), BF16),
            jax.ShapeDtypeStruct((count, 256), BF16),
            jax.ShapeDtypeStruct((count, 128), F32),
            jax.ShapeDtypeStruct((128, count), BF16),
            jax.ShapeDtypeStruct((count, 128), F32),
            jax.ShapeDtypeStruct((384, 256), F32),
        ],
        in_specs=[pl.BlockSpec(memory_space=pltpu.SMEM), vm, any_space, any_space, any_space, vm, vm, vm],
        out_specs=[vm, any_space, any_space, any_space] + [vm] * 9,
        scratch_shapes=[
            pltpu.VMEM(shape, BF16),
            pltpu.VMEM(shape, BF16),
            pltpu.VMEM((15, half, width), BF16),
            pltpu.VMEM((2, half, width), F32),
            pltpu.VMEM((count, 256), BF16),
            pltpu.VMEM((384, 256), F32),
            pltpu.VMEM((peers, 384, 256), F32),
            pltpu.SemaphoreType.DMA((peers,)),
            pltpu.SemaphoreType.DMA((peers,)),
            pltpu.SemaphoreType.DMA((CUBE + 2,)),
            *sum_sems(),
            *gather_sems(),
            *gather_sems(),
            *spread_sems(n),
            *spread_sems(n),
        ],
        compiler_params=pltpu.CompilerParams(collective_id=1, has_side_effects=True, vmem_limit_bytes=62 * MIB),
    )(lengths, tokens.reshape(2, half, width), pack_a, pack_b, cot.reshape(2, half, width), *spreaders())


def mlp_kernel(
    n, own, w_ref, y_turned, mid_hbm, w_hbm, pack_d, cot_hbm,
    hidden, down, grads_b, tiles_d, grads_o, d_mid, dy_ref,
    wide, wide_g, part, heap, total, w_gu, by_gate, by_up, d_gate, d_up, grads_d, lsem, *sems,
):
    s, t, j, base = whereabouts()
    half, width = own.shape[1:]
    rows = 2 * half
    in_kernel = len(pack_d.shape) == 3
    two_sem, attn_sem, low_sem, d_sem, back_sem = sems[0:5], sems[5:10], sems[10:16], sems[16:19], sems[19:22]

    load_w = pltpu.make_async_copy(w_hbm, w_gu, lsem.at[0])
    load_mid = pltpu.make_async_copy(mid_hbm, d_mid, lsem.at[1])
    load_w.start()
    load_mid.start()
    greet_all(n)
    load_cot = pltpu.make_async_copy(cot_hbm, wide_g, lsem.at[6])
    load_cot.start()
    g_two = Gather(own, wide, two_sem)
    g_two.start(0)
    if in_kernel:
        spread_d = Spread(n, pack_d, down, d_sem)
        tick = Trickle(spread_d.trickle())
    else:
        copy_d = pltpu.make_async_copy(pack_d, down, lsem.at[2])
        tick = Trickle([copy_d])
    for p in range(3):
        g_two.advance(p, tick)
    tick.flush()
    g_two.finish()
    load_w.wait()

    def forward(jj, c):
        at = pl.ds(pl.multiple_of(jj * rows, rows), rows)
        low = wide[jj].reshape(rows, width)
        gate = dot_nt(w_gu[0:UNITS, :], low)
        up = dot_nt(w_gu[UNITS:, :], low)
        sigma = jax.nn.sigmoid(gate)
        silu = gate * sigma
        hidden[:, at] = (silu * up).astype(BF16)
        by_gate[:, at] = (up * sigma * (1.0 + gate * (1.0 - sigma))).astype(BF16)
        by_up[:, at] = silu.astype(BF16)
        return c

    lax.fori_loop(0, CUBE, forward, 0)
    load_cot.wait()
    if in_kernel:
        spread_d.finish()
    else:
        copy_d.wait()

    low_sum = Sum(part, heap, total, low_sem)
    for idx, r in enumerate(Sum.ORDER):
        jj = flip(j, r)
        at = pl.ds(pl.multiple_of(jj * rows, rows), rows)
        grad = dot_nt(down[...], wide_g[jj].reshape(rows, width))
        dg = (grad * by_gate[:, at].astype(F32)).astype(BF16)
        du = (grad * by_up[:, at].astype(F32)).astype(BF16)
        d_gate[:, at] = dg
        d_up[:, at] = du
        for col in range(0, width, 512):
            cols = pl.ds(col, 512)
            block = dot_tn(dg, w_gu[0:UNITS, cols]) + dot_tn(du, w_gu[UNITS:, cols])
            part[jj, :, :, cols] = block.astype(BF16).reshape(2, half, 512)
        low_sum.send(r)
        if idx:
            low_sum.take(Sum.ORDER[idx - 1])
    low_sum.take(Sum.ORDER[-1])

    def weight_grad(left, right, out, first_row):
        def one(m, c):
            cols = pl.ds(pl.multiple_of(m * 256, 256), 256)
            block = dot(left[...], right[:, :, :, cols].reshape(CUBE * rows, 256))
            out[first_row : first_row + UNITS, cols] = block.astype(BF16)
            return c

        lax.fori_loop(0, width // 256, one, 0)

    weight_grad(hidden, wide_g, grads_d, 0)
    low_sum.phase(0)
    weight_grad(d_gate, wide, w_gu, 0)
    low_sum.phase(1)
    weight_grad(d_up, wide, w_gu, UNITS)
    save_gu = pltpu.make_async_copy(w_gu, grads_b, lsem.at[3])
    save_gu.start()
    if in_kernel:
        back_d = Back(n, grads_d, tiles_d, back_sem)
        tick = Trickle(back_d.trickle())
    else:
        save_d = pltpu.make_async_copy(grads_d, tiles_d, lsem.at[4])
        tick = Trickle([save_d])
    low_sum.phase(2)
    low_sum.trade()
    low_sum.finish()
    load_mid.wait()

    gain_two = w_ref[161:162, :].astype(F32)
    for h in range(2):

        def norm_back_two(at):
            mid = d_mid[h, at]
            root = lax.rsqrt(jnp.mean(mid * mid, axis=-1, keepdims=True) + EPS)
            normed = mid * root
            scaled = total[h, at] * gain_two
            grad = wide_g[j, h, at].astype(F32) + root * (
                scaled - normed * jnp.mean(scaled * normed, axis=-1, keepdims=True)
            )
            d_mid[h, at] = grad
            own[h, at] = grad.astype(BF16)

        row_loop(half, 16, norm_back_two)

    Gather(own, wide_g, attn_sem).run(tick)
    tick.flush()

    def project(jj, c):
        at = pl.ds(pl.multiple_of(jj * rows, rows), rows)
        dy_ref[at, :] = dot_nt(wide_g[jj].reshape(rows, width), w_ref[176:304, :]).astype(BF16)
        return c

    lax.fori_loop(0, CUBE, project, 0)

    def output_grad(m, c):
        cols = pl.ds(pl.multiple_of(m * 256, 256), 256)
        block = dot(y_turned[...], wide_g[:, :, :, cols].reshape(CUBE * rows, 256))
        grads_o[:, cols] = block.astype(BF16)
        return c

    lax.fori_loop(0, width // 256, output_grad, 0)
    save_gu.wait()
    if in_kernel:
        back_d.finish()
    else:
        save_d.wait()


def mlp_call(n, own, w_a, y_turned, mid, w_gu, pack_d, cot_all):
    half, width = own.shape[1:]
    count = CUBE * 2 * half
    vm = pl.BlockSpec(memory_space=pltpu.VMEM)
    any_space = pl.BlockSpec(memory_space=pl.ANY)
    if width // n % 128:
        pack_d = spread_call(n, pack_d, width, 6)
    shape = (CUBE, 2, half, width)
    return pl.pallas_call(
        functools.partial(mlp_with_own, n),
        out_shape=[
            jax.ShapeDtypeStruct((UNITS, count), BF16),
            jax.ShapeDtypeStruct((UNITS, width), BF16),
            jax.ShapeDtypeStruct((2 * UNITS, width), BF16),
            jax.ShapeDtypeStruct((UNITS, width) if width // n % 128 else (n, UNITS, width // n), BF16),
            jax.ShapeDtypeStruct((128, width), BF16),
            jax.ShapeDtypeStruct((2, half, width), F32),
            jax.ShapeDtypeStruct((count, 128), BF16),
        ],
        in_specs=[any_space, vm, vm] + [any_space] * 4,
        out_specs=[vm, vm, any_space, any_space, vm, vm, vm],
        scratch_shapes=[
            pltpu.VMEM((2, half, width), BF16),
            pltpu.VMEM(shape, BF16),
            pltpu.VMEM(shape, BF16),
            pltpu.VMEM(shape, BF16),
            pltpu.VMEM((15, half, width), BF16),
            pltpu.VMEM((2, half, width), F32),
            pltpu.VMEM((2 * UNITS, width), BF16),
            pltpu.VMEM((UNITS, count), BF16),
            pltpu.VMEM((UNITS, count), BF16),
            pltpu.VMEM((UNITS, count), BF16),
            pltpu.VMEM((UNITS, count), BF16),
            pltpu.VMEM((UNITS, width), BF16),
            pltpu.SemaphoreType.DMA((7,)),
            *gather_sems(),
            *gather_sems(),
            *sum_sems(),
            *spread_sems(n),
            *spread_sems(n),
        ],
        compiler_params=pltpu.CompilerParams(collective_id=3, has_side_effects=True, vmem_limit_bytes=63 * MIB),
    )(own, w_a, y_turned, mid, w_gu, pack_d, cot_all)


def mlp_with_own(n, own_hbm, w_ref, y_turned, mid_hbm, w_hbm, pack_d, cot_hbm, *rest):
    outs, (own, *scratch) = rest[:7], rest[7:]
    lsem = scratch[11]
    load = pltpu.make_async_copy(own_hbm, own, lsem.at[5])
    load.start()
    load.wait()
    mlp_kernel(n, own, w_ref, y_turned, mid_hbm, w_hbm, pack_d, cot_hbm, *outs, *scratch)


def tail_kernel(
    n, lengths, q_ref, k_ref, v_ref, y_ref, den_ref, state_ref, w_ref, tok_ref, dy_ref, hidden, down,
    grads_o, mid, d_mid, low_hbm, grads_b, first, second, third,
    output_ref, grad_ref, tiles_b, tiles_a,
    part, heap_a, heap_b, wide, total, c_ref, c_kept, v_kept, side, dv, turned, dqkv, grads_a,
    state_mine, state_theirs, xsend, xrecv, lsem, *sems,
):
    groups = n // CUBE
    s, t, j, base = whereabouts()
    tokens = q_ref.shape[0]
    rows = tokens // CUBE
    half = rows // 2
    width = w_ref.shape[1]
    two, three = lengths[0], lengths[0] + lengths[1]
    start = base * rows
    in_kernel = len(tiles_a.shape) == 3
    sum_out, sum_one, bsems, asems = sems[0:6], sems[6:12], sems[12:15], sems[15:18]

    load_low = pltpu.make_async_copy(low_hbm, wide, lsem.at[2])
    load_low.start()
    load_mid = pltpu.make_async_copy(mid, grad_ref, lsem.at[0])
    load_mid.start()
    greet_all(n)
    out_sum = Sum(part, heap_b, total, sum_out, UP_LAST, HALVES)
    back_b = Back(n, grads_b, tiles_b, bsems) if in_kernel else None

    tick = Trickle(back_b.trickle()) if in_kernel else Trickle([])

    state_mine[...] = jnp.zeros_like(state_mine)
    state = state_ref[...].astype(BF16)
    blocks = tokens // BLOCK

    def early(tb, carry):
        tq = pl.ds(pl.multiple_of(tb * BLOCK, BLOCK), BLOCK)
        _, seg = segments(two, three, start + tb * BLOCK, BLOCK, 0)
        keep = (seg == 1).astype(F32)
        c = (dy_ref[tq, :].astype(F32) / den_ref[tq, 0:1]).astype(BF16)
        m = -jnp.sum(c.astype(F32) * y_ref[tq, :], axis=-1, keepdims=True)
        m_high = m.astype(BF16).astype(F32)
        lane = lax.broadcasted_iota(jnp.int32, (BLOCK, 128), 1)
        extra = jnp.where(lane == 0, m_high, jnp.where(lane == 1, m - m_high, 0.0)).astype(BF16)
        c_ext = jnp.concatenate([c, extra], axis=1)
        c_ref[tq, :] = c_ext
        c_kept[tq, :] = c_ext * keep.astype(BF16)
        v_kept[tq, :] = v_ref[tq, :] * keep.astype(BF16)
        u = q_ref[tq, :]
        quad, line = lift(u, keep, first[...], second[...], third[...])
        state_mine[0:256, :] += dot_tn(quad, c_ext)
        state_mine[256:384, :] += dot_tn(line, c_ext)
        d_quad = dot_nt(c_ext, state[0:256]) * keep
        d_line = dot_nt(c_ext, state[256:384]) * keep
        side[tq, 0:FEAT] = lift_back(u, d_quad, d_line, first[...], second[...])
        return carry

    tick(4)
    lax.fori_loop(0, blocks, early, 0)
    done = exchange(groups, state_mine, state_theirs, xsend, xrecv, False)
    for r in Sum.ORDER:
        jj = flip(j, r)
        at = pl.ds(pl.multiple_of(jj * rows, rows), rows)
        for col in range(0, width, 512):
            cols = pl.ds(col, 512)
            part[jj, :, :, cols] = dot_tn(hidden[:, at], down[:, cols]).astype(BF16).reshape(2, half, 512)
        out_sum.send(r)
    for r in Sum.ORDER:
        out_sum.take(r)

    for tb in range(blocks):
        tq = pl.ds(tb * BLOCK, BLOCK)
        qt = q_ref[tq, :] * BF16(0.25)
        score = dot_nt(qt, k_ref[tq, :])
        mask = pair_mask(two, three, start + tb * BLOCK, start + tb * BLOCK, BLOCK)
        grad = jnp.where(mask, dot_nt(c_ref[tq, :], v_ref[tq, :]) * (1.0 + score), 0.0).astype(BF16)
        acc = dot(grad, k_ref[tq, :])
        for lo in range(0, tb * BLOCK, 512):
            sq = pl.ds(lo, min(512, tb * BLOCK - lo))
            score = dot_nt(qt, k_ref[sq, :])
            grad = (dot_nt(c_kept[tq, :], v_kept[sq, :]) * (1.0 + score)).astype(BF16)
            acc = acc + dot(grad, k_ref[sq, :])
        side[tq, 0:FEAT] = (side[tq, 0:FEAT] + acc * 0.5) * 0.5
        tick()
    out_sum.phase(0)
    for sb in range(blocks):
        sq = pl.ds(sb * BLOCK, BLOCK)
        ks = k_ref[sq, :] * BF16(0.25)
        score = dot_nt(ks, q_ref[sq, :])
        mask = pair_mask_turned(two, three, start + sb * BLOCK, start + sb * BLOCK, BLOCK)
        grad = jnp.where(mask, dot_nt(v_ref[sq, :], c_ref[sq, :]) * (1.0 + score), 0.0).astype(BF16)
        weight = jnp.where(mask, pair_weight(score), 0.0).astype(BF16)
        acc = dot(grad, q_ref[sq, :])
        near = dot(weight, c_ref[sq, :])
        far = jnp.zeros((BLOCK, 256), F32)
        for lo in range((sb + 1) * BLOCK, tokens, 512):
            tq = pl.ds(lo, min(512, tokens - lo))
            score = dot_nt(ks, q_ref[tq, :])
            grad = (dot_nt(v_kept[sq, :], c_kept[tq, :]) * (1.0 + score)).astype(BF16)
            acc = acc + dot(grad, q_ref[tq, :])
            far = far + dot(pair_weight(score).astype(BF16), c_kept[tq, :])
        _, seg = segments(two, three, start + sb * BLOCK, BLOCK, 0)
        side[sq, FEAT : 2 * FEAT] = acc * 0.5
        dv[sq, :] = (near + far * (seg == 1).astype(F32))[:, :128]
        tick()
        if sb == blocks // 2:
            out_sum.phase(1)
    tick.flush()
    out_sum.phase(2)
    out_sum.trade()
    state_back = done().astype(BF16)

    def late(sb, carry):
        sq = pl.ds(pl.multiple_of(sb * BLOCK, BLOCK), BLOCK)
        _, seg = segments(two, three, start + sb * BLOCK, BLOCK, 0)
        keep = (seg == 1).astype(F32)
        u = k_ref[sq, :]
        v = v_ref[sq, :]
        quad, line = lift(u, keep, first[...], second[...], third[...])
        d_quad = dot_nt(v, state_back[0:256]) * keep
        d_line = dot_nt(v, state_back[256:384]) * keep
        more = dot(quad, state_back[0:256]) + dot(line, state_back[256:384])
        dk = (side[sq, FEAT : 2 * FEAT] + lift_back(u, d_quad, d_line, first[...], second[...])) * 0.5
        dqkv[sq, 0:128] = (dv[sq, :] + more[:, :128]).astype(BF16)
        packed = dot(side[sq, 0:FEAT].astype(BF16), third[...]) + dot(dk.astype(BF16), third_shifted(third[...]))
        dqkv[sq, 128:256] = packed.astype(BF16)
        turned[:, sq] = dqkv[sq, :].T
        return carry

    lax.fori_loop(0, blocks, late, 0)
    out_sum.finish()
    load_mid.wait()
    for h in range(2):

        def finish_output(at):
            output_ref[h, at] = (grad_ref[h, at] + total[h, at]).astype(BF16)

        row_loop(half, 16, finish_output)
    load_mid = pltpu.make_async_copy(d_mid, grad_ref, lsem.at[1])
    load_mid.start()

    load_low.wait()
    one_sum = Sum(part, heap_a, total, sum_one)
    w_one = w_ref[0:160, :]
    for idx, r in enumerate(Sum.ORDER):
        jj = flip(j, r)
        for h in range(2):
            at = pl.ds(pl.multiple_of(jj * rows + h * half, half), half)
            part[jj, h] = dot(dqkv[at, 0:160], w_one).astype(BF16)
        one_sum.send(r)
        if idx:
            one_sum.take(Sum.ORDER[idx - 1])
    one_sum.take(Sum.ORDER[-1])

    def one_grad(m, c):
        cols = pl.ds(pl.multiple_of(m * 256, 256), 256)
        block = dot(turned[0:160, :], wide[:, :, :, cols].reshape(tokens, 256))
        grads_a[0:160, cols] = block.astype(BF16)
        return c

    lax.fori_loop(0, width // 256, one_grad, 0)
    grads_a[160:288, :] = grads_o[...]
    if in_kernel:
        back_a = Back(n, grads_a, tiles_a, asems)
        back_a.start()
    else:
        copy = pltpu.make_async_copy(grads_a, tiles_a, lsem.at[3])
        copy.start()
    for p in range(3):
        one_sum.phase(p)
    one_sum.trade()
    one_sum.finish()

    gain_one = w_ref[160:161, :].astype(F32)
    load_mid.wait()
    for h in range(2):

        def norm_back_one(at):
            x = tok_ref[h, at].astype(F32)
            root = lax.rsqrt(jnp.mean(x * x, axis=-1, keepdims=True) + EPS)
            normed = x * root
            scaled = total[h, at] * gain_one
            grad_ref[h, at] = grad_ref[h, at] + root * (
                scaled - normed * jnp.mean(scaled * normed, axis=-1, keepdims=True)
            )

        row_loop(half, 16, norm_back_one)

    if in_kernel:
        back_b.finish()
        back_a.finish()
    else:
        copy.wait()


def third_shifted(third):
    return jnp.concatenate([jnp.zeros_like(third[:, :FEAT]), third[:, : 128 - FEAT]], axis=1)


def tail_call(n, lengths, q, k, v, y, den, state, w_a, mid, tokens, d_mid, dy, hidden, down, grads_o, low_one, grads_b):
    groups = n // CUBE
    _, half, width = mid.shape
    rows = 2 * half
    count = CUBE * rows
    wide_columns = width // n % 128 == 0
    vm = pl.BlockSpec(memory_space=pltpu.VMEM)
    any_space = pl.BlockSpec(memory_space=pl.ANY)
    peers = max(groups - 1, 1)
    out_shape = [
        jax.ShapeDtypeStruct((2, half, width), BF16),
        jax.ShapeDtypeStruct((2, half, width), F32),
        jax.ShapeDtypeStruct((n, grads_b.shape[0], width // n) if wide_columns else (8, 128), BF16),
        jax.ShapeDtypeStruct((n, 288, width // n) if wide_columns else (288, width), BF16),
    ]
    output, grad, tiles_b, tiles_a = pl.pallas_call(
        functools.partial(tail_kernel, n),
        out_shape=out_shape,
        in_specs=[pl.BlockSpec(memory_space=pltpu.SMEM)] + [vm] * 12 + [any_space] * 4 + [vm] * 3,
        out_specs=[vm, vm, any_space, any_space],
        scratch_shapes=[
            pltpu.VMEM((CUBE, 2, half, width), BF16),
            pltpu.VMEM((15, half, width), BF16),
            pltpu.VMEM((15, half, width), BF16),
            pltpu.VMEM((CUBE, 2, half, width), BF16),
            pltpu.VMEM((2, half, width), F32),
            pltpu.VMEM((count, 256), BF16),
            pltpu.VMEM((count, 256), BF16),
            pltpu.VMEM((count, 256), BF16),
            pltpu.VMEM((count, 128), F32),
            pltpu.VMEM((count, 128), F32),
            pltpu.VMEM((256, count), BF16),
            pltpu.VMEM((count, 256), BF16),
            pltpu.VMEM((288, width), BF16),
            pltpu.VMEM((384, 256), F32),
            pltpu.VMEM((peers, 384, 256), F32),
            pltpu.SemaphoreType.DMA((peers,)),
            pltpu.SemaphoreType.DMA((peers,)),
            pltpu.SemaphoreType.DMA((4,)),
            *sum_sems(),
            *sum_sems(),
            *spread_sems(n),
            *spread_sems(n),
        ],
        compiler_params=pltpu.CompilerParams(collective_id=2, has_side_effects=True, vmem_limit_bytes=63 * MIB),
    )(
        lengths, q, k, v, y, den, state, w_a, tokens.reshape(2, half, width), dy, hidden, down, grads_o,
        mid, d_mid, low_one, grads_b, *spreaders(),
    )
    if not wide_columns:
        tiles_b = back_call(n, grads_b, 9)
        tiles_a = back_call(n, tiles_a, 10)
    return output.reshape(rows, width), grad.reshape(rows, width), tiles_b, tiles_a


def units_first(w):
    return jnp.pad(w, ((0, CUBE * UNITS - w.shape[0]), (0, 0))).reshape(CUBE, UNITS, w.shape[1])


def body(
    n, tokens, gain_attn, w_query, w_key, w_value, w_output, gain_mlp, w_gate, w_up, w_down, seq_lengths, cotangent
):
    per = HEADS // lax.axis_size("tensor")
    gains = jnp.concatenate([gain_attn[None], gain_mlp[None], jnp.zeros((14, gain_attn.shape[0]), BF16)], axis=0)
    pack_a = jnp.concatenate(
        [
            w_value.T.reshape(per, 128, -1),
            w_query.T.reshape(per, FEAT, -1),
            w_key.T.reshape(per, FEAT, -1),
            jnp.broadcast_to(gains[None], (per, *gains.shape)),
            w_output.reshape(per, 128, -1),
        ],
        axis=1,
    )
    pack_b = jnp.concatenate([units_first(w_gate.T), units_first(w_up.T)], axis=1)
    w_a, w_gu, cot_all, low_one, low_two, mid, q, k, v, y, y_turned, den, state = head_call(
        n, seq_lengths, pack_a, pack_b, tokens, cotangent
    )
    hidden, down, grads_b, tiles_d, grads_o, d_mid, dy = mlp_call(
        n, low_two, w_a, y_turned, mid, w_gu, units_first(w_down), cot_all
    )
    if tiles_d.ndim == 2:
        tiles_d = back_call(n, tiles_d, 7)
    output, grad_tokens, tiles_b, tiles_a = tail_call(
        n, seq_lengths, q, k, v, y, den, state, w_a, mid, tokens, d_mid, dy, hidden, down, grads_o, low_one, grads_b
    )

    def arrived(tiles):
        return tiles.reshape(-1, CUBE, *tiles.shape[1:]).astype(F32).sum(axis=0)

    back_b, back_d, back_a = arrived(tiles_b), arrived(tiles_d), arrived(tiles_a)

    def units(part):
        return part.reshape(CUBE * UNITS, -1)[: w_gate.shape[1]]

    grad_gate = units(back_b[:, :UNITS]).T
    grad_up = units(back_b[:, UNITS : 2 * UNITS]).T
    grad_down = units(back_d)
    grad_value = back_a[:, 0:128].reshape(per * 128, -1).T
    grad_query = back_a[:, 128:144].reshape(per * FEAT, -1).T
    grad_key = back_a[:, 144:160].reshape(per * FEAT, -1).T
    grad_output = back_a[:, 160:288].reshape(per * 128, -1)

    def weighed(*pairs):
        return sum(jnp.sum(w.astype(F32) * g, axis=1) for w, g in pairs)

    gain_one_part = weighed((w_value, grad_value), (w_query, grad_query), (w_key, grad_key))
    gain_two_part = weighed((w_gate, grad_gate), (w_up, grad_up))
    both = lax.psum(jnp.stack([gain_one_part, gain_two_part]), "tensor")
    grad_gain_one = both[0] / gain_attn.astype(F32)
    grad_gain_two = both[1] / gain_mlp.astype(F32)
    return (
        output,
        grad_tokens,
        grad_gain_one,
        grad_query,
        grad_key,
        grad_value,
        grad_output,
        grad_gain_two,
        grad_gate,
        grad_up,
        grad_down,
    )


def solution(mesh):
    return jax.shard_map(
        functools.partial(body, mesh.shape["seq"]),
        mesh=mesh,
        in_specs=(
            P("seq", None),
            P("seq"),
            P("seq", "tensor"),
            P("seq", "tensor"),
            P("seq", "tensor"),
            P("tensor", "seq"),
            P("seq"),
            P("seq", "tensor"),
            P("seq", "tensor"),
            P("tensor", "seq"),
            P(),
            P("seq", None),
        ),
        out_specs=(
            P("seq", None),
            P("seq", None),
            P("seq"),
            P("seq", "tensor"),
            P("seq", "tensor"),
            P("seq", "tensor"),
            P("tensor", "seq"),
            P("seq"),
            P("seq", "tensor"),
            P("seq", "tensor"),
            P("tensor", "seq"),
        ),
        check_vma=False,
    )
```

time: 714 us -> 583 us (0.82)
  the two profiles are of different devices: /device:TPU:9 before, /device:TPU:0 now
where the time goes in v3:
time: 583 us; the launch traced here: 573 us
  Pallas kernels  547 us (94%)
  local copies, waits for them, and re-layouts  13.1 us (2%)
  other arithmetic  9.06 us (2%)
    pallas_call x1, Pallas kernels, head_call(): pl.pallas_call(functools.partial(head_kernel, n), out_shape=[jax.ShapeDty...  200 us
    pallas_call x1, Pallas kernels, mlp_call(): pl.pallas_call(functools.partial(mlp_with_own, n), out_shape=[jax.ShapeDt...  182 us
    pallas_call x1, Pallas kernels, tail_call(): pl.pallas_call(functools.partial(tail_kernel, n), out_shape=out_shape, in...  165 us

profile of v3, /device:TPU:0, one launch (start us, length us, event | category | flops | bytes accessed | tf_op | source)
XLA Modules:
  0.0 572.9 jit_solution(2782668566468774612)
XLA Ops:
  0.6 0.0 copy-start.10
  0.7 0.0 copy-start.1
  0.7 1.2 copy.35
  1.9 0.0 copy-start
  1.9 0.9 copy.36
  2.9 0.9 copy.37
  3.8 0.1 pad.19.clone
  3.8 0.7 maximum_maximum_fusion
  4.6 0.0 copy-done.10
  4.6 0.0 copy-start.6
  4.7 0.0 copy-done.1
  4.7 0.1 pad.10
  4.7 0.0 copy-done
  4.7 0.1 pad.11
  4.8 1.2 pad_maximum_fusion.pack_b
  6.0 0.0 copy-done.6
  6.0 0.0 copy-start.9
  6.0 199.6 %shard_map.257 = (bf16[304,2048]{1,0:T(8,128)(2,1)}, bf16[704,2048]{1,0:T(8,128)(2,1)}, bf16[8,2,128,2048]{3,2,1,0:T(8,128)(2,1)}, bf16[8,2,128,2048]{3,2,1,0:T(...) custom-call(s32[3]{0:T(128)} %lengths.3, ...), custom_call_target="tpu_custom_call" | custom-call | tf_op jit(solution)/shard_map/pallas_call | solution.py:664
  205.6 0.0 copy-done.9
  205.6 0.9 pad.12
  206.5 182.3 %shard_map.258 = (bf16[352,2048]{1,0:T(8,128)(2,1)}, bf16[352,2048]{1,0:T(8,128)(2,1)}, bf16[704,2048]{1,0:T(8,128)(2,1)}, bf16[16,352,128]{2,1,0:T(8,128)(2,1)}...) custom-call(bf16[2,128,2048]{2,1,0:T(8,128)(2,1)} %get-tuple-element.42.own_hbm, ...), custom_call_target="tpu_custom_call" | custom-call | tf_op jit(solution)/shard_map/pallas_call | solution.py:848
  388.8 164.9 %shard_map.259 = (bf16[2,128,2048]{2,1,0:T(8,128)(2,1)}, f32[2,128,2048]{2,1,0:T(8,128)}, bf16[16,704,128]{2,1,0:T(8,128)(2,1)}, bf16[16,288,128]{2,1,0:T(8,128)(2,1)}) custom-call(s32[3]{0:T(128)} %lengths.3, bf16[2048,16]{1,0:T(8,128)(2,1)} %get-tuple-element.35.q_ref, bf16[2048,16]{1,0:T(8,128)(2,1)} %get-tuple-element.36.k_ref, ...), custom_call_target="tpu_custom_call" | custom-call | tf_op jit(solution)/shard_map/pallas_call | solution.py:1105
  553.8 0.0 copy-start.11
  553.8 0.0 copy-start.12
  553.8 1.6 convert_reduce_fusion.2
  555.4 0.0 copy-done.11
  555.4 0.1 copy.39
  555.5 0.0 copy-done.12
  555.5 0.1 copy.40
  555.7 0.0 copy-start.8
  555.7 0.9 fusion.1
  556.6 0.2 copy.38
  556.8 0.0 copy-done.8
  556.8 0.0 copy-start.4
  556.8 0.1 multiply_reduce_fusion.2
  556.9 2.6 convert_reduce_fusion
  559.6 0.0 copy-done.4
  559.6 0.0 copy-start.2
  559.6 0.2 fusion
  559.8 0.9 copy-done.2
  560.7 0.0 copy-start.13
  560.7 0.0 copy-start.14
  560.7 0.0 copy-start.5
  560.7 1.9 multiply_reduce_fusion
  562.7 2.5 psum.7
  565.2 0.0 copy-done.13
  565.2 0.0 copy-done.14
  565.2 0.5 bitcast_divide_fusion
  565.7 0.7 copy.41
  566.4 0.7 copy.42
  567.2 0.0 copy-done.5
  567.2 0.2 convert_reduce_fusion.1
  567.4 0.0 copy-start.7
  567.4 1.2 slice.52
  568.6 0.5 copy-done.7
  569.1 0.0 copy-start.3
  569.1 1.0 copy.49
  570.1 1.0 copy-done.3
  571.1 1.3 copy.50
  (11 shorter events, 0.2 us)
Async XLA Ops:
  0.6 4.0 copy-start.10
  0.7 4.0 copy-start.1
  1.9 2.9 copy-start
  4.6 1.3 copy-start.6
  6.0 199.6 %copy-start.9 = (bf16[2752,128]{1,0:T(8,128)(2,1)S(1)}, bf16[2752,128]{1,0:T(8,128)(2,1)}, u32[]{:S(2)}) copy-start(bf16[2752,128]{1,0:T(8,128)(2,1)} %param.27) | copy-start | bytes 2113540
  553.8 1.6 copy-start.11
  553.8 1.7 copy-start.12
  555.7 1.1 copy-start.8
  556.8 2.8 copy-start.4
  559.6 1.1 copy-start.2
  560.7 4.5 copy-start.13
  560.7 4.5 copy-start.14
  560.7 6.5 %copy-start.5 = (bf16[16,352,128]{2,1,0:T(8,128)(2,1)S(1)}, bf16[16,352,128]{2,1,0:T(8,128)(2,1)}, u32[]{:S(2)}) copy-start(bf16[16,352,128]{2,1,0:T(8,128)(2,1)} %get-tuple-element.58) | copy-start | bytes 4325380
  567.4 1.7 copy-start.7
  569.1 2.0 copy-start.3

commit v4 on v3

--- a/solution.py
+++ b/solution.py
@@ -18,6 +18,7 @@
 BF16 = jnp.bfloat16
 ORDERS = ((0, 1, 2), (1, 2, 0), (2, 0, 1))
 PIECES = ((0, 48), (48, 48), (96, 32))
+WAVES = ((4, 1, 2), (6, 5, 3), (7,))
 UP_FIRST = ((2, 0, 1), (2, 1, 0))
 UP_LAST = ((0, 1, 2), (1, 0, 2))
 HALVES = ((0, 64), (64, 64))
@@ -87,10 +88,6 @@
         off, rows = self.pieces[i]
         return self.full.at[flip(self.j, r), self.t, pl.ds(off, rows)]
 
-    def other(self, r, i):
-        off, rows = self.pieces[i]
-        return self.full.at[flip(self.j, r), 1 - self.t, pl.ds(off, rows)]
-
     def hop(self, p, i, r):
         d = self.orders[i][p]
         off, rows = self.pieces[i]
@@ -98,68 +95,76 @@
         k = r | (1 << d)
         return remote(src, self.view(r, i), self.ssem.at[i, k], self.rsem.at[i, k], (self.base + flip(self.j, 1 << d), self.t))
 
-    def arrival(self, p, i, r):
-        d = self.orders[i][p]
-        k = r | (1 << d)
-        return remote(self.view(k, i), self.view(k, i), self.ssem.at[i, k], self.rsem.at[i, k], (self.base + flip(self.j, 1 << d), self.t))
-
-    def across(self, r, i, mine):
-        ref = self.view(r, i) if mine else self.other(r, i)
-        return remote(ref, ref, self.csend.at[i, r], self.crecv.at[i, r], (self.s, 1 - self.t))
+    def came(self, i, k):
+        p = max(q for q in range(3) if k >> self.orders[i][q] & 1)
+        return p, k ^ (1 << self.orders[i][p])
+
+    def arrival(self, i, k):
+        p, _ = self.came(i, k)
+        device = (self.base + flip(self.j, 1 << self.orders[i][p]), self.t)
+        return remote(self.view(k, i), self.view(k, i), self.ssem.at[i, k], self.rsem.at[i, k], device)
+
+    def across(self, r, mine):
+        ref = self.full.at[flip(self.j, r), self.t if mine else 1 - self.t]
+        return remote(ref, ref, self.csend.at[r], self.crecv.at[r], (self.s, 1 - self.t))
 
     def local(self):
         return pltpu.make_async_copy(self.own, self.full.at[self.j], self.lsem)
 
-    def start(self, p):
-        if p == 0:
-            self.local().start()
+    def start(self):
+        self.local().start()
+        for q in range(3):
+            for i in range(len(self.pieces)):
+                self.hop(q, i, 0).start()
+
+    def arrived(self, k):
         for i in range(len(self.pieces)):
-            for r in subsets(self.orders[i][:p]):
-                self.hop(p, i, r).start()
-
-    def arrive(self, p):
-        for i in range(len(self.pieces)):
-            for r in subsets(self.orders[i][:p]):
-                self.arrival(p, i, r).wait_recv()
-
-    def share(self, p):
-        for i in range(len(self.pieces)):
-            for r in subsets(self.orders[i][:p]):
-                self.across(r | (1 << self.orders[i][p]), i, True).start()
+            p, _ = self.came(i, k)
+            self.arrival(i, k).wait_recv()
+            for q in range(p + 1, 3):
+                self.hop(q, i, k).start()
+        self.across(k, True).start()
+
+    def wave(self, w, tick=lambda: None):
+        for k in WAVES[w]:
+            self.arrived(k)
+            tick()
+
+    def settle(self, r):
+        self.across(r, False).wait_recv()
+
+    def sent(self):
+        for k in range(1, CUBE):
+            self.across(k, True).wait_send()
+            for i in range(len(self.pieces)):
+                p, r = self.came(i, k)
+                self.hop(p, i, r).wait_send()
 
     def finish(self):
-        for i in range(len(self.pieces)):
-            for r in range(1, CUBE):
-                self.across(r, i, False).wait_recv()
-        for i in range(len(self.pieces)):
-            for r in range(1, CUBE):
-                self.across(r, i, True).wait_send()
-        for p in range(3):
-            for i in range(len(self.pieces)):
-                for r in subsets(self.orders[i][:p]):
-                    self.hop(p, i, r).wait_send()
+        for r in range(1, CUBE):
+            self.settle(r)
+        self.sent()
         self.local().wait()
 
-    def advance(self, p, tick=lambda: None):
-        for i in range(len(self.pieces)):
-            for r in subsets(self.orders[i][:p]):
-                k = r | (1 << self.orders[i][p])
-                self.arrival(p, i, r).wait_recv()
-                if p < 2:
-                    self.hop(p + 1, i, r).start()
-                    self.hop(p + 1, i, k).start()
-                self.across(k, i, True).start()
-                tick()
-
-    def run(self, tick=lambda: None):
-        self.start(0)
-        for p in range(3):
-            self.advance(p, tick)
-        self.finish()
+    def blocks(self, tick=lambda: None):
+        self.start()
+        self.local().wait()
+        yield 0
+        before = None
+        for k in WAVES[0] + WAVES[1] + WAVES[2]:
+            self.arrived(k)
+            tick()
+            if before:
+                self.settle(before)
+                yield before
+            before = k
+        self.settle(before)
+        yield before
+        self.sent()
 
 
 def gather_sems():
-    return [pltpu.SemaphoreType.DMA((3, CUBE))] * 4 + [pltpu.SemaphoreType.DMA]
+    return [pltpu.SemaphoreType.DMA((3, CUBE))] * 2 + [pltpu.SemaphoreType.DMA((CUBE,))] * 2 + [pltpu.SemaphoreType.DMA]
 
 
 SLOT = {0: 0, 1: 4, 2: 6}
@@ -197,7 +202,7 @@
     def send(self, r):
         self.across(r).start()
 
-    def take(self, r):
+    def take(self, r, leave=True):
         self.across(r).wait_recv()
         jj = flip(self.j, r)
         step = 32
@@ -210,28 +215,47 @@
             return c
 
         lax.fori_loop(0, self.part.shape[2] // step, one, 0)
+        if leave:
+            self.leave(r)
+
+    def leave(self, r):
         for i in range(len(self.pieces)):
-            if r >> self.orders[i][0] & 1:
+            if r >> self.orders[i][0] & 1 and r != 1 << self.orders[i][0]:
                 self.hop(0, i, r).start()
 
     def phase(self, p, tick=lambda: None):
-        for i in range(len(self.pieces)):
+        count = len(self.pieces)
+        for i, r in [(i, subsets(self.orders[i][p + 1 :])[-1 - m]) for m in range((4 >> p) - 1) for i in range(count)]:
             d = self.orders[i][p]
             off, rows = self.pieces[i]
-            for r in reversed(subsets(self.orders[i][p + 1 :])):
-                self.hop(p, i, r | (1 << d)).wait_recv()
-                jj = flip(self.j, r)
-                k = slot_of(self.orders[i], p, r)
-                for q in range(0, rows, 16):
-                    at = pl.ds(off + q, 16)
-                    new = self.part[jj, self.t, at].astype(F32) + self.heap[CUBE + k, at].astype(F32)
-                    if p == 2:
-                        self.total[self.t, at] = new
-                    else:
-                        self.part[jj, self.t, at] = new.astype(BF16)
-                if p < 2 and r >> self.orders[i][p + 1] & 1:
-                    self.hop(p + 1, i, r).start()
-                tick()
+            self.hop(p, i, r | (1 << d)).wait_recv()
+            jj = flip(self.j, r)
+            k = slot_of(self.orders[i], p, r)
+            for q in range(0, rows, 16):
+                at = pl.ds(off + q, 16)
+                new = self.part[jj, self.t, at].astype(F32) + self.heap[CUBE + k, at].astype(F32)
+                self.part[jj, self.t, at] = new.astype(BF16)
+            e = self.orders[i][p + 1]
+            if r >> e & 1 and (p == 1 or r != 1 << e):
+                self.hop(p + 1, i, r).start()
+            tick()
+        for i in range(count):
+            self.hop(p, i, 1 << self.orders[i][p]).start()
+
+    def close(self, tick=lambda: None):
+        for i in range(len(self.pieces)):
+            off, rows = self.pieces[i]
+            for p in range(3):
+                self.hop(p, i, 1 << self.orders[i][p]).wait_recv()
+            slots = [CUBE + slot_of(self.orders[i], p, 0) for p in range(3)]
+            for q in range(0, rows, 16):
+                at = pl.ds(off + q, 16)
+                new = self.part[self.j, self.t, at].astype(F32)
+                for k in slots:
+                    new = new + self.heap[k, at].astype(F32)
+                self.total[self.t, at] = new
+            tick()
+        self.trade()
 
     def both(self, half):
         ref = self.total.at[half]
@@ -240,11 +264,15 @@
     def trade(self):
         self.both(self.t).start()
 
-    def finish(self):
+    def crossed(self):
+        for r in range(CUBE):
+            self.across(r).wait_send()
+
+    def finish(self, crossed=False):
         self.both(1 - self.t).wait_recv()
         self.both(self.t).wait_send()
-        for r in range(CUBE):
-            self.across(r).wait_send()
+        if not crossed:
+            self.crossed()
         for p in range(3):
             for i in range(len(self.pieces)):
                 d = self.orders[i][p]
@@ -256,9 +284,9 @@
             self.send(r)
         for r in self.ORDER:
             self.take(r)
-        for p in range(3):
-            self.phase(p)
-        self.trade()
+        self.phase(0)
+        self.phase(1)
+        self.close()
         self.finish()
 
 
@@ -509,8 +537,8 @@
 
 
 def head_kernel(
-    n, lengths, tok_ref, pack_a, pack_b, cot_hbm, first, second, third,
-    w_ref, w_b, cot_all, low_hbm, own, mid_ref, q_ref, k_ref, v_ref, y_ref, y_turned, den_ref, state_ref,
+    n, lengths, tok_ref, pack_a, pack_o, pack_b, cot_hbm, first, second, third,
+    w_ref, wo_ref, w_b, cot_all, low_hbm, own, mid_ref, q_ref, k_ref, v_ref, y_ref, y_turned, den_ref, state_ref,
     wide, part, heap, total, kept, state_mine, state_theirs, xsend, xrecv, lsem, *sems,
 ):
     groups = n // CUBE
@@ -521,7 +549,8 @@
     two, three = lengths[0], lengths[0] + lengths[1]
     start = base * rows
     in_kernel = len(pack_a.shape) == 3
-    sum_sem, tok_sem, cot_sem, a_sem, b_sem = sems[0:6], sems[6:11], sems[11:16], sems[16:19], sems[19:22]
+    sum_sem, tok_sem, cot_sem = sems[0:6], sems[6:11], sems[11:16]
+    a_sem, b_sem, o_sem = sems[16:19], sems[19:22], sems[22:25]
 
     greet_all(n)
     g_tok = Gather(tok_ref, wide, tok_sem)
@@ -529,18 +558,20 @@
     if in_kernel:
         spread_a = Spread(n, pack_a, w_ref, a_sem)
         spread_b = Spread(n, pack_b, w_b, b_sem)
+        spread_o = Spread(n, pack_o, wo_ref, o_sem)
         spread_a.start()
-        tick = Trickle(spread_b.trickle())
+        tick = Trickle(spread_o.trickle() + spread_b.trickle())
     else:
         copy_a = pltpu.make_async_copy(pack_a, w_ref, lsem.at[CUBE])
         copy_b = pltpu.make_async_copy(pack_b, w_b, lsem.at[CUBE + 1])
+        copy_o = pltpu.make_async_copy(pack_o, wo_ref, lsem.at[CUBE + 2])
         copy_a.start()
-        tick = Trickle([copy_b])
-    g_tok.start(0)
-    for p in range(3):
-        g_tok.advance(p)
+        tick = Trickle([copy_o, copy_b])
+    g_tok.start()
+    for w in range(3):
+        g_tok.wave(w)
     tick.flush()
-    g_cot.start(0)
+    g_cot.start()
     g_tok.finish()
     if in_kernel:
         spread_a.finish()
@@ -558,29 +589,28 @@
                 root = lax.rsqrt(jnp.mean(x * x, axis=-1, keepdims=True) + EPS)
                 wide[jj, h, at] = (x * root * gain_one).astype(BF16)
 
-            row_loop(half, 16, norm)
-            low = wide[jj, h]
-            at = pl.ds(pl.multiple_of(jj * rows + h * half, half), half)
-            k = dot_nt(low, w_ref[144:160, :]).astype(BF16)
-            v = dot_nt(low, w_ref[0:128, :]).astype(BF16)
-            lane = lax.broadcasted_iota(jnp.int32, (half, 128), 1)
-            v_ext = jnp.concatenate([v, jnp.where(lane < 2, 1.0, 0.0).astype(BF16)], axis=1)
-            q_ref[at, :] = dot_nt(low, w_ref[128:144, :]).astype(BF16)
-            k_ref[at, :] = k
-            v_ref[at, :] = v_ext
-            _, seg = segments(two, three, start + jj * rows + h * half, half, 0)
-            keep = (seg == 1).astype(F32)
-            kept[at, :] = v_ext * keep.astype(BF16)
-            quad, line = lift(k, keep, first[...], second[...], third[...])
-            state_mine[0:256, :] += dot_tn(quad, v_ext)
-            state_mine[256:384, :] += dot_tn(line, v_ext)
+            row_loop(half, 64, norm)
+        at = pl.ds(pl.multiple_of(jj * rows, rows), rows)
+        qkv = dot_nt(wide[jj].reshape(rows, width), w_ref[0:160, :]).astype(BF16)
+        v, k = qkv[:, 0:128], qkv[:, 144:160]
+        lane = lax.broadcasted_iota(jnp.int32, (rows, 128), 1)
+        v_ext = jnp.concatenate([v, jnp.where(lane < 2, 1.0, 0.0).astype(BF16)], axis=1)
+        q_ref[at, :] = qkv[:, 128:144]
+        k_ref[at, :] = k
+        v_ref[at, :] = v_ext
+        _, seg = segments(two, three, start + jj * rows, rows, 0)
+        keep = (seg == 1).astype(F32)
+        kept[at, :] = v_ext * keep.astype(BF16)
+        quad, line = lift(k, keep, first[...], second[...], third[...])
+        state_mine[0:256, :] += dot_tn(quad, v_ext)
+        state_mine[256:384, :] += dot_tn(line, v_ext)
         return c
 
     lax.fori_loop(0, CUBE, project, 0)
     save = pltpu.make_async_copy(wide, low_hbm, lsem.at[0])
     save.start()
     done = exchange(groups, state_mine, state_theirs, xsend, xrecv, True)
-    g_cot.advance(0)
+    g_cot.wave(0)
 
     blocks = tokens // BLOCK
     for tb in range(blocks):
@@ -599,12 +629,16 @@
         y_ref[tq, :] = acc[:, :128]
         den_ref[tq, :] = acc[:, 128:]
 
-    g_cot.advance(1)
+    g_cot.wave(1)
     state = done()
     state_ref[...] = state
     high, lowp = two_terms(state)
     out_sum = Sum(part, heap, total, sum_sem)
-    out_w = w_ref[176:304, :]
+    if in_kernel:
+        spread_o.finish()
+    else:
+        copy_o.wait()
+    out_w = wo_ref[...]
 
     for idx, r in enumerate(Sum.ORDER):
         jj = flip(j, r)
@@ -624,9 +658,9 @@
         if idx:
             out_sum.take(Sum.ORDER[idx - 1])
     out_sum.take(Sum.ORDER[-1])
-    for p in range(3):
-        out_sum.phase(p)
-    out_sum.trade()
+    out_sum.phase(0)
+    out_sum.phase(1)
+    out_sum.close()
     out_sum.finish()
 
     gain_two = w_ref[161:162, :].astype(F32)
@@ -640,7 +674,7 @@
 
         row_loop(half, 16, second_norm)
 
-    g_cot.advance(2)
+    g_cot.wave(2)
     g_cot.finish()
     save.wait()
     if in_kernel:
@@ -649,7 +683,7 @@
         copy_b.wait()
 
 
-def head_call(n, lengths, pack_a, pack_b, tokens, cot):
+def head_call(n, lengths, pack_a, pack_o, pack_b, tokens, cot):
     groups = n // CUBE
     rows, width = tokens.shape
     half = rows // 2
@@ -660,11 +694,13 @@
     w_rows = (pack_a.shape[1], pack_b.shape[1])
     if width // n % 128:
         pack_a, pack_b = spread_call(n, pack_a, width, 4), spread_call(n, pack_b, width, 5)
+        pack_o = spread_call(n, pack_o, width, 11)
     shape = (CUBE, 2, half, width)
     return pl.pallas_call(
         functools.partial(head_kernel, n),
         out_shape=[
             jax.ShapeDtypeStruct((w_rows[0], width), BF16),
+            jax.ShapeDtypeStruct((128, width), BF16),
             jax.ShapeDtypeStruct((w_rows[1], width), BF16),
             jax.ShapeDtypeStruct(shape, BF16),
             jax.ShapeDtypeStruct(shape, BF16),
@@ -678,8 +714,8 @@
             jax.ShapeDtypeStruct((count, 128), F32),
             jax.ShapeDtypeStruct((384, 256), F32),
         ],
-        in_specs=[pl.BlockSpec(memory_space=pltpu.SMEM), vm, any_space, any_space, any_space, vm, vm, vm],
-        out_specs=[vm, any_space, any_space, any_space] + [vm] * 9,
+        in_specs=[pl.BlockSpec(memory_space=pltpu.SMEM), vm] + [any_space] * 4 + [vm] * 3,
+        out_specs=[vm, vm, any_space, any_space, any_space] + [vm] * 9,
         scratch_shapes=[
             pltpu.VMEM(shape, BF16),
             pltpu.VMEM(shape, BF16),
@@ -690,27 +726,29 @@
             pltpu.VMEM((peers, 384, 256), F32),
             pltpu.SemaphoreType.DMA((peers,)),
             pltpu.SemaphoreType.DMA((peers,)),
-            pltpu.SemaphoreType.DMA((CUBE + 2,)),
+            pltpu.SemaphoreType.DMA((CUBE + 3,)),
             *sum_sems(),
             *gather_sems(),
             *gather_sems(),
             *spread_sems(n),
             *spread_sems(n),
+            *spread_sems(n),
         ],
         compiler_params=pltpu.CompilerParams(collective_id=1, has_side_effects=True, vmem_limit_bytes=62 * MIB),
-    )(lengths, tokens.reshape(2, half, width), pack_a, pack_b, cot.reshape(2, half, width), *spreaders())
+    )(lengths, tokens.reshape(2, half, width), pack_a, pack_o, pack_b, cot.reshape(2, half, width), *spreaders())
 
 
 def mlp_kernel(
-    n, own, w_ref, y_turned, mid_hbm, w_hbm, pack_d, cot_hbm,
-    hidden, down, grads_b, tiles_d, grads_o, d_mid, dy_ref,
-    wide, wide_g, part, heap, total, w_gu, by_gate, by_up, d_gate, d_up, grads_d, lsem, *sems,
+    n, own, w_ref, wo_ref, y_turned, mid_hbm, w_hbm, pack_d, cot_hbm,
+    grads_u, tiles_d, tiles_g, out_half, grads_o, d_mid, dy_ref,
+    wide, wide_g, part, heap, total, w_gu, hidden, down, by_gate, by_up, d_gate, d_up, grads_d, lsem, *sems,
 ):
     s, t, j, base = whereabouts()
     half, width = own.shape[1:]
     rows = 2 * half
     in_kernel = len(pack_d.shape) == 3
-    two_sem, attn_sem, low_sem, d_sem, back_sem = sems[0:5], sems[5:10], sems[10:16], sems[16:19], sems[19:22]
+    two_sem, attn_sem, low_sem, out_sem = sems[0:5], sems[5:10], sems[10:16], sems[16:22]
+    d_sem, back_d_sem, back_g_sem = sems[22:25], sems[25:28], sems[28:31]
 
     load_w = pltpu.make_async_copy(w_hbm, w_gu, lsem.at[0])
     load_mid = pltpu.make_async_copy(mid_hbm, d_mid, lsem.at[1])
@@ -720,20 +758,17 @@
     load_cot = pltpu.make_async_copy(cot_hbm, wide_g, lsem.at[6])
     load_cot.start()
     g_two = Gather(own, wide, two_sem)
-    g_two.start(0)
     if in_kernel:
         spread_d = Spread(n, pack_d, down, d_sem)
         tick = Trickle(spread_d.trickle())
     else:
         copy_d = pltpu.make_async_copy(pack_d, down, lsem.at[2])
         tick = Trickle([copy_d])
-    for p in range(3):
-        g_two.advance(p, tick)
-    tick.flush()
-    g_two.finish()
-    load_w.wait()
-
-    def forward(jj, c):
+
+    for r in g_two.blocks(lambda: tick(2)):
+        if r == 0:
+            load_w.wait()
+        jj = flip(j, r)
         at = pl.ds(pl.multiple_of(jj * rows, rows), rows)
         low = wide[jj].reshape(rows, width)
         gate = dot_nt(w_gu[0:UNITS, :], low)
@@ -743,9 +778,7 @@
         hidden[:, at] = (silu * up).astype(BF16)
         by_gate[:, at] = (up * sigma * (1.0 + gate * (1.0 - sigma))).astype(BF16)
         by_up[:, at] = silu.astype(BF16)
-        return c
-
-    lax.fori_loop(0, CUBE, forward, 0)
+    tick.flush()
     load_cot.wait()
     if in_kernel:
         spread_d.finish()
@@ -780,20 +813,22 @@
         lax.fori_loop(0, width // 256, one, 0)
 
     weight_grad(hidden, wide_g, grads_d, 0)
-    low_sum.phase(0)
-    weight_grad(d_gate, wide, w_gu, 0)
-    low_sum.phase(1)
-    weight_grad(d_up, wide, w_gu, UNITS)
-    save_gu = pltpu.make_async_copy(w_gu, grads_b, lsem.at[3])
-    save_gu.start()
     if in_kernel:
-        back_d = Back(n, grads_d, tiles_d, back_sem)
+        back_d = Back(n, grads_d, tiles_d, back_d_sem)
+        back_g = Back(n, w_gu.at[pl.ds(0, UNITS)], tiles_g, back_g_sem)
         tick = Trickle(back_d.trickle())
     else:
         save_d = pltpu.make_async_copy(grads_d, tiles_d, lsem.at[4])
+        save_g = pltpu.make_async_copy(w_gu.at[pl.ds(0, UNITS)], tiles_g, lsem.at[7])
         tick = Trickle([save_d])
-    low_sum.phase(2)
-    low_sum.trade()
+    low_sum.phase(0, tick)
+    weight_grad(d_gate, wide, w_gu, 0)
+    low_sum.phase(1, tick)
+    weight_grad(d_up, wide, w_gu, UNITS)
+    save_u = pltpu.make_async_copy(w_gu.at[pl.ds(UNITS, UNITS)], grads_u, lsem.at[3])
+    save_u.start()
+    tick.flush()
+    low_sum.close()
     low_sum.finish()
     load_mid.wait()
 
@@ -813,15 +848,38 @@
 
         row_loop(half, 16, norm_back_two)
 
-    Gather(own, wide_g, attn_sem).run(tick)
+    tick = Trickle(back_g.trickle() if in_kernel else [save_g])
+    out_sum = Sum(part, heap, total, out_sem)
+    waiting = list(Sum.ORDER)
+    crossing = []
+
+    def out_block():
+        if waiting:
+            r = waiting.pop(0)
+            jj = flip(j, r)
+            at = pl.ds(pl.multiple_of(jj * rows, rows), rows)
+            for col in range(0, width, 512):
+                cols = pl.ds(col, 512)
+                part[jj, :, :, cols] = dot_tn(hidden[:, at], down[:, cols]).astype(BF16).reshape(2, half, 512)
+            out_sum.send(r)
+            crossing.append(r)
+        if len(crossing) > 1 or crossing and not waiting:
+            out_sum.take(crossing.pop(0), leave=False)
+
+    def between():
+        tick(2)
+        out_block()
+
+    for r in Gather(own, wide_g, attn_sem, UP_FIRST, HALVES).blocks(between):
+        jj = flip(j, r)
+        at = pl.ds(pl.multiple_of(jj * rows, rows), rows)
+        dy_ref[at, :] = dot_nt(wide_g[jj].reshape(rows, width), wo_ref[...]).astype(BF16)
     tick.flush()
-
-    def project(jj, c):
-        at = pl.ds(pl.multiple_of(jj * rows, rows), rows)
-        dy_ref[at, :] = dot_nt(wide_g[jj].reshape(rows, width), w_ref[176:304, :]).astype(BF16)
-        return c
-
-    lax.fori_loop(0, CUBE, project, 0)
+    while waiting or crossing:
+        out_block()
+    out_sum.crossed()
+    save_half = pltpu.make_async_copy(part.at[:, t], out_half, lsem.at[8])
+    save_half.start()
 
     def output_grad(m, c):
         cols = pl.ds(pl.multiple_of(m * 256, 256), 256)
@@ -830,14 +888,17 @@
         return c
 
     lax.fori_loop(0, width // 256, output_grad, 0)
-    save_gu.wait()
+    save_u.wait()
+    save_half.wait()
     if in_kernel:
         back_d.finish()
+        back_g.finish()
     else:
         save_d.wait()
-
-
-def mlp_call(n, own, w_a, y_turned, mid, w_gu, pack_d, cot_all):
+        save_g.wait()
+
+
+def mlp_call(n, own, w_a, w_o, y_turned, mid, w_gu, pack_d, cot_all):
     half, width = own.shape[1:]
     count = CUBE * 2 * half
     vm = pl.BlockSpec(memory_space=pltpu.VMEM)
@@ -845,19 +906,20 @@
     if width // n % 128:
         pack_d = spread_call(n, pack_d, width, 6)
     shape = (CUBE, 2, half, width)
+    tiles = (UNITS, width) if width // n % 128 else (n, UNITS, width // n)
     return pl.pallas_call(
         functools.partial(mlp_with_own, n),
         out_shape=[
-            jax.ShapeDtypeStruct((UNITS, count), BF16),
             jax.ShapeDtypeStruct((UNITS, width), BF16),
-            jax.ShapeDtypeStruct((2 * UNITS, width), BF16),
-            jax.ShapeDtypeStruct((UNITS, width) if width // n % 128 else (n, UNITS, width // n), BF16),
+            jax.ShapeDtypeStruct(tiles, BF16),
+            jax.ShapeDtypeStruct(tiles, BF16),
+            jax.ShapeDtypeStruct((CUBE, half, width), BF16),
             jax.ShapeDtypeStruct((128, width), BF16),
             jax.ShapeDtypeStruct((2, half, width), F32),
             jax.ShapeDtypeStruct((count, 128), BF16),
         ],
-        in_specs=[any_space, vm, vm] + [any_space] * 4,
-        out_specs=[vm, vm, any_space, any_space, vm, vm, vm],
+        in_specs=[any_space, vm, vm, vm] + [any_space] * 4,
+        out_specs=[any_space] * 4 + [vm] * 3,
         scratch_shapes=[
             pltpu.VMEM((2, half, width), BF16),
             pltpu.VMEM(shape, BF16),
@@ -867,33 +929,37 @@
             pltpu.VMEM((2, half, width), F32),
             pltpu.VMEM((2 * UNITS, width), BF16),
             pltpu.VMEM((UNITS, count), BF16),
+            pltpu.VMEM((UNITS, width), BF16),
+            pltpu.VMEM((UNITS, count), BF16),
             pltpu.VMEM((UNITS, count), BF16),
             pltpu.VMEM((UNITS, count), BF16),
             pltpu.VMEM((UNITS, count), BF16),
             pltpu.VMEM((UNITS, width), BF16),
-            pltpu.SemaphoreType.DMA((7,)),
+            pltpu.SemaphoreType.DMA((9,)),
             *gather_sems(),
             *gather_sems(),
             *sum_sems(),
+            *sum_sems(),
+            *spread_sems(n),
             *spread_sems(n),
             *spread_sems(n),
         ],
         compiler_params=pltpu.CompilerParams(collective_id=3, has_side_effects=True, vmem_limit_bytes=63 * MIB),
-    )(own, w_a, y_turned, mid, w_gu, pack_d, cot_all)
-
-
-def mlp_with_own(n, own_hbm, w_ref, y_turned, mid_hbm, w_hbm, pack_d, cot_hbm, *rest):
+    )(own, w_a, w_o, y_turned, mid, w_gu, pack_d, cot_all)
+
+
+def mlp_with_own(n, own_hbm, w_ref, wo_ref, y_turned, mid_hbm, w_hbm, pack_d, cot_hbm, *rest):
     outs, (own, *scratch) = rest[:7], rest[7:]
-    lsem = scratch[11]
+    lsem = scratch[13]
     load = pltpu.make_async_copy(own_hbm, own, lsem.at[5])
     load.start()
     load.wait()
-    mlp_kernel(n, own, w_ref, y_turned, mid_hbm, w_hbm, pack_d, cot_hbm, *outs, *scratch)
+    mlp_kernel(n, own, w_ref, wo_ref, y_turned, mid_hbm, w_hbm, pack_d, cot_hbm, *outs, *scratch)
 
 
 def tail_kernel(
-    n, lengths, q_ref, k_ref, v_ref, y_ref, den_ref, state_ref, w_ref, tok_ref, dy_ref, hidden, down,
-    grads_o, mid, d_mid, low_hbm, grads_b, first, second, third,
+    n, lengths, q_ref, k_ref, v_ref, y_ref, den_ref, state_ref, w_ref, tok_ref, dy_ref, grads_o,
+    out_half, mid, d_mid, low_hbm, grads_b, first, second, third,
     output_ref, grad_ref, tiles_b, tiles_a,
     part, heap_a, heap_b, wide, total, c_ref, c_kept, v_kept, side, dv, turned, dqkv, grads_a,
     state_mine, state_theirs, xsend, xrecv, lsem, *sems,
@@ -913,6 +979,8 @@
     load_low.start()
     load_mid = pltpu.make_async_copy(mid, grad_ref, lsem.at[0])
     load_mid.start()
+    load_out = pltpu.make_async_copy(out_half, part.at[:, t], lsem.at[4])
+    load_out.start()
     greet_all(n)
     out_sum = Sum(part, heap_b, total, sum_out, UP_LAST, HALVES)
     back_b = Back(n, grads_b, tiles_b, bsems) if in_kernel else None
@@ -945,19 +1013,12 @@
         side[tq, 0:FEAT] = lift_back(u, d_quad, d_line, first[...], second[...])
         return carry
 
+    load_out.wait()
+    for r in Sum.ORDER:
+        out_sum.leave(r)
     tick(4)
     lax.fori_loop(0, blocks, early, 0)
     done = exchange(groups, state_mine, state_theirs, xsend, xrecv, False)
-    for r in Sum.ORDER:
-        jj = flip(j, r)
-        at = pl.ds(pl.multiple_of(jj * rows, rows), rows)
-        for col in range(0, width, 512):
-            cols = pl.ds(col, 512)
-            part[jj, :, :, cols] = dot_tn(hidden[:, at], down[:, cols]).astype(BF16).reshape(2, half, 512)
-        out_sum.send(r)
-    for r in Sum.ORDER:
-        out_sum.take(r)
-
     for tb in range(blocks):
         tq = pl.ds(tb * BLOCK, BLOCK)
         qt = q_ref[tq, :] * BF16(0.25)
@@ -996,8 +1057,7 @@
         if sb == blocks // 2:
             out_sum.phase(1)
     tick.flush()
-    out_sum.phase(2)
-    out_sum.trade()
+    out_sum.close()
     state_back = done().astype(BF16)
 
     def late(sb, carry):
@@ -1018,7 +1078,7 @@
         return carry
 
     lax.fori_loop(0, blocks, late, 0)
-    out_sum.finish()
+    out_sum.finish(crossed=True)
     load_mid.wait()
     for h in range(2):
 
@@ -1056,9 +1116,9 @@
     else:
         copy = pltpu.make_async_copy(grads_a, tiles_a, lsem.at[3])
         copy.start()
-    for p in range(3):
-        one_sum.phase(p)
-    one_sum.trade()
+    one_sum.phase(0)
+    one_sum.phase(1)
+    one_sum.close()
     one_sum.finish()
 
     gain_one = w_ref[160:161, :].astype(F32)
@@ -1087,7 +1147,7 @@
     return jnp.concatenate([jnp.zeros_like(third[:, :FEAT]), third[:, : 128 - FEAT]], axis=1)
 
 
-def tail_call(n, lengths, q, k, v, y, den, state, w_a, mid, tokens, d_mid, dy, hidden, down, grads_o, low_one, grads_b):
+def tail_call(n, lengths, q, k, v, y, den, state, w_a, mid, tokens, d_mid, dy, grads_o, out_half, low_one, grads_b):
     groups = n // CUBE
     _, half, width = mid.shape
     rows = 2 * half
@@ -1105,7 +1165,7 @@
     output, grad, tiles_b, tiles_a = pl.pallas_call(
         functools.partial(tail_kernel, n),
         out_shape=out_shape,
-        in_specs=[pl.BlockSpec(memory_space=pltpu.SMEM)] + [vm] * 12 + [any_space] * 4 + [vm] * 3,
+        in_specs=[pl.BlockSpec(memory_space=pltpu.SMEM)] + [vm] * 10 + [any_space] * 5 + [vm] * 3,
         out_specs=[vm, vm, any_space, any_space],
         scratch_shapes=[
             pltpu.VMEM((CUBE, 2, half, width), BF16),
@@ -1125,7 +1185,7 @@
             pltpu.VMEM((peers, 384, 256), F32),
             pltpu.SemaphoreType.DMA((peers,)),
             pltpu.SemaphoreType.DMA((peers,)),
-            pltpu.SemaphoreType.DMA((4,)),
+            pltpu.SemaphoreType.DMA((5,)),
             *sum_sems(),
             *sum_sems(),
             *spread_sems(n),
@@ -1133,8 +1193,8 @@
         ],
         compiler_params=pltpu.CompilerParams(collective_id=2, has_side_effects=True, vmem_limit_bytes=63 * MIB),
     )(
-        lengths, q, k, v, y, den, state, w_a, tokens.reshape(2, half, width), dy, hidden, down, grads_o,
-        mid, d_mid, low_one, grads_b, *spreaders(),
+        lengths, q, k, v, y, den, state, w_a, tokens.reshape(2, half, width), dy, grads_o,
+        out_half, mid, d_mid, low_one, grads_b, *spreaders(),
     )
     if not wide_columns:
         tiles_b = back_call(n, grads_b, 9)
@@ -1157,33 +1217,33 @@
             w_query.T.reshape(per, FEAT, -1),
             w_key.T.reshape(per, FEAT, -1),
             jnp.broadcast_to(gains[None], (per, *gains.shape)),
-            w_output.reshape(per, 128, -1),
         ],
         axis=1,
     )
+    pack_o = w_output.reshape(per, 128, -1)
     pack_b = jnp.concatenate([units_first(w_gate.T), units_first(w_up.T)], axis=1)
-    w_a, w_gu, cot_all, low_one, low_two, mid, q, k, v, y, y_turned, den, state = head_call(
-        n, seq_lengths, pack_a, pack_b, tokens, cotangent
+    w_a, w_o, w_gu, cot_all, low_one, low_two, mid, q, k, v, y, y_turned, den, state = head_call(
+        n, seq_lengths, pack_a, pack_o, pack_b, tokens, cotangent
     )
-    hidden, down, grads_b, tiles_d, grads_o, d_mid, dy = mlp_call(
-        n, low_two, w_a, y_turned, mid, w_gu, units_first(w_down), cot_all
+    grads_u, tiles_d, tiles_g, out_half, grads_o, d_mid, dy = mlp_call(
+        n, low_two, w_a, w_o, y_turned, mid, w_gu, units_first(w_down), cot_all
     )
     if tiles_d.ndim == 2:
-        tiles_d = back_call(n, tiles_d, 7)
-    output, grad_tokens, tiles_b, tiles_a = tail_call(
-        n, seq_lengths, q, k, v, y, den, state, w_a, mid, tokens, d_mid, dy, hidden, down, grads_o, low_one, grads_b
+        tiles_d, tiles_g = back_call(n, tiles_d, 7), back_call(n, tiles_g, 8)
+    output, grad_tokens, tiles_u, tiles_a = tail_call(
+        n, seq_lengths, q, k, v, y, den, state, w_a, mid, tokens, d_mid, dy, grads_o, out_half, low_one, grads_u
     )
 
     def arrived(tiles):
         return tiles.reshape(-1, CUBE, *tiles.shape[1:]).astype(F32).sum(axis=0)
 
-    back_b, back_d, back_a = arrived(tiles_b), arrived(tiles_d), arrived(tiles_a)
+    back_g, back_u, back_d, back_a = arrived(tiles_g), arrived(tiles_u), arrived(tiles_d), arrived(tiles_a)
 
     def units(part):
         return part.reshape(CUBE * UNITS, -1)[: w_gate.shape[1]]
 
-    grad_gate = units(back_b[:, :UNITS]).T
-    grad_up = units(back_b[:, UNITS : 2 * UNITS]).T
+    grad_gate = units(back_g).T
+    grad_up = units(back_u).T
     grad_down = units(back_d)
     grad_value = back_a[:, 0:128].reshape(per * 128, -1).T
     grad_query = back_a[:, 128:144].reshape(per * FEAT, -1).T

time: 583 us -> 552 us (0.947)
  the two profiles are of different devices: /device:TPU:0 before, /device:TPU:9 now
where the time goes in v4:
time: 552 us; the launch traced here: 543 us
  Pallas kernels  520 us (94%)
  local copies, waits for them, and re-layouts  11.4 us (2%)
  other arithmetic  8.59 us (2%)
    pallas_call x1, Pallas kernels, mlp_call(): pl.pallas_call(functools.partial(mlp_with_own, n), out_shape=[jax.ShapeDt...  197 us
    pallas_call x1, Pallas kernels, head_call(): pl.pallas_call(functools.partial(head_kernel, n), out_shape=[jax.ShapeDty...  186 us
    pallas_call x1, Pallas kernels, tail_call(): pl.pallas_call(functools.partial(tail_kernel, n), out_shape=out_shape, in...  137 us

profile of v4, /device:TPU:9, one launch (start us, length us, event | category | flops | bytes accessed | tf_op | source)
XLA Modules:
  0.0 543.4 jit_solution(1147388469288463312)
XLA Ops:
  0.6 0.0 copy-start
  0.7 1.2 pad.10
  1.9 0.1 copy-done
  2.0 0.0 copy-start.7
  2.0 0.0 copy-start.13
  2.0 0.0 copy-start.14
  2.0 0.0 copy-start.9
  2.1 0.0 copy-start.11
  2.1 1.2 pad_maximum_fusion.pack_b
  3.3 0.0 copy-done.7
  3.3 0.2 copy.35
  3.5 0.1 pad.23.clone
  3.5 0.0 copy-done.13
  3.5 0.0 copy-done.14
  3.5 0.1 maximum_maximum_fusion
  3.6 0.0 copy-done.9
  3.6 0.1 copy.36
  3.7 0.0 copy-done.11
  3.8 0.1 copy.37
  3.9 0.8 pad_maximum_fusion.1.pack_a
  4.6 0.0 copy-start.8
  4.6 185.8 %shard_map.257 = (bf16[176,2048]{1,0:T(8,128)(2,1)}, bf16[128,2048]{1,0:T(8,128)(2,1)}, bf16[704,2048]{1,0:T(8,128)(2,1)}, bf16[8,2,128,2048]{3,2,1,0:T(8,128)(2...) custom-call(s32[3]{0:T(128)} %lengths.3, ...), custom_call_target="tpu_custom_call" | custom-call | tf_op jit(solution)/shard_map/pallas_call | solution.py:699
  190.4 0.0 copy-done.8
  190.4 0.9 pad.12
  191.3 197.2 %shard_map.258 = (bf16[352,2048]{1,0:T(8,128)(2,1)}, bf16[16,352,128]{2,1,0:T(8,128)(2,1)}, bf16[16,352,128]{2,1,0:T(8,128)(2,1)}, bf16[8,128,2048]{2,1,0:T(8,12...) custom-call(bf16[2,128,2048]{2,1,0:T(8,128)(2,1)} %get-tuple-element.43.own_hbm, ...), custom_call_target="tpu_custom_call" | custom-call | tf_op jit(solution)/shard_map/pallas_call | solution.py:910
  388.5 136.6 %shard_map.259 = (bf16[2,128,2048]{2,1,0:T(8,128)(2,1)}, f32[2,128,2048]{2,1,0:T(8,128)}, bf16[16,352,128]{2,1,0:T(8,128)(2,1)}, bf16[16,288,128]{2,1,0:T(8,128)(2,1)}) custom-call(s32[3]{0:T(128)} %lengths.3, bf16[2048,16]{1,0:T(8,128)(2,1)} %get-tuple-element.36.q_ref, bf16[2048,16]{1,0:T(8,128)(2,1)} %get-tuple-element.37.k_ref, ...), custom_call_target="tpu_custom_call" | custom-call | tf_op jit(solution)/shard_map/pallas_call | solution.py:1165
  525.1 0.0 copy-start.10
  525.2 0.0 copy-start.12
  525.2 1.6 convert_reduce_fusion.3
  526.8 0.0 copy-done.10
  526.8 0.1 copy.39
  526.9 0.0 copy-done.12
  526.9 0.1 copy.40
  527.1 0.9 fusion
  527.9 0.2 copy.38
  528.1 0.0 copy-start.3
  528.1 0.1 multiply_reduce_fusion.2
  528.3 0.0 copy-start.5
  528.3 1.9 convert_reduce_fusion.1
  530.1 0.0 copy-done.3
  530.2 0.0 copy-done.5
  530.2 0.0 copy-start.1
  530.2 0.2 convert_reduce_fusion.2
  530.4 0.9 copy-done.1
  531.3 0.0 copy-start.4
  531.3 1.9 multiply_reduce_fusion
  533.2 2.5 psum.7
  535.7 0.5 bitcast_divide_fusion
  536.2 0.7 copy.41
  537.0 0.7 copy.42
  537.7 0.0 copy-done.4
  537.7 0.2 convert_reduce_fusion
  537.9 0.0 copy-start.6
  537.9 1.2 slice.42
  539.1 0.5 copy-done.6
  539.7 0.0 copy-start.2
  539.7 1.0 copy.45
  540.6 1.0 copy-done.2
  541.6 1.3 copy.46
  (8 shorter events, 0.1 us)
Async XLA Ops:
  0.6 1.3 copy-start
  2.0 1.3 copy-start.7
  2.0 1.5 copy-start.13
  2.0 1.5 copy-start.14
  2.0 1.6 copy-start.9
  2.1 1.7 copy-start.11
  4.6 185.8 %copy-start.8 = (bf16[2752,128]{1,0:T(8,128)(2,1)S(1)}, bf16[2752,128]{1,0:T(8,128)(2,1)}, u32[]{:S(2)}) copy-start(bf16[2752,128]{1,0:T(8,128)(2,1)} %param.27) | copy-start | bytes 2113540
  525.1 1.6 copy-start.10
  525.2 1.7 copy-start.12
  528.1 2.0 copy-start.3
  528.3 1.9 copy-start.5
  530.2 1.1 copy-start.1
  531.3 6.4 %copy-start.4 = (bf16[16,352,128]{2,1,0:T(8,128)(2,1)S(1)}, bf16[16,352,128]{2,1,0:T(8,128)(2,1)}, u32[]{:S(2)}) copy-start(bf16[16,352,128]{2,1,0:T(8,128)(2,1)} %get-tuple-element.60) | copy-start | bytes 4325380
  537.9 1.7 copy-start.6
  539.7 2.0 copy-start.2

commit v5 on v4

--- a/solution.py
+++ b/solution.py
@@ -570,7 +570,6 @@
     g_tok.start()
     for w in range(3):
         g_tok.wave(w)
-    tick.flush()
     g_cot.start()
     g_tok.finish()
     if in_kernel:
@@ -606,7 +605,9 @@
         state_mine[256:384, :] += dot_tn(line, v_ext)
         return c
 
-    lax.fori_loop(0, CUBE, project, 0)
+    for jj in range(CUBE):
+        tick(2)
+        project(jj, 0)
     save = pltpu.make_async_copy(wide, low_hbm, lsem.at[0])
     save.start()
     done = exchange(groups, state_mine, state_theirs, xsend, xrecv, True)
@@ -628,6 +629,7 @@
             acc = acc + far * (seg == 1).astype(F32)
         y_ref[tq, :] = acc[:, :128]
         den_ref[tq, :] = acc[:, 128:]
+        tick(2)
 
     g_cot.wave(1)
     state = done()
@@ -655,10 +657,12 @@
         for h in range(2):
             part[jj, h] = dot(y_low[h * half : (h + 1) * half], out_w).astype(BF16)
         out_sum.send(r)
+        tick(1)
         if idx:
             out_sum.take(Sum.ORDER[idx - 1])
     out_sum.take(Sum.ORDER[-1])
-    out_sum.phase(0)
+    out_sum.phase(0, lambda: tick(1))
+    tick.flush()
     out_sum.phase(1)
     out_sum.close()
     out_sum.finish()

time: 552 us -> 538 us (0.975)
  Pallas kernels: 520 us -> 505 us
    pallas_call x1, Pallas kernels: 186 us -> 166 us  [head_call(): pl.pallas_call(functools.partial(head_kernel, n), out_shape=[jax.ShapeDty...]
    pallas_call x1, Pallas kernels: 197 us -> 203 us  [mlp_call(): pl.pallas_call(functools.partial(mlp_with_own, n), out_shape=[jax.ShapeDt...]
where the time goes in v5:
time: 538 us; the launch traced here: 529 us
  Pallas kernels  505 us (94%)
  local copies, waits for them, and re-layouts  11.4 us (2%)
  other arithmetic  8.59 us (2%)
    pallas_call x1, Pallas kernels, mlp_call(): pl.pallas_call(functools.partial(mlp_with_own, n), out_shape=[jax.ShapeDt...  203 us
    pallas_call x1, Pallas kernels, head_call(): pl.pallas_call(functools.partial(head_kernel, n), out_shape=[jax.ShapeDty...  166 us
    pallas_call x1, Pallas kernels, tail_call(): pl.pallas_call(functools.partial(tail_kernel, n), out_shape=out_shape, in...  136 us

profile of v5, /device:TPU:9, one launch (start us, length us, event | category | flops | bytes accessed | tf_op | source)
XLA Modules:
  0.0 529.0 jit_solution(11959631892161657151)
XLA Ops:
  0.6 0.0 copy-start
  0.7 1.2 pad.10
  1.9 0.1 copy-done
  2.0 0.0 copy-start.7
  2.0 0.0 copy-start.13
  2.0 0.0 copy-start.14
  2.0 0.0 copy-start.9
  2.1 0.0 copy-start.11
  2.1 1.2 pad_maximum_fusion.pack_b
  3.3 0.0 copy-done.7
  3.3 0.2 copy.35
  3.5 0.1 pad.23.clone
  3.5 0.0 copy-done.13
  3.5 0.0 copy-done.14
  3.5 0.1 maximum_maximum_fusion
  3.6 0.0 copy-done.9
  3.6 0.1 copy.36
  3.7 0.0 copy-done.11
  3.8 0.1 copy.37
  3.9 0.8 pad_maximum_fusion.1.pack_a
  4.6 0.0 copy-start.8
  4.6 166.2 %shard_map.257 = (bf16[176,2048]{1,0:T(8,128)(2,1)}, bf16[128,2048]{1,0:T(8,128)(2,1)}, bf16[704,2048]{1,0:T(8,128)(2,1)}, bf16[8,2,128,2048]{3,2,1,0:T(8,128)(2...) custom-call(s32[3]{0:T(128)} %lengths.3, ...), custom_call_target="tpu_custom_call" | custom-call | tf_op jit(solution)/shard_map/pallas_call | solution.py:703
  170.9 0.0 copy-done.8
  170.9 0.9 pad.12
  171.8 203.2 %shard_map.258 = (bf16[352,2048]{1,0:T(8,128)(2,1)}, bf16[16,352,128]{2,1,0:T(8,128)(2,1)}, bf16[16,352,128]{2,1,0:T(8,128)(2,1)}, bf16[8,128,2048]{2,1,0:T(8,12...) custom-call(bf16[2,128,2048]{2,1,0:T(8,128)(2,1)} %get-tuple-element.43.own_hbm, ...), custom_call_target="tpu_custom_call" | custom-call | tf_op jit(solution)/shard_map/pallas_call | solution.py:914
  375.0 135.9 %shard_map.259 = (bf16[2,128,2048]{2,1,0:T(8,128)(2,1)}, f32[2,128,2048]{2,1,0:T(8,128)}, bf16[16,352,128]{2,1,0:T(8,128)(2,1)}, bf16[16,288,128]{2,1,0:T(8,128)(2,1)}) custom-call(s32[3]{0:T(128)} %lengths.3, bf16[2048,16]{1,0:T(8,128)(2,1)} %get-tuple-element.36.q_ref, bf16[2048,16]{1,0:T(8,128)(2,1)} %get-tuple-element.37.k_ref, ...), custom_call_target="tpu_custom_call" | custom-call | tf_op jit(solution)/shard_map/pallas_call | solution.py:1169
  511.0 0.0 copy-start.10
  511.0 0.0 copy-start.12
  511.0 1.6 convert_reduce_fusion.3
  512.6 0.0 copy-done.10
  512.6 0.1 copy.39
  512.7 0.0 copy-done.12
  512.7 0.1 copy.40
  512.9 0.9 fusion
  513.8 0.2 copy.38
  514.0 0.0 copy-start.3
  514.0 0.1 multiply_reduce_fusion.2
  514.1 0.0 copy-start.5
  514.1 1.9 convert_reduce_fusion.1
  516.0 0.0 copy-done.3
  516.0 0.0 copy-done.5
  516.0 0.0 copy-start.1
  516.0 0.2 convert_reduce_fusion.2
  516.2 0.9 copy-done.1
  517.1 0.0 copy-start.4
  517.1 1.9 multiply_reduce_fusion
  519.1 2.5 psum.7
  521.5 0.5 bitcast_divide_fusion
  522.1 0.7 copy.41
  522.8 0.7 copy.42
  523.5 0.0 copy-done.4
  523.5 0.2 convert_reduce_fusion
  523.8 0.0 copy-start.6
  523.8 1.2 slice.42
  525.0 0.5 copy-done.6
  525.5 0.0 copy-start.2
  525.5 1.0 copy.45
  526.5 1.0 copy-done.2
  527.5 1.3 copy.46
  (8 shorter events, 0.1 us)
Async XLA Ops:
  0.6 1.3 copy-start
  2.0 1.3 copy-start.7
  2.0 1.5 copy-start.13
  2.0 1.5 copy-start.14
  2.0 1.6 copy-start.9
  2.1 1.7 copy-start.11
  4.6 166.2 %copy-start.8 = (bf16[2752,128]{1,0:T(8,128)(2,1)S(1)}, bf16[2752,128]{1,0:T(8,128)(2,1)}, u32[]{:S(2)}) copy-start(bf16[2752,128]{1,0:T(8,128)(2,1)} %param.27) | copy-start | bytes 2113540
  511.0 1.6 copy-start.10
  511.0 1.7 copy-start.12
  514.0 2.0 copy-start.3
  514.1 1.9 copy-start.5
  516.0 1.1 copy-start.1
  517.1 6.4 %copy-start.4 = (bf16[16,352,128]{2,1,0:T(8,128)(2,1)S(1)}, bf16[16,352,128]{2,1,0:T(8,128)(2,1)}, u32[]{:S(2)}) copy-start(bf16[16,352,128]{2,1,0:T(8,128)(2,1)} %get-tuple-element.60) | copy-start | bytes 4325380
  523.8 1.7 copy-start.6
  525.5 2.0 copy-start.2

commit v6 on v5

--- a/solution.py
+++ b/solution.py
@@ -539,7 +539,7 @@
 def head_kernel(
     n, lengths, tok_ref, pack_a, pack_o, pack_b, cot_hbm, first, second, third,
     w_ref, wo_ref, w_b, cot_all, low_hbm, own, mid_ref, q_ref, k_ref, v_ref, y_ref, y_turned, den_ref, state_ref,
-    wide, part, heap, total, kept, state_mine, state_theirs, xsend, xrecv, lsem, *sems,
+    wide, part, heap, total, kept, state_mine, state_theirs, xsend, xrecv, lsem, *sems, results,
 ):
     groups = n // CUBE
     s, t, j, base = whereabouts()
@@ -661,6 +661,8 @@
         if idx:
             out_sum.take(Sum.ORDER[idx - 1])
     out_sum.take(Sum.ORDER[-1])
+    for copy in results:
+        copy.start()
     out_sum.phase(0, lambda: tick(1))
     tick.flush()
     out_sum.phase(1)
@@ -681,10 +683,23 @@
     g_cot.wave(2)
     g_cot.finish()
     save.wait()
+    for copy in results:
+        copy.wait()
     if in_kernel:
         spread_b.finish()
     else:
         copy_b.wait()
+
+
+HELD = (0, 1, 7, 8, 9, 10, 11, 12, 13)
+
+
+def head_with_results(n, *refs):
+    ins, outs, held, sem, rest = refs[:9], list(refs[9:23]), refs[23:32], refs[32], refs[33:]
+    results = [pltpu.make_async_copy(ref, outs[at], sem.at[m]) for m, (at, ref) in enumerate(zip(HELD, held))]
+    for at, ref in zip(HELD, held):
+        outs[at] = ref
+    head_kernel(n, *ins, *outs, *rest, results=results)
 
 
 def head_call(n, lengths, pack_a, pack_o, pack_b, tokens, cot):
@@ -701,7 +716,7 @@
         pack_o = spread_call(n, pack_o, width, 11)
     shape = (CUBE, 2, half, width)
     return pl.pallas_call(
-        functools.partial(head_kernel, n),
+        functools.partial(head_with_results, n),
         out_shape=[
             jax.ShapeDtypeStruct((w_rows[0], width), BF16),
             jax.ShapeDtypeStruct((128, width), BF16),
@@ -719,8 +734,18 @@
             jax.ShapeDtypeStruct((384, 256), F32),
         ],
         in_specs=[pl.BlockSpec(memory_space=pltpu.SMEM), vm] + [any_space] * 4 + [vm] * 3,
-        out_specs=[vm, vm, any_space, any_space, any_space] + [vm] * 9,
+        out_specs=[any_space] * 5 + [vm] * 2 + [any_space] * 7,
         scratch_shapes=[
+            pltpu.VMEM((w_rows[0], width), BF16),
+            pltpu.VMEM((128, width), BF16),
+            pltpu.VMEM((count, FEAT), BF16),
+            pltpu.VMEM((count, FEAT), BF16),
+            pltpu.VMEM((count, 256), BF16),
+            pltpu.VMEM((count, 128), F32),
+            pltpu.VMEM((128, count), BF16),
+            pltpu.VMEM((count, 128), F32),
+            pltpu.VMEM((384, 256), F32),
+            pltpu.SemaphoreType.DMA((len(HELD),)),
             pltpu.VMEM(shape, BF16),
             pltpu.VMEM(shape, BF16),
             pltpu.VMEM((15, half, width), BF16),
@@ -743,7 +768,7 @@
 
 
 def mlp_kernel(
-    n, own, w_ref, wo_ref, y_turned, mid_hbm, w_hbm, pack_d, cot_hbm,
+    n, load_own, own, w_ref, wo_ref, y_turned, mid_hbm, w_hbm, pack_d, cot_hbm,
     grads_u, tiles_d, tiles_g, out_half, grads_o, d_mid, dy_ref,
     wide, wide_g, part, heap, total, w_gu, hidden, down, by_gate, by_up, d_gate, d_up, grads_d, lsem, *sems,
 ):
@@ -759,6 +784,7 @@
     load_w.start()
     load_mid.start()
     greet_all(n)
+    load_own.wait()
     load_cot = pltpu.make_async_copy(cot_hbm, wide_g, lsem.at[6])
     load_cot.start()
     g_two = Gather(own, wide, two_sem)
@@ -957,8 +983,7 @@
     lsem = scratch[13]
     load = pltpu.make_async_copy(own_hbm, own, lsem.at[5])
     load.start()
-    load.wait()
-    mlp_kernel(n, own, w_ref, wo_ref, y_turned, mid_hbm, w_hbm, pack_d, cot_hbm, *outs, *scratch)
+    mlp_kernel(n, load, own, w_ref, wo_ref, y_turned, mid_hbm, w_hbm, pack_d, cot_hbm, *outs, *scratch)
 
 
 def tail_kernel(

time: 538 us -> 535 us (level)
  no operation moved by 1% of the time
where the time goes in v6:
time: 535 us; the launch traced here: 526 us
  Pallas kernels  502 us (94%)
  local copies, waits for them, and re-layouts  11.4 us (2%)
  other arithmetic  8.59 us (2%)
    pallas_call x1, Pallas kernels, mlp_call(): pl.pallas_call(functools.partial(mlp_with_own, n), out_shape=[jax.ShapeDt...  202 us
    pallas_call x1, Pallas kernels, head_call(): pl.pallas_call(functools.partial(head_with_results, n), out_shape=[jax.Sh...  164 us
    pallas_call x1, Pallas kernels, tail_call(): pl.pallas_call(functools.partial(tail_kernel, n), out_shape=out_shape, in...  136 us

profile of v6, /device:TPU:9, one launch (start us, length us, event | category | flops | bytes accessed | tf_op | source)
XLA Modules:
  0.0 525.8 jit_solution(14484828797775858171)
XLA Ops:
  0.6 0.0 copy-start
  0.7 1.2 pad.10
  1.9 0.1 copy-done
  2.0 0.0 copy-start.7
  2.0 0.0 copy-start.13
  2.0 0.0 copy-start.14
  2.0 0.0 copy-start.9
  2.1 0.0 copy-start.11
  2.1 1.2 pad_maximum_fusion.refs_4_
  3.3 0.0 copy-done.7
  3.3 0.2 copy.35
  3.5 0.1 pad.23.clone
  3.5 0.0 copy-done.13
  3.5 0.0 copy-done.14
  3.5 0.1 maximum_maximum_fusion
  3.6 0.0 copy-done.9
  3.6 0.1 copy.36
  3.7 0.0 copy-done.11
  3.8 0.1 copy.37
  3.9 0.8 pad_maximum_fusion.1.refs_2_
  4.6 0.0 copy-start.8
  4.6 164.3 %shard_map.257 = (bf16[176,2048]{1,0:T(8,128)(2,1)}, bf16[128,2048]{1,0:T(8,128)(2,1)}, bf16[704,2048]{1,0:T(8,128)(2,1)}, bf16[8,2,128,2048]{3,2,1,0:T(8,128)(2...) custom-call(s32[3]{0:T(128)} %lengths.1, ...), custom_call_target="tpu_custom_call" | custom-call | tf_op jit(solution)/shard_map/pallas_call | solution.py:718
  169.0 0.0 copy-done.8
  169.0 0.9 pad.12
  169.9 202.0 %shard_map.258 = (bf16[352,2048]{1,0:T(8,128)(2,1)}, bf16[16,352,128]{2,1,0:T(8,128)(2,1)}, bf16[16,352,128]{2,1,0:T(8,128)(2,1)}, bf16[8,128,2048]{2,1,0:T(8,12...) custom-call(bf16[2,128,2048]{2,1,0:T(8,128)(2,1)} %get-tuple-element.43.own_hbm, ...), custom_call_target="tpu_custom_call" | custom-call | tf_op jit(solution)/shard_map/pallas_call | solution.py:940
  371.9 135.9 %shard_map.259 = (bf16[2,128,2048]{2,1,0:T(8,128)(2,1)}, f32[2,128,2048]{2,1,0:T(8,128)}, bf16[16,352,128]{2,1,0:T(8,128)(2,1)}, bf16[16,288,128]{2,1,0:T(8,128)(2,1)}) custom-call(s32[3]{0:T(128)} %lengths.1, bf16[2048,16]{1,0:T(8,128)(2,1)} %get-tuple-element.36.q_ref, bf16[2048,16]{1,0:T(8,128)(2,1)} %get-tuple-element.37.k_ref, ...), custom_call_target="tpu_custom_call" | custom-call | tf_op jit(solution)/shard_map/pallas_call | solution.py:1194
  507.8 0.0 copy-start.10
  507.8 0.0 copy-start.12
  507.9 1.6 convert_reduce_fusion.3
  509.4 0.0 copy-done.10
  509.5 0.1 copy.39
  509.6 0.0 copy-done.12
  509.6 0.1 copy.40
  509.7 0.9 fusion
  510.6 0.2 copy.38
  510.8 0.0 copy-start.3
  510.8 0.1 multiply_reduce_fusion.2
  511.0 0.0 copy-start.5
  511.0 1.9 convert_reduce_fusion.1
  512.8 0.0 copy-done.3
  512.8 0.0 copy-done.5
  512.9 0.0 copy-start.1
  512.9 0.2 convert_reduce_fusion.2
  513.1 0.9 copy-done.1
  514.0 0.0 copy-start.4
  514.0 1.9 multiply_reduce_fusion
  515.9 2.5 psum.7
  518.4 0.5 bitcast_divide_fusion
  518.9 0.7 copy.41
  519.7 0.7 copy.42
  520.4 0.0 copy-done.4
  520.4 0.2 convert_reduce_fusion
  520.6 0.0 copy-start.6
  520.6 1.2 slice.42
  521.8 0.5 copy-done.6
  522.3 0.0 copy-start.2
  522.3 1.0 copy.45
  523.3 1.0 copy-done.2
  524.3 1.3 copy.46
  (8 shorter events, 0.1 us)
Async XLA Ops:
  0.6 1.3 copy-start
  2.0 1.3 copy-start.7
  2.0 1.5 copy-start.13
  2.0 1.5 copy-start.14
  2.0 1.6 copy-start.9
  2.1 1.7 copy-start.11
  4.6 164.3 %copy-start.8 = (bf16[2752,128]{1,0:T(8,128)(2,1)S(1)}, bf16[2752,128]{1,0:T(8,128)(2,1)}, u32[]{:S(2)}) copy-start(bf16[2752,128]{1,0:T(8,128)(2,1)} %param.27) | copy-start | bytes 2113540
  507.8 1.6 copy-start.10
  507.8 1.7 copy-start.12
  510.8 2.0 copy-start.3
  511.0 1.9 copy-start.5
  512.9 1.1 copy-start.1
  514.0 6.4 %copy-start.4 = (bf16[16,352,128]{2,1,0:T(8,128)(2,1)S(1)}, bf16[16,352,128]{2,1,0:T(8,128)(2,1)}, u32[]{:S(2)}) copy-start(bf16[16,352,128]{2,1,0:T(8,128)(2,1)} %get-tuple-element.60) | copy-start | bytes 4325380
  520.6 1.7 copy-start.6
  522.3 2.0 copy-start.2
